TPU v7x, 32 devices: a whole 2x2x4 slice. The times are simulated.
32 devices in a mesh: gx: 4 (over y, x), gy: 8 (over z, core).
Axes of the slice: x: 2, y: 2, z: 4, core: 2. Of those that a mesh axis runs over, the one named last changes fastest.
Arguments:
- features: bfloat16 [4, 8, 1, 192, 512], P('gx', 'gy'), may hold values from -6 to 6
- occupancy: int32 [4, 8, 1, 512], P('gx', 'gy'), may hold values 0 or 1
- brick_pos: int32 [4, 8, 1], P('gx', 'gy'), may hold values from 0 to 3, as said below
- weight: bfloat16 [192, 27, 192], replicated, may hold values from -0.125 to 0.125
- cotangent: bfloat16 [4, 8, 1, 192, 512], P('gx', 'gy'), may hold values from -6 to 6
Outputs:
- output: bfloat16 [4, 8, 1, 192, 512], P('gx', 'gy')
- x_grad: bfloat16 [4, 8, 1, 192, 512], P('gx', 'gy')
- w_grad: float32 [192, 27, 192], P('gx', None, 'gy')
Inputs may be any that keep to these rules, and one draw needn't show every extreme that they name: `brick_pos`: the 1 positions of one device are distinct.
All inputs are finite; a program needn't handle non-finite values. No bound on the sum of `occupancy` on one device may be relied on, other than what follows from the above.
Results may differ from a plain program's by a relative error of at most 0.014.
Values may be sent and summed in bfloat16 or wider, within the bound.
No kernel may reach another device: no remote copies, remote signals or barrier semaphores. Data moves between devices by JAX's collectives and lax.ppermute only.
A program may use at most 64 MiB of HBM per device.

v0:
```python
import jax
import jax.numpy as jnp
from jax import lax
from jax.sharding import PartitionSpec as P

BE = 8
TX = 2
TY = 2
HZ = 1


def extended(block, sides, width):
    for axis, dim in sides:
        count = lax.axis_size(axis)
        forward = [(i, i + 1) for i in range(count - 1)]
        backward = [(target, source) for source, target in forward]
        low = lax.ppermute(
            lax.slice_in_dim(block, block.shape[dim] - width, None, axis=dim), axis, forward
        )
        high = lax.ppermute(lax.slice_in_dim(block, 0, width, axis=dim), axis, backward)
        block = jnp.concatenate([low, block, high], axis=dim)
    return block


def silu_slope(values_in):
    sigma = jax.nn.sigmoid(values_in)
    return sigma * (1.0 + values_in * (1.0 - sigma))


def tap_columns(window):
    channels = window.shape[3]
    pieces = []
    for tap_x in range(3):
        for tap_y in range(3):
            for tap_z in range(3):
                start_x, start_y, start_z = (2 - tap_x, 2 - tap_y, 2 - tap_z)
                piece_view = window[
                    start_x : start_x + BE, start_y : start_y + BE, start_z : start_z + BE, :
                ]
                pieces.append(piece_view.reshape(BE * BE * BE, channels))
    return jnp.concatenate(pieces, axis=1)


def corner_starts(positions):
    start_x = positions // (TY * HZ) * BE
    start_y = positions // HZ % TY * BE
    start_z = positions % HZ * BE
    return (start_x, start_y, start_z)


def cut_cube(lattice, starts, slot_id, edge_len):
    zero_idx = jnp.zeros((), jnp.int32)
    return lax.dynamic_slice(
        lattice,
        (starts[0][slot_id], starts[1][slot_id], starts[2][slot_id], zero_idx),
        (edge_len, edge_len, edge_len, lattice.shape[3]),
    )


def place_bricks(bricks, starts):
    slot_count, channels = (bricks.shape[0], bricks.shape[2])
    lattice = jnp.zeros((TX * BE, TY * BE, HZ * BE, channels), bricks.dtype)
    zero_idx = jnp.zeros((), jnp.int32)
    cube_part = bricks[0].reshape(BE, BE, BE, channels)
    lattice = lax.dynamic_update_slice(
        lattice, cube_part, (starts[0][0], starts[1][0], starts[2][0], zero_idx)
    )
    return lattice


def fold_rims(padded, outer_cycle):
    inner_sum = padded[1:-1, 1:-1, 1:-1, :]
    rim_cycle = outer_cycle[:, :, 1:-1, :]
    inner_sum = inner_sum.at[0, :, :, :].add(rim_cycle[0, 2:-2])
    inner_sum = inner_sum.at[-1, :, :, :].add(rim_cycle[-1, 2:-2])
    inner_sum = inner_sum.at[:, 0, :, :].add(rim_cycle[2:-2, 0])
    inner_sum = inner_sum.at[:, -1, :, :].add(rim_cycle[2:-2, -1])
    inner_sum = inner_sum.at[0, 0, :, :].add(rim_cycle[0, 0])
    inner_sum = inner_sum.at[0, -1, :, :].add(rim_cycle[0, -1])
    inner_sum = inner_sum.at[-1, 0, :, :].add(rim_cycle[-1, 0])
    inner_sum = inner_sum.at[-1, -1, :, :].add(rim_cycle[-1, -1])
    return inner_sum


def shards(features, occupancy, brick_pos, weight, cotangent):
    bricks = features[0, 0].transpose(0, 2, 1)
    slot_count, voxels, channels = bricks.shape
    live_mask = occupancy[0, 0].astype(jnp.bfloat16)[:, :, None]
    starts = corner_starts(brick_pos[0, 0])
    masked = bricks * live_mask
    zero_idx = jnp.zeros((), jnp.int32)
    tap_weight = weight.transpose(1, 0, 2).reshape(27 * channels, channels)
    padded = jnp.zeros((TX * BE + 2, TY * BE + 2, HZ * BE + 2, channels), jnp.float32)
    slot_id = 0
    tap_terms = jnp.einsum(
        "vi,ki->vk", masked[slot_id], tap_weight, preferred_element_type=jnp.float32
    ).reshape(BE, BE, BE, 27, channels)
    spread = jnp.zeros((BE + 2, BE + 2, BE + 2, channels), jnp.float32)
    for tap_x in range(3):
        for tap_y in range(3):
            for tap_z in range(3):
                tap_id = 9 * tap_x + 3 * tap_y + tap_z
                spread = spread.at[
                    2 - tap_x : 2 - tap_x + BE,
                    2 - tap_y : 2 - tap_y + BE,
                    2 - tap_z : 2 - tap_z + BE,
                    :,
                ].add(tap_terms[:, :, :, tap_id, :])
    padded = lax.dynamic_update_slice(
        padded, spread, (starts[0][slot_id], starts[1][slot_id], starts[2][slot_id], zero_idx)
    )
    outer_cycle = extended(padded.astype(jnp.bfloat16), (("gx", 0), ("gy", 1)), 1).astype(
        padded.dtype
    )
    folded = fold_rims(padded, outer_cycle)
    slot_id = 0
    pre_list = [cut_cube(folded, starts, slot_id, BE).reshape(voxels, channels)]
    pre_act = jnp.stack(pre_list, axis=0)
    output = (jax.nn.silu(pre_act) * live_mask).astype(jnp.bfloat16)
    cot_last = cotangent[0, 0].transpose(0, 2, 1)
    slope = (cot_last.astype(jnp.float32) * silu_slope(pre_act) * live_mask).astype(jnp.bfloat16)
    grad_lattice = place_bricks(slope, starts)
    grad_wide = extended(grad_lattice, (("gx", 0), ("gy", 1)), 1)
    grad_wide = jnp.pad(grad_wide, ((0, 0), (0, 0), (1, 1), (0, 0)))
    slot_id = 0
    window = cut_cube(grad_wide, starts, slot_id, BE + 2)
    columns = tap_columns(window)
    back_grad = jnp.dot(columns, tap_weight, preferred_element_type=jnp.float32)
    back_list = [(back_grad * live_mask[slot_id]).astype(jnp.bfloat16)]
    tap_sum = jnp.einsum("vk,vi->ki", columns, masked[slot_id], preferred_element_type=jnp.float32)
    x_grad = jnp.stack(back_list, axis=0).transpose(0, 2, 1)
    weight_sum = tap_sum.reshape(27, channels, channels).transpose(1, 0, 2)
    total_bricks = slot_count * lax.axis_size("gx") * lax.axis_size("gy")
    summed = lax.psum(weight_sum, ("gx", "gy"))
    row_count = channels // lax.axis_size("gx")
    col_count = channels // lax.axis_size("gy")
    own_share = lax.dynamic_slice(
        summed,
        (lax.axis_index("gx") * row_count, zero_idx, lax.axis_index("gy") * col_count),
        (row_count, 27, col_count),
    )
    w_grad = own_share / total_bricks
    return (output.transpose(0, 2, 1)[None, None], x_grad[None, None], w_grad)


def solution(mesh):
    placed = (
        P("gx", "gy", None, None, None),
        P("gx", "gy", None, None),
        P("gx", "gy", None),
        P(),
        P("gx", "gy", None, None, None),
    )
    return jax.shard_map(
        shards,
        mesh=mesh,
        in_specs=placed,
        out_specs=(
            P("gx", "gy", None, None, None),
            P("gx", "gy", None, None, None),
            P("gx", None, "gy"),
        ),
        check_vma=False,
    )
```

profile of v0, /device:TPU:0, one launch (start us, length us, event | category | flops | bytes accessed | tf_op | source)
XLA Modules:
  0.0 397.6 jit_solution(6655674544943218270)
XLA Ops:
  10.0 2.0 fusion
  12.1 5.0 %copy-done.4 = f32[8,8,8,27,192]{4,2,3,1,0:T(8,128)} copy-done((f32[8,8,8,27,192]{4,2,3,1,0:T(8,128)}, f32[8,8,8,27,192]{4,2,3,1,0:T(8,128)S(1)}, u32[]{:S(2)}) %copy-start.4) | copy-done | bytes 10616856
  19.4 4.1 %scatter-add.119 = f32[10,10,10,192]{3,2,1,0:T(8,128)} dynamic-update-slice(f32[10,10,10,192]{3,2,1,0:T(8,128)} %scatter-add.116, f32[8,8,8,192]{3,2,1,0:T(8,128)} %fusion.48, s32[]{:T(128)} %constant.1169.clone.1, s32[]{:T(128)} %constant.1169.clone.1, s32[]{:T(128)} %constant.1170.clone.1, s32[]{:T(128)} %constant.1171.clone.1) | dynamic-update-slice | bytes 786436 | tf_op jit(solution)/shard_map/scatter-add | solution.py:108
  23.5 2.1 fusion.47
  25.6 2.3 fusion.45
  27.9 4.2 %scatter-add.121 = f32[10,10,10,192]{3,2,1,0:T(8,128)} dynamic-update-slice(f32[10,10,10,192]{3,2,1,0:T(8,128)} %fusion.47, f32[8,8,8,192]{3,2,1,0:T(8,128)} %fusion.45, s32[]{:T(128)} %constant.1169.clone.1, s32[]{:T(128)} %constant.1170.clone.1, s32[]{:T(128)} %constant.1169.clone.1, s32[]{:T(128)} %constant.1171.clone.1) | dynamic-update-slice | bytes 786436 | tf_op jit(solution)/shard_map/scatter-add | solution.py:108
  32.1 2.3 fusion.44
  34.4 4.2 %scatter-add.124 = f32[10,10,10,192]{3,2,1,0:T(8,128)} dynamic-update-slice(f32[10,10,10,192]{3,2,1,0:T(8,128)} %scatter-add.121, f32[8,8,8,192]{3,2,1,0:T(8,128)} %fusion.44, s32[]{:T(128)} %constant.1169.clone.1, s32[]{:T(128)} %constant.1170.clone.1, s32[]{:T(128)} %constant.1170.clone.1, s32[]{:T(128)} %constant.1171.clone.1) | dynamic-update-slice | bytes 786436 | tf_op jit(solution)/shard_map/scatter-add | solution.py:108
  38.5 2.1 fusion.43
  40.6 2.3 fusion.41
  42.9 4.2 %scatter-add.126 = f32[10,10,10,192]{3,2,1,0:T(8,128)} dynamic-update-slice(f32[10,10,10,192]{3,2,1,0:T(8,128)} %fusion.43, f32[8,8,8,192]{3,2,1,0:T(8,128)} %fusion.41, s32[]{:T(128)} %constant.1169.clone.1, s32[]{:T(128)} %constant.1171.clone.1, s32[]{:T(128)} %constant.1169.clone.1, s32[]{:T(128)} %constant.1171.clone.1) | dynamic-update-slice | bytes 786436 | tf_op jit(solution)/shard_map/scatter-add | solution.py:108
  47.1 2.3 fusion.40
  49.4 4.2 %scatter-add.129 = f32[10,10,10,192]{3,2,1,0:T(8,128)} dynamic-update-slice(f32[10,10,10,192]{3,2,1,0:T(8,128)} %scatter-add.126, f32[8,8,8,192]{3,2,1,0:T(8,128)} %fusion.40, s32[]{:T(128)} %constant.1169.clone.1, s32[]{:T(128)} %constant.1171.clone.1, s32[]{:T(128)} %constant.1170.clone.1, s32[]{:T(128)} %constant.1171.clone.1) | dynamic-update-slice | bytes 786436 | tf_op jit(solution)/shard_map/scatter-add | solution.py:108
  53.6 2.1 fusion.39
  55.7 2.3 fusion.37
  57.9 4.2 %scatter-add.131 = f32[10,10,10,192]{3,2,1,0:T(8,128)} dynamic-update-slice(f32[10,10,10,192]{3,2,1,0:T(8,128)} %fusion.39, f32[8,8,8,192]{3,2,1,0:T(8,128)} %fusion.37, s32[]{:T(128)} %constant.1170.clone.1, s32[]{:T(128)} %constant.1169.clone.1, s32[]{:T(128)} %constant.1169.clone.1, s32[]{:T(128)} %constant.1171.clone.1) | dynamic-update-slice | bytes 786436 | tf_op jit(solution)/shard_map/scatter-add | solution.py:108
  62.1 2.3 fusion.36
  64.4 4.2 %scatter-add.134 = f32[10,10,10,192]{3,2,1,0:T(8,128)} dynamic-update-slice(f32[10,10,10,192]{3,2,1,0:T(8,128)} %scatter-add.131, f32[8,8,8,192]{3,2,1,0:T(8,128)} %fusion.36, s32[]{:T(128)} %constant.1170.clone.1, s32[]{:T(128)} %constant.1169.clone.1, s32[]{:T(128)} %constant.1170.clone.1, s32[]{:T(128)} %constant.1171.clone.1) | dynamic-update-slice | bytes 786436 | tf_op jit(solution)/shard_map/scatter-add | solution.py:108
  68.6 2.1 fusion.35
  70.7 2.3 fusion.33
  72.9 4.2 %scatter-add.136 = f32[10,10,10,192]{3,2,1,0:T(8,128)} dynamic-update-slice(f32[10,10,10,192]{3,2,1,0:T(8,128)} %fusion.35, f32[8,8,8,192]{3,2,1,0:T(8,128)} %fusion.33, s32[]{:T(128)} %constant.1170.clone.1, s32[]{:T(128)} %constant.1170.clone.1, s32[]{:T(128)} %constant.1169.clone.1, s32[]{:T(128)} %constant.1171.clone.1) | dynamic-update-slice | bytes 786436 | tf_op jit(solution)/shard_map/scatter-add | solution.py:108
  77.1 2.3 fusion.32
  79.4 4.2 %scatter-add.139 = f32[10,10,10,192]{3,2,1,0:T(8,128)} dynamic-update-slice(f32[10,10,10,192]{3,2,1,0:T(8,128)} %scatter-add.136, f32[8,8,8,192]{3,2,1,0:T(8,128)} %fusion.32, s32[]{:T(128)} %constant.1170.clone.1, s32[]{:T(128)} %constant.1170.clone.1, s32[]{:T(128)} %constant.1170.clone.1, s32[]{:T(128)} %constant.1171.clone.1) | dynamic-update-slice | bytes 786436 | tf_op jit(solution)/shard_map/scatter-add | solution.py:108
  83.6 2.1 fusion.31
  85.7 2.3 fusion.29
  88.0 4.2 %scatter-add.141 = f32[10,10,10,192]{3,2,1,0:T(8,128)} dynamic-update-slice(f32[10,10,10,192]{3,2,1,0:T(8,128)} %fusion.31, f32[8,8,8,192]{3,2,1,0:T(8,128)} %fusion.29, s32[]{:T(128)} %constant.1170.clone.1, s32[]{:T(128)} %constant.1171.clone.1, s32[]{:T(128)} %constant.1169.clone.1, s32[]{:T(128)} %constant.1171.clone.1) | dynamic-update-slice | bytes 786436 | tf_op jit(solution)/shard_map/scatter-add | solution.py:108
  92.2 2.3 fusion.28
  94.5 4.2 %scatter-add.144 = f32[10,10,10,192]{3,2,1,0:T(8,128)} dynamic-update-slice(f32[10,10,10,192]{3,2,1,0:T(8,128)} %scatter-add.141, f32[8,8,8,192]{3,2,1,0:T(8,128)} %fusion.28, s32[]{:T(128)} %constant.1170.clone.1, s32[]{:T(128)} %constant.1171.clone.1, s32[]{:T(128)} %constant.1170.clone.1, s32[]{:T(128)} %constant.1171.clone.1) | dynamic-update-slice | bytes 786436 | tf_op jit(solution)/shard_map/scatter-add | solution.py:108
  98.7 2.1 fusion.27
  100.8 2.3 fusion.25
  103.1 4.2 %scatter-add.146 = f32[10,10,10,192]{3,2,1,0:T(8,128)} dynamic-update-slice(f32[10,10,10,192]{3,2,1,0:T(8,128)} %fusion.27, f32[8,8,8,192]{3,2,1,0:T(8,128)} %fusion.25, s32[]{:T(128)} %constant.1171.clone.1, s32[]{:T(128)} %constant.1169.clone.1, s32[]{:T(128)} %constant.1169.clone.1, s32[]{:T(128)} %constant.1171.clone.1) | dynamic-update-slice | bytes 786436 | tf_op jit(solution)/shard_map/scatter-add | solution.py:108
  107.3 2.3 fusion.24
  109.5 4.2 %scatter-add.149 = f32[10,10,10,192]{3,2,1,0:T(8,128)} dynamic-update-slice(f32[10,10,10,192]{3,2,1,0:T(8,128)} %scatter-add.146, f32[8,8,8,192]{3,2,1,0:T(8,128)} %fusion.24, s32[]{:T(128)} %constant.1171.clone.1, s32[]{:T(128)} %constant.1169.clone.1, s32[]{:T(128)} %constant.1170.clone.1, s32[]{:T(128)} %constant.1171.clone.1) | dynamic-update-slice | bytes 786436 | tf_op jit(solution)/shard_map/scatter-add | solution.py:108
  113.7 2.1 fusion.23
  116.4 4.2 %fusion.21 = f32[8,8,8,192]{3,2,1,0:T(8,128)} fusion(f32[8,8,8,27,192]{4,2,3,1,0:T(8,128)} %copy-done.4, f32[10,10,10,192]{3,2,1,0:T(8,128)} %fusion.23, s32[]{:T(128)} %bitcast.29, s32[]{:T(128)} %bitcast.30, s32[]{:T(128)} %bitcast.31), kind=kLoop, calls=%fused_computation.40 | loop fusion | flops 98304 | bytes 1179660 | tf_op jit(solution)/shard_map/add | solution.py:108
  120.7 6.1 %scatter-add.151 = f32[10,10,10,192]{3,2,1,0:T(8,128)} dynamic-update-slice(f32[10,10,10,192]{3,2,1,0:T(8,128)} %fusion.23, f32[8,8,8,192]{3,2,1,0:T(8,128)} %fusion.21, s32[]{:T(128)} %bitcast.29, s32[]{:T(128)} %bitcast.30, s32[]{:T(128)} %bitcast.31, s32[]{:T(128)} %constant.1171.clone.1) | dynamic-update-slice | bytes 786436 | tf_op jit(solution)/shard_map/scatter-add | solution.py:108
  126.8 2.3 fusion.20
  129.1 4.2 %scatter-add.154 = f32[10,10,10,192]{3,2,1,0:T(8,128)} dynamic-update-slice(f32[10,10,10,192]{3,2,1,0:T(8,128)} %scatter-add.151, f32[8,8,8,192]{3,2,1,0:T(8,128)} %fusion.20, s32[]{:T(128)} %constant.1171.clone.1, s32[]{:T(128)} %constant.1170.clone.1, s32[]{:T(128)} %constant.1170.clone.1, s32[]{:T(128)} %constant.1171.clone.1) | dynamic-update-slice | bytes 786436 | tf_op jit(solution)/shard_map/scatter-add | solution.py:108
  133.3 2.1 fusion.19
  135.4 2.3 fusion.17
  137.7 4.2 %scatter-add.156 = f32[10,10,10,192]{3,2,1,0:T(8,128)} dynamic-update-slice(f32[10,10,10,192]{3,2,1,0:T(8,128)} %fusion.19, f32[8,8,8,192]{3,2,1,0:T(8,128)} %fusion.17, s32[]{:T(128)} %constant.1171.clone.1, s32[]{:T(128)} %constant.1171.clone.1, s32[]{:T(128)} %constant.1169.clone.1, s32[]{:T(128)} %constant.1171.clone.1) | dynamic-update-slice | bytes 786436 | tf_op jit(solution)/shard_map/scatter-add | solution.py:108
  141.8 2.3 fusion.16
  144.1 4.2 %scatter-add.159 = f32[10,10,10,192]{3,2,1,0:T(8,128)} dynamic-update-slice(f32[10,10,10,192]{3,2,1,0:T(8,128)} %scatter-add.156, f32[8,8,8,192]{3,2,1,0:T(8,128)} %fusion.16, s32[]{:T(128)} %constant.1171.clone.1, s32[]{:T(128)} %constant.1171.clone.1, s32[]{:T(128)} %constant.1170.clone.1, s32[]{:T(128)} %constant.1171.clone.1) | dynamic-update-slice | bytes 786436 | tf_op jit(solution)/shard_map/scatter-add | solution.py:108
  148.3 2.1 fusion.15
  153.6 4.8 %collective-permute-start = (bf16[1,18,10,192]{3,2,1,0:T(8,128)(2,1)}, bf16[1,18,10,192]{3,2,1,0:T(8,128)(2,1)S(1)}, u32[]{:S(2)}, u32[]{:S(2)}) collective-permute-start(bf16[1,18,10,192]{3,2,1,0:T(8,128)(2,1)} %get-tuple-element.431), channel_id=1, source_target_pairs={{0,8},{8,16},{16,24},{1,9},{9,17},{17,25},{2,10},{10,18},{18,26},{... | collective-permute-start | bytes 207368 | tf_op jit(solution)/shard_map/ppermute | solution.py:17
  159.9 1.7 slice.1698
  163.4 3.4 collective-permute-done.1
  171.1 3.2 collective-permute-done.3
  174.3 1.7 fusion.57
  176.0 1.6 fusion.56
  177.5 1.6 fusion.55
  179.2 1.6 fusion.54
  182.1 3.2 fusion.58
  190.1 3.4 collective-permute-start.4
  195.4 4.4 %collective-permute-done.5 = bf16[1,16,8,192]{3,2,1,0:T(8,128)(2,1)S(1)} collective-permute-done((bf16[1,16,8,192]{3,2,1,0:T(8,128)(2,1)S(1)}, bf16[1,16,8,192]{3,2,1,0:T(8,128)(2,1)S(1)}, u32[]{:S(2)}, u32[]{:S(2)}) %collective-permute-start.5) | collective-permute-done | bytes 49184 | tf_op jit(solution)/shard_map/ppermute | solution.py:20
  199.9 4.2 %collective-permute-start.6 = (bf16[18,1,8,192]{3,2,1,0:T(8,128)(2,1)S(1)}, bf16[18,1,8,192]{3,2,1,0:T(8,128)(2,1)S(1)}, u32[]{:S(2)}, u32[]{:S(2)}) collective-permute-start(bf16[18,1,8,192]{3,2,1,0:T(8,128)(2,1)S(1)} %get-tuple-element.434), channel_id=1, source_target_pairs={{0,1},{1,2},{2,3},{3,4},{4,5},{5,6},{6,7},{8,9},{9,10},{10,11},{11... | collective-permute-start | bytes 165896 | tf_op jit(solution)/shard_map/ppermute | solution.py:17
  206.1 2.1 collective-permute-done.7
  209.4 2.4 fusion.64
  213.3 10.1 %concatenate.141 = bf16[512,5184]{1,0:T(8,128)(2,1)} concatenate(bf16[512,192]{1,0:T(8,128)(2,1)} %bitcast.301, bf16[512,192]{1,0:T(8,128)(2,1)} %bitcast.300, bf16[512,192]{1,0:T(8,128)(2,1)} %bitcast.299, bf16[512,192]{1,0:T(8,128)(2,1)} %bitcast.298, bf16[512,192]{1,0:T(8,128)(2,1)} %bitcast.297, bf16[512,192]{1,0:T(8,128)(2,1)} %bitcast.296, bf16[512,192]{1,0:T(8,128)(2,1)} %bitcast.295, ...), dimensions={1} | concatenate | bytes 10616832 | tf_op jit(solution)/shard_map/concatenate | solution.py:41
  223.3 8.1 %copy.65 = bf16[5184,512]{1,0:T(8,128)(2,1)} copy(bf16[5184,512]{0,1:T(8,128)(2,1)} %bitcast.271) | data formatting | bytes 10616832 | tf_op jit(solution)/shard_map/vk,vi->ki/dot_general | solution.py:130
  231.4 6.4 %convolution_bitcast_fusion = f32[192,27,192]{2,0,1:T(8,128)} fusion(bf16[27,192,512]{2,1,0:T(8,128)(2,1)} %bitcast.272, bf16[1,192,512]{1,2,0:T(8,128)(2,1)S(1)} %bitcast_multiply_fusion), kind=kOutput, calls=%fused_computation.11 | convolution fusion | flops 1019215872 | bytes 9486336 | tf_op jit(solution)/shard_map/vk,vi->ki/dot_general | solution.py:130
  239.6 5.1 %fusion.4 = bf16[1,1,1,192,512]{4,3,2,1,0:T(8,128)(2,1)} fusion(bf16[512,5184]{1,0:T(8,128)(2,1)} %concatenate.141, bf16[5184,192]{1,0:T(8,128)(2,1)S(1)} %bitcast.270, f32[512]{0:T(512)S(1)} %convert_element_type.74), kind=kOutput, calls=%fused_computation.16 | convolution fusion | flops 1019412480 | bytes 7497728 | tf_op jit(solution)/shard_map/dot_general | solution.py:128
  244.8 143.4 %all-reduce.4.cloned.1.call-done = f32[192,27,192]{2,0,1:T(8,128)} async-done(((f32[192,27,192]{2,0,1:T(8,128)}), f32[192,27,192]{2,0,1:T(8,128)}) %all-reduce.4.cloned.1.call-update) | async-done | bytes 3981328 | tf_op jit(solution)/shard_map/psum | solution.py:134
  388.2 1.6 dynamic-slice_multiply_fusion
  (58 shorter events, 30.9 us)
Async XLA Ops:
  7.2 2.8 copy-start
  7.2 381.0 %all-reduce.4.cloned.1.call-start = ((), (), s32[]{:S(2)}) async-start(), calls=%async_computation | async-start | bytes 10616832 | tf_op jit(solution)/shard_map/psum | solution.py:134
  12.0 5.1 %copy-start.4 = (f32[8,8,8,27,192]{4,2,3,1,0:T(8,128)}, f32[8,8,8,27,192]{4,2,3,1,0:T(8,128)S(1)}, u32[]{:S(2)}) copy-start(f32[8,8,8,27,192]{4,2,3,1,0:T(8,128)S(1)} %fusion) | copy-start | bytes 31850500
  150.4 1.4 copy-start.3
  152.0 7.9 %copy-start.5 = (f32[18,18,10,192]{3,2,1,0:T(8,128)}, f32[18,18,10,192]{3,2,1,0:T(8,128)S(1)}, u32[]{:S(2)}) copy-start(f32[18,18,10,192]{3,2,1,0:T(8,128)S(1)} %constant_dynamic-update-slice_fusion.1) | copy-start | bytes 7464964
  152.4 9.2 %copy-start.1 = (bf16[18,18,10,192]{3,2,1,0:T(8,128)(2,1)}, bf16[18,18,10,192]{3,2,1,0:T(8,128)(2,1)S(1)}, u32[]{:S(2)}) copy-start(bf16[18,18,10,192]{3,2,1,0:T(8,128)(2,1)S(1)} %convert_element_type.72) | copy-start | bytes 3732484
  153.6 9.8 %collective-permute-start = (bf16[1,18,10,192]{3,2,1,0:T(8,128)(2,1)}, bf16[1,18,10,192]{3,2,1,0:T(8,128)(2,1)S(1)}, u32[]{:S(2)}, u32[]{:S(2)}) collective-permute-start(bf16[1,18,10,192]{3,2,1,0:T(8,128)(2,1)} %get-tuple-element.431), channel_id=1, source_target_pairs={{0,8},{8,16},{16,24},{1,9},{9,17},{17,25},{2,10},{10,18},{18,26},{... | collective-permute-start | bytes 207368 | tf_op jit(solution)/shard_map/ppermute | solution.py:17
  158.4 4.2 %copy-start.7 = (s32[4]{0:T(128)S(1)}, s32[4]{0:T(128)}, u32[]{:S(2)}) copy-start(s32[4]{0:T(128)} %constant.1179.clone.1) | copy-start | bytes 52
  158.4 8.4 %collective-permute-start.1 = (bf16[1,18,10,192]{3,2,1,0:T(8,128)(2,1)}, bf16[1,18,10,192]{3,2,1,0:T(8,128)(2,1)S(1)}, u32[]{:S(2)}, u32[]{:S(2)}) collective-permute-start(bf16[1,18,10,192]{3,2,1,0:T(8,128)(2,1)} %get-tuple-element.432), channel_id=1, source_target_pairs={{8,0},{16,8},{24,16},{9,1},{17,9},{25,17},{10,2},{18,10},{26,18},{... | collective-permute-start | bytes 207368 | tf_op jit(solution)/shard_map/ppermute | solution.py:20
  162.7 11.6 %copy-start.2 = (bf16[18,18,10,192]{3,2,1,0:T(8,128)(2,1)S(1)}, bf16[18,18,10,192]{3,2,1,0:T(8,128)(2,1)}, u32[]{:S(2)}) copy-start(bf16[18,18,10,192]{3,2,1,0:T(8,128)(2,1)} %copy-done.1) | copy-start | bytes 3732484
  167.9 3.2 collective-permute-start.2
  169.2 5.1 %collective-permute-start.3 = (bf16[20,1,10,192]{3,2,1,0:T(8,128)(2,1)S(1)}, bf16[20,1,10,192]{3,2,1,0:T(8,128)(2,1)S(1)}, u32[]{:S(2)}, u32[]{:S(2)}) collective-permute-start(bf16[20,1,10,192]{3,2,1,0:T(8,128)(2,1)S(1)} %get-tuple-element.430), channel_id=1, source_target_pairs={{1,0},{2,1},{3,2},{4,3},{5,4},{6,5},{7,6},{9,8},{10,9},{11,10},{12... | collective-permute-start | bytes 230408 | tf_op jit(solution)/shard_map/ppermute | solution.py:20
  190.1 5.3 %collective-permute-start.4 = (bf16[1,16,8,192]{3,2,1,0:T(8,128)(2,1)S(1)}, bf16[1,16,8,192]{3,2,1,0:T(8,128)(2,1)S(1)}, u32[]{:S(2)}, u32[]{:S(2)}) collective-permute-start(bf16[1,16,8,192]{3,2,1,0:T(8,128)(2,1)S(1)} %get-tuple-element.436), channel_id=1, source_target_pairs={{0,8},{8,16},{16,24},{1,9},{9,17},{17,25},{2,10},{10,18},{18,26},{... | collective-permute-start | bytes 147464 | tf_op jit(solution)/shard_map/ppermute | solution.py:17
  193.5 6.3 %collective-permute-start.5 = (bf16[1,16,8,192]{3,2,1,0:T(8,128)(2,1)S(1)}, bf16[1,16,8,192]{3,2,1,0:T(8,128)(2,1)S(1)}, u32[]{:S(2)}, u32[]{:S(2)}) collective-permute-start(bf16[1,16,8,192]{3,2,1,0:T(8,128)(2,1)S(1)} %get-tuple-element.435), channel_id=1, source_target_pairs={{8,0},{16,8},{24,16},{9,1},{17,9},{25,17},{10,2},{18,10},{26,18},{... | collective-permute-start | bytes 147464 | tf_op jit(solution)/shard_map/ppermute | solution.py:20
  199.9 6.2 %collective-permute-start.6 = (bf16[18,1,8,192]{3,2,1,0:T(8,128)(2,1)S(1)}, bf16[18,1,8,192]{3,2,1,0:T(8,128)(2,1)S(1)}, u32[]{:S(2)}, u32[]{:S(2)}) collective-permute-start(bf16[18,1,8,192]{3,2,1,0:T(8,128)(2,1)S(1)} %get-tuple-element.434), channel_id=1, source_target_pairs={{0,1},{1,2},{2,3},{3,4},{4,5},{5,6},{6,7},{8,9},{9,10},{10,11},{11... | collective-permute-start | bytes 165896 | tf_op jit(solution)/shard_map/ppermute | solution.py:17
  204.1 4.1 %collective-permute-start.7 = (bf16[18,1,8,192]{3,2,1,0:T(8,128)(2,1)S(1)}, bf16[18,1,8,192]{3,2,1,0:T(8,128)(2,1)S(1)}, u32[]{:S(2)}, u32[]{:S(2)}) collective-permute-start(bf16[18,1,8,192]{3,2,1,0:T(8,128)(2,1)S(1)} %get-tuple-element.433), channel_id=1, source_target_pairs={{1,0},{2,1},{3,2},{4,3},{5,4},{6,5},{7,6},{9,8},{10,9},{11,10},{12... | collective-permute-start | bytes 165896 | tf_op jit(solution)/shard_map/ppermute | solution.py:20
  237.9 0.9 copy-start.6
Sparse Core Ops, SparseCore 0:
  238.0 150.0 all-reduce.3
where the time goes:
time: 401 us; the launch traced here: 398 us
  waiting for transfers between devices  157 us (39%)
  local copies, waits for them, and re-layouts  113 us (28%)
  other arithmetic  79.6 us (20%)
  starting transfers between devices  19.1 us (5%)
  between operations  15.2 us (4%)
  matrix products  13.6 us (3%)
    psum x1, waiting for transfers between devices, shards(): summed = lax.psum(weight_sum, ('gx', 'gy'))  143 us
    scatter-add x18, local copies, waits for them, and re-layouts, shards(): spread = spread.at[2 - tap_x:2 - tap_x + BE, 2 - tap_y:2 - tap_y + BE, 2...  74.3 us
    add x17, other arithmetic, shards(): spread = spread.at[2 - tap_x:2 - tap_x + BE, 2 - tap_y:2 - tap_y + BE, 2...  39.5 us
    scatter-add x9, other arithmetic, shards(): spread = spread.at[2 - tap_x:2 - tap_x + BE, 2 - tap_y:2 - tap_y + BE, 2...  19 us
    ppermute x4, starting transfers between devices, extended(): lax.ppermute(lax.slice_in_dim(block, block.shape[dim] - width, None, axis...  13.7 us
    ppermute x4, waiting for transfers between devices, extended(): lax.ppermute(lax.slice_in_dim(block, 0, width, axis=dim), axis, backward)  13.1 us
    unnamed x20, local copies, waits for them, and re-layouts  10.6 us
    concatenate x1, local copies, waits for them, and re-layouts, tap_columns(): return jnp.concatenate(pieces, axis=1)  10.1 us
  transfers between devices with their start and end apart: 9, of which 6 were waited for; matrix products, arithmetic and copies ran while one was open for 3% of the time, Pallas kernels for 0%

commit v1 on v0

v1 whole, which is shorter than its diff:
```python
import functools

import jax
import jax.numpy as jnp
from jax import lax
from jax.experimental import pallas as pl
from jax.experimental.pallas import tpu as pltpu
from jax.sharding import PartitionSpec as P

BE = 8
PLANE = BE * BE
VOX = BE * PLANE
BF = jnp.bfloat16
F32 = jnp.float32
NT = (((1,), (1,)), ((), ()))


def call(body, outs, ins, scratch=(), flops=0, smem=()):
    specs = [
        pl.BlockSpec(memory_space=pltpu.SMEM if k in smem else pltpu.VMEM)
        for k in range(len(ins))
    ]
    moved = sum(a.size * a.dtype.itemsize for a in ins)
    moved += sum(a.size * a.dtype.itemsize for a in outs)
    return pl.pallas_call(
        body,
        out_shape=tuple(outs),
        in_specs=specs,
        out_specs=tuple(pl.BlockSpec(memory_space=pltpu.VMEM) for _ in outs),
        scratch_shapes=list(scratch),
        compiler_params=pltpu.CompilerParams(vmem_limit_bytes=48 * 1024 * 1024),
        cost_estimate=pl.CostEstimate(flops=flops, bytes_accessed=moved, transcendentals=0),
    )(*ins)


def shape(dims, dtype):
    return jax.ShapeDtypeStruct(dims, dtype)


X_ROWS = 3 * PLANE + 16
Y_XM, Y_COT = 12 * 16, 10 * BE
Y_ROWS = Y_XM + Y_COT + 16


def spot(pos_ref):
    pos = pos_ref[0]
    return pos >> 1, pos & 1


def prep_body(pos_ref, feat_ref, occ_ref, cot_ref, xm_ref, cm_ref, up_ref, down_ref):
    px, py = spot(pos_ref)
    live = occ_ref[...].astype(F32)
    channels = feat_ref.shape[0]
    xm = (feat_ref[...].astype(F32) * live).T.astype(BF)
    cm = (cot_ref[...].astype(F32) * live).T.astype(BF)
    xm_ref[...] = xm
    cm_ref[...] = cm
    at_high = jnp.full((1, channels), px, jnp.int32).astype(F32).astype(BF)
    at_low = 1 - at_high
    flag = jnp.full((16, channels), py, jnp.int32).astype(F32).astype(BF)
    up_ref[0 : 2 * PLANE] = xm[VOX - 2 * PLANE :] * at_high
    up_ref[2 * PLANE : 3 * PLANE] = cm[VOX - PLANE :] * at_high
    up_ref[3 * PLANE :] = flag
    down_ref[0 : 2 * PLANE] = xm[: 2 * PLANE] * at_low
    down_ref[2 * PLANE : 3 * PLANE] = cm[:PLANE] * at_low
    down_ref[3 * PLANE :] = flag


def weights_body(w_ref, wt_ref):
    def one(tap, carry):
        wt_ref[tap] = w_ref[tap].astype(F32).T.astype(BF)
        return carry

    lax.fori_loop(0, w_ref.shape[0], one, 0)


def x_planes(recv_ref, valid):
    channels = recv_ref.shape[1]
    xm = recv_ref[0 : 2 * PLANE].reshape(2, PLANE, channels) * valid
    cot = recv_ref[2 * PLANE : 3 * PLANE].astype(F32).reshape(1, PLANE, channels) * valid.astype(F32)
    flag = recv_ref[3 * PLANE : 3 * PLANE + 1].reshape(1, 1, channels)
    return xm, cot, (1 - flag, flag)


def scalar_rows(value, channels):
    return jnp.full((1, 1, channels), value, jnp.int32).astype(F32).astype(BF)


def strips_body(pos_ref, xm_ref, cm_ref, low_ref, high_ref, up_ref, down_ref):
    px, py = spot(pos_ref)
    channels = xm_ref.shape[1]
    one = scalar_rows(1, channels)
    own_at = (scalar_rows(1 - py, channels), scalar_rows(py, channels))
    xl, cl, at_l = x_planes(low_ref, one)
    xh, ch, at_h = x_planes(high_ref, one)
    own = xm_ref[...].reshape(BE, PLANE, channels)
    cot = cm_ref[...].astype(F32).reshape(BE, PLANE, channels)
    flag = jnp.full((16, channels), px, jnp.int32).astype(F32).astype(BF)
    for side, out in ((1, up_ref), (0, down_ref)):
        rows = slice(PLANE - 16, PLANE) if side else slice(0, 16)
        line = slice(PLANE - BE, PLANE) if side else slice(0, BE)
        out[0:32] = (xl[:, rows] * at_l[side]).reshape(32, channels)
        out[32:160] = (own[:, rows] * own_at[side]).reshape(128, channels)
        out[160:192] = (xh[:, rows] * at_h[side]).reshape(32, channels)
        lines = jnp.concatenate(
            [
                cl[:, line] * at_l[side].astype(F32),
                cot[:, line] * own_at[side].astype(F32),
                ch[:, line] * at_h[side].astype(F32),
            ],
            axis=0,
        )
        out[Y_XM : Y_XM + Y_COT] = lines.reshape(Y_COT, channels).astype(BF)
        out[Y_XM + Y_COT :] = flag


def y_rows(recv_ref, px, channels):
    strip = recv_ref[0:Y_XM].reshape(12, 16, channels)
    lines = recv_ref[Y_XM : Y_XM + Y_COT].astype(F32).reshape(10, BE, channels)
    flag = recv_ref[Y_XM + Y_COT : Y_XM + Y_COT + 1].reshape(1, 1, channels)
    zero_at, one_at = 1 - flag, flag
    here_high = scalar_rows(px, channels)
    here_low = 1 - here_high
    same = zero_at * here_low + one_at * here_high
    xm = jnp.concatenate(
        [
            strip[0:2] * here_low + strip[8:10] * (zero_at * here_high),
            strip[2:10] * same,
            strip[10:12] * here_high + strip[2:4] * (one_at * here_low),
        ],
        axis=0,
    )
    f = lambda v: v.astype(F32)
    cot = jnp.concatenate(
        [
            lines[0:1] * f(here_low) + lines[8:9] * f(zero_at * here_high),
            lines[1:9] * f(same),
            lines[9:10] * f(here_high) + lines[1:2] * f(one_at * here_low),
        ],
        axis=0,
    )
    return xm, cot


def window_body(pos_ref, xm_ref, cm_ref, xlow_ref, xhigh_ref, ylow_ref, yhigh_ref, even_ref, odd_ref, cot_ref, ring_ref):
    px, py = spot(pos_ref)
    channels = xm_ref.shape[1]
    f = lambda v: v.astype(F32)
    high_x, high_y = scalar_rows(px, channels), scalar_rows(py, channels)
    low_x, low_y = 1 - high_x, 1 - high_y
    xl, cl, at_l = x_planes(xlow_ref, low_x)
    xh, ch, at_h = x_planes(xhigh_ref, high_x)
    sl, tl = y_rows(ylow_ref, px, channels)
    sh, th = y_rows(yhigh_ref, px, channels)
    own = xm_ref[...].reshape(BE, PLANE, channels)
    cot = cm_ref[...].astype(F32).reshape(BE, PLANE, channels)
    same_l = at_l[0] * low_y + at_l[1] * high_y
    same_h = at_h[0] * low_y + at_h[1] * high_y
    none8 = jnp.zeros((BE, 16, channels), BF)
    own_low = jnp.concatenate([xl[:, 48:64] * at_l[0], none8, xh[:, 48:64] * at_h[0]], axis=0)
    own_high = jnp.concatenate([xl[:, 0:16] * at_l[1], none8, xh[:, 0:16] * at_h[1]], axis=0)
    below = sl * low_y + own_low * high_y
    above = sh * high_y + own_high * low_y
    mid = jnp.concatenate([xl * same_l, own, xh * same_h], axis=0)
    even_ref[:, 0:16] = below
    even_ref[:, 16:80] = mid
    even_ref[:, 80:96] = above
    odd = jnp.concatenate([f(below)[:, 8:16], f(mid), f(above)[:, 0:8]], axis=1).astype(BF)
    odd_ref[...] = odd
    ring = odd[1:11].reshape(800, channels)
    if channels % 128 == 64:
        cut = channels - 64
        ring_ref[0:800, :] = ring[:, :cut]
        ring_ref[800:, 0:64] = ring[0:400, cut:]
        ring_ref[800:, 64:128] = ring[400:800, cut:]
    else:
        ring_ref[...] = ring
    none8 = jnp.zeros((BE, BE, channels), F32)
    cot_low = jnp.concatenate([cl[:, 56:64] * f(at_l[0]), none8, ch[:, 56:64] * f(at_h[0])], axis=0)
    cot_high = jnp.concatenate([cl[:, 0:8] * f(at_l[1]), none8, ch[:, 0:8] * f(at_h[1])], axis=0)
    cot_below = tl * f(low_y) + cot_low * f(high_y)
    cot_above = th * f(high_y) + cot_high * f(low_y)
    cot_mid = jnp.concatenate([cl * f(same_l), cot, ch * f(same_h)], axis=0)
    cot_ref[...] = jnp.concatenate([cot_below, cot_mid, cot_above], axis=1).astype(BF)


def unpack_ring(ring):
    if ring.shape[0] == 800:
        return ring
    tail = jnp.concatenate([ring[800:, 0:64], ring[800:, 64:128]], axis=0)
    return jnp.concatenate([ring[0:800], tail], axis=1)


def z_shift(values, by):
    moved = pltpu.roll(values, by % BE, 1)
    place = lax.broadcasted_iota(jnp.int32, values.shape, 1)
    keep = place >= by if by > 0 else place < BE + by
    return jnp.where(keep, moved, 0.0)


def forward_body(parts, even_ref, odd_ref, cot_ref, occ_ref, wt_ref, out_ref, slope_ref, rows_ref):
    channels = even_ref.shape[2]
    me = lax.axis_index("gx")

    def taken(a, b):
        if b == 1:
            piece = odd_ref[a : a + 10]
        else:
            piece = even_ref[a : a + 10, 8 * b : 8 * b + 80]
        return piece.reshape(800, channels)

    pre = None
    for c in range(3):
        total = None
        for a in range(3):
            for b in range(3):
                term = jnp.dot(taken(a, b), wt_ref[9 * a + 3 * b + c], preferred_element_type=F32)
                total = term if total is None else total + term
        total = total.reshape(100, BE, channels)
        if c != 1:
            total = z_shift(total, 1 - c)
        pre = total if pre is None else pre + total
    sigma = 1.0 / (1.0 + jnp.exp(-pre))
    cot = cot_ref[...].astype(F32).reshape(100, BE, channels)
    slope = (cot * (sigma * (1.0 + pre * (1.0 - sigma)))).astype(BF)
    slope_ref[...] = slope.reshape(10, 80, channels)
    act = (pre * sigma).reshape(10, 80, channels)[1:9, 8:72].reshape(VOX, channels)
    out_ref[...] = (act.T * occ_ref[...].astype(F32)).astype(BF)
    own = slope.astype(F32).reshape(10, 80, channels)[1:9, 8:72].reshape(VOX, channels).astype(BF)
    block = channels // parts
    row = lax.broadcasted_iota(jnp.int32, (block, channels), 0)
    col = lax.broadcasted_iota(jnp.int32, (block, channels), 1)
    for k in range(parts):
        pick = (col == row + block * lax.bitwise_xor(me, jnp.int32(k))).astype(F32).astype(BF)
        rows_ref[k] = lax.dot_general(pick, own, NT, preferred_element_type=F32).astype(BF)


def backward_body(slope_ref, occ_ref, w_ref, out_ref):
    channels = slope_ref.shape[2]
    slope = slope_ref[...]
    middle = slope.astype(F32)[:, 8:72].astype(BF)
    grad = None
    for c in range(3):
        total = None
        for a in range(3):
            for b in range(3):
                if b == 1:
                    piece = middle[2 - a : 10 - a]
                else:
                    piece = slope[2 - a : 10 - a, 8 * (2 - b) : 8 * (2 - b) + 64]
                piece = piece.reshape(VOX, channels)
                term = jnp.dot(piece, w_ref[9 * a + 3 * b + c], preferred_element_type=F32)
                total = term if total is None else total + term
        total = total.reshape(PLANE, BE, channels)
        if c != 1:
            total = z_shift(total, c - 1)
        grad = total if grad is None else grad + total
    out_ref[...] = (grad.reshape(VOX, channels).T * occ_ref[...].astype(F32)).astype(BF)


def packing(width):
    full = width // 128
    rest = width - 128 * full
    per = 128 // rest if rest else 0
    return full, rest, per, 9 * full + (-(-9 // per) if rest else 0)


def lines_of(slots, rows):
    return -(-slots * rows // 16) * 16


def kernel_grad_body(parts, chips, *refs):
    rings, lines = refs[:parts], refs[parts]
    others = refs[parts + 1 : 2 * parts]
    outs = refs[2 * parts :]
    channels = 128 + (rings[0].shape[0] - 800) * 64 // 400 if rings[0].shape[0] > 800 else rings[0].shape[1]
    block = channels // parts
    width = 3 * block
    place = lax.broadcasted_iota(jnp.int32, (block, VOX), 1) & (BE - 1)
    left, windows = [], []
    for k in range(parts):
        g = (lines[0] if k == 0 else others[k - 1][...]).astype(F32)
        back = jnp.where(place < BE - 1, pltpu.roll(g, VOX - 1, 1), 0.0)
        ahead = jnp.where(place > 0, pltpu.roll(g, 1, 1), 0.0)
        left.append(jnp.concatenate([back, g, ahead], axis=0).astype(BF))
        ring = unpack_ring(rings[k][...]).reshape(10, 80, channels)
        windows.append((ring, ring.astype(F32)[:, 8:72].astype(BF)))
    left = jnp.concatenate(left, axis=1)
    full, rest, per, slots = packing(width)
    leftover = []
    store = outs[-1]
    for a in range(3):
        for b in range(3):
            right = []
            for ring, middle in windows:
                piece = middle[a : a + 8] if b == 1 else ring[a : a + 8, 8 * b : 8 * b + 64]
                right.append(piece.reshape(VOX, channels))
            total = jnp.dot(left, jnp.concatenate(right, axis=0), preferred_element_type=F32).T
            for n in range(full):
                store[(3 * a + b) * full + n] = total[:, 128 * n : 128 * n + 128]
            if rest:
                leftover.append(total[:, 128 * full :])
    if rest:
        for n in range(slots - 9 * full):
            some = leftover[n * per : (n + 1) * per]
            spare = 128 - rest * len(some)
            if spare:
                some = some + [jnp.zeros((channels, spare), F32)]
            store[9 * full + n] = jnp.concatenate(some, axis=1)
    if len(outs) == 1:
        return
    send_ref, keep_ref, _ = outs
    rows = channels // (2 * chips)
    count = lines_of(slots, rows)
    core = lax.axis_index("gy") & 1
    pad = [jnp.zeros((count - slots * rows, 128), F32)] if count > slots * rows else []
    for chip in range(chips):
        for whose, out in ((1 - core, send_ref), (core, keep_ref)):
            start = pl.multiple_of(rows * (2 * chip + whose), 8)
            piece = store[:, pl.ds(start, rows), :].reshape(slots * rows, 128)
            out[chip] = jnp.concatenate([piece] + pad, axis=0).astype(out.dtype)


def pair_body(chips, keep_ref, recv_ref, own_ref, send_ref):
    me = lax.axis_index("gy") >> 1
    own_ref[...] = keep_ref[me] + recv_ref[me].astype(F32)
    for k in range(1, chips):
        it = lax.bitwise_xor(me, jnp.int32(k))
        send_ref[k - 1] = (keep_ref[it] + recv_ref[it].astype(F32)).astype(BF)


def last_body(slots, width, scale, *refs):
    out_ref = refs[-1]
    total = refs[0][...]
    for other in refs[1:-1]:
        total = total + other[...].astype(F32)
    total = total * scale
    rows, block = out_ref.shape[1], width // 3
    full, rest, per, _ = packing(width)
    for ab in range(9):
        parts = [total[rows * (ab * full + n) : rows * (ab * full + n + 1)] for n in range(full)]
        if rest:
            at = rows * (9 * full + ab // per)
            lane = rest * (ab % per)
            parts.append(total[at : at + rows, lane : lane + rest])
        line = parts[0] if len(parts) == 1 else jnp.concatenate(parts, axis=1)
        for c in range(3):
            out_ref[3 * ab + c] = line[:, block * c : block * (c + 1)]


def xor_step(value, axis, step):
    count = lax.axis_size(axis)
    return lax.ppermute(value, axis, [(i, i ^ step) for i in range(count)])


def both_ways(up, down, axis):
    count = lax.axis_size(axis)
    forward = [(i, i + 1) for i in range(count - 1)]
    backward = [(i + 1, i) for i in range(count - 1)]
    return lax.ppermute(up, axis, forward), lax.ppermute(down, axis, backward)


def shards(features, occupancy, brick_pos, weight, cotangent):
    channels = features.shape[3]
    parts, line = lax.axis_size("gx"), lax.axis_size("gy")
    chips = line // 2
    block, rows = channels // parts, channels // line
    feat = features.reshape(channels, VOX)
    cot = cotangent.reshape(channels, VOX)
    occ = occupancy.reshape(1, VOX)
    pos = brick_pos.reshape(1)
    taps = weight.transpose(1, 0, 2)

    brick = shape((VOX, channels), BF)
    face = shape((X_ROWS, channels), BF)
    xm, cm, up, down = call(prep_body, [brick, brick, face, face], [pos, feat, occ, cot], smem=(0,))
    low, high = both_ways(up, down, "gx")
    (taps_t,) = call(weights_body, [shape(taps.shape, BF)], [taps], flops=taps.size * 64)
    strip = shape((Y_ROWS, channels), BF)
    up, down = call(strips_body, [strip, strip], [pos, xm, cm, low, high], smem=(0,))
    ylow, yhigh = both_ways(up, down, "gy")
    packed = (1200, channels - 64) if channels % 128 == 64 else (800, channels)
    even, odd, wide_cot, ring = call(
        window_body,
        [
            shape((12, 96, channels), BF),
            shape((12, 80, channels), BF),
            shape((10, 80, channels), BF),
            shape(packed, BF),
        ],
        [pos, xm, cm, low, high, ylow, yhigh],
        smem=(0,),
    )
    rings = [ring] + [xor_step(ring, "gx", k) for k in range(1, parts)]
    flops = 2 * VOX * 27 * channels * channels
    output, slope, lines = call(
        functools.partial(forward_body, parts),
        [
            shape((channels, VOX), BF),
            shape((10, 80, channels), BF),
            shape((parts, block, VOX), BF),
        ],
        [even, odd, wide_cot, occ, taps_t],
        flops=flops * 3 // 2,
    )
    others = [xor_step(lines[k], "gx", k) for k in range(1, parts)]
    (x_grad,) = call(backward_body, [shape((channels, VOX), BF)], [slope, occ, taps], flops=flops)

    width = 3 * block
    slots = packing(width)[3]
    count = lines_of(slots, rows)
    body = functools.partial(kernel_grad_body, parts, chips)
    table = (slots, channels, 128)
    if rows % 8 == 0:
        send, keep = call(
            body,
            [shape((chips, count, 128), BF), shape((chips, count, 128), F32)],
            rings + [lines] + others,
            scratch=[pltpu.VMEM(table, F32)],
            flops=flops,
        )
    else:
        (store,) = call(body, [shape(table, F32)], rings + [lines] + others, flops=flops)
        store = store.reshape(slots, chips, 2, rows, 128).transpose(2, 1, 0, 3, 4)
        store = store.reshape(2, chips, slots * rows, 128)
        store = jnp.pad(store, ((0, 0), (0, 0), (0, count - slots * rows), (0, 0)))
        core = lax.axis_index("gy") & 1
        keep = lax.dynamic_index_in_dim(store, core, 0, False)
        send = lax.dynamic_index_in_dim(store, 1 - core, 0, False).astype(BF)
    recv = xor_step(send, "gy", 1)
    own, sends = call(
        functools.partial(pair_body, chips),
        [shape((count, 128), F32), shape((chips - 1, count, 128), BF)],
        [keep, recv],
    )
    came = [xor_step(sends[k - 1], "gy", 2 * k) for k in range(1, chips)]
    (w_grad,) = call(
        functools.partial(last_body, slots, width, 1.0 / (parts * line)),
        [shape((27, rows, block), F32)],
        [own] + came,
    )
    return (
        output.reshape(features.shape),
        x_grad.reshape(features.shape),
        w_grad.transpose(2, 0, 1),
    )


def solution(mesh):
    placed = (
        P("gx", "gy", None, None, None),
        P("gx", "gy", None, None),
        P("gx", "gy", None),
        P(),
        P("gx", "gy", None, None, None),
    )
    return jax.shard_map(
        shards,
        mesh=mesh,
        in_specs=placed,
        out_specs=(
            P("gx", "gy", None, None, None),
            P("gx", "gy", None, None, None),
            P("gx", None, "gy"),
        ),
        check_vma=False,
    )
```

time: 401 us -> 64.6 us (0.16)
  waiting for transfers between devices: 157 us -> 19.5 us
  local copies, waits for them, and re-layouts: 113 us -> 4.31 us
  other arithmetic: 79.6 us -> 0 us
  Pallas kernels: 0 us -> 14.6 us
  between operations: 15.2 us -> 1.4 us
  matrix products: 13.6 us -> 0 us
  starting transfers between devices: 19.1 us -> 24.4 us
    psum x1 -> x0, waiting for transfers between devices: 143 us -> none  [shards(): summed = lax.psum(weight_sum, ('gx', 'gy'))]
    scatter-add x18 -> x0, local copies, waits for them, and re-layouts: 74.3 us -> none  [shards(): spread = spread.at[2 - tap_x:2 - tap_x + BE, 2 - tap_y:2 - tap_y + BE, 2...]
    add x17 -> x0, other arithmetic: 39.5 us -> none  [shards(): spread = spread.at[2 - tap_x:2 - tap_x + BE, 2 - tap_y:2 - tap_y + BE, 2...]
    scatter-add x17 -> x0, other arithmetic: 32.6 us -> none  [the longest x9 19 us: shards(): spread = spread.at[2 - tap_x:2 - tap_x + BE, 2 - tap_y:2 - tap_y + BE, 2...]
    pallas_call x0 -> x9, Pallas kernels: none -> 14.6 us  [call(): pl.pallas_call(body, out_shape=tuple(outs), in_specs=specs, out_specs=tup...]
    dot_general x3 -> x0, matrix products: 13.6 us -> none  [the longest x1 6.44 us: shards(): jnp.einsum('vk,vi->ki', columns, masked[slot_id], preferred_element_type=...]
    concatenate x1 -> x0, local copies, waits for them, and re-layouts: 10.1 us -> none  [tap_columns(): return jnp.concatenate(pieces, axis=1)]
    dot_general x1 -> x0, local copies, waits for them, and re-layouts: 8.13 us -> none  [shards(): jnp.einsum('vk,vi->ki', columns, masked[slot_id], preferred_element_type=...]
  transfers between devices with their start and end apart: 9 -> 14, of which waited for: 6 -> 7; matrix products, arithmetic and copies ran while one was open for 3% -> 0% of each run, Pallas kernels for 0% -> 17%
where the time goes in v1:
time: 64.6 us; the launch traced here: 64.3 us
  starting transfers between devices  24.4 us (38%)
  waiting for transfers between devices  19.5 us (30%)
  Pallas kernels  14.6 us (23%)
  local copies, waits for them, and re-layouts  4.31 us (7%)
  between operations  1.4 us (2%)
    ppermute x10, starting transfers between devices, xor_step(): return lax.ppermute(value, axis, [(i, i ^ step) for i in range(count)])  15.7 us
    pallas_call x9, Pallas kernels, call(): pl.pallas_call(body, out_shape=tuple(outs), in_specs=specs, out_specs=tup...  14.6 us
    ppermute x10, waiting for transfers between devices, xor_step(): return lax.ppermute(value, axis, [(i, i ^ step) for i in range(count)])  14.2 us
    ppermute x4, starting transfers between devices, both_ways(): return (lax.ppermute(up, axis, forward), lax.ppermute(down, axis, backward))  8.73 us
    ppermute x4, waiting for transfers between devices, both_ways(): return (lax.ppermute(up, axis, forward), lax.ppermute(down, axis, backward))  5.3 us
    unnamed x12, local copies, waits for them, and re-layouts  4.28 us
  transfers between devices with their start and end apart: 14, of which 7 were waited for; matrix products, arithmetic and copies ran while one was open for 0% of the time, Pallas kernels for 17%

profile of v1, /device:TPU:0, one launch (start us, length us, event | category | flops | bytes accessed | tf_op | source)
XLA Modules:
  0.0 64.3 jit_solution(3477329853496752959)
XLA Ops:
  1.3 0.0 copy-start.2
  1.3 0.9 %copy-done.2 = bf16[1,1,1,192,512]{4,3,2,1,0:T(8,128)(2,1)S(1)} copy-done((bf16[1,1,1,192,512]{4,3,2,1,0:T(8,128)(2,1)S(1)}, bf16[1,1,1,192,512]{4,3,2,1,0:T(8,128)(2,1)}, u32[]{:S(2)}) %copy-start.2) | copy-done | bytes 196632
  2.2 0.0 copy-start.3
  2.2 0.9 %copy-done.3 = bf16[1,1,1,192,512]{4,3,2,1,0:T(8,128)(2,1)S(1)} copy-done((bf16[1,1,1,192,512]{4,3,2,1,0:T(8,128)(2,1)S(1)}, bf16[1,1,1,192,512]{4,3,2,1,0:T(8,128)(2,1)}, u32[]{:S(2)}) %copy-start.3) | copy-done | bytes 196632
  3.1 0.0 copy-start.4
  3.1 0.7 %copy-done.4 = s32[1,1,1,512]{3,2,1,0:T(1,128)S(1)} copy-done((s32[1,1,1,512]{3,2,1,0:T(1,128)S(1)}, s32[1,1,1,512]{3,2,1,0:T(1,128)}, u32[]{:S(2)}) %copy-start.4) | copy-done | bytes 2072
  3.8 0.2 shard_map.76
  4.0 4.8 %collective-permute-start = (bf16[208,192]{1,0:T(8,128)(2,1)S(1)}, bf16[208,192]{1,0:T(8,128)(2,1)S(1)}, u32[]{:S(2)}, u32[]{:S(2)}) collective-permute-start(bf16[208,192]{1,0:T(8,128)(2,1)S(1)} %get-tuple-element.22), channel_id=1, source_target_pairs={{0,8},{8,16},{16,24},{1,9},{9,17},{17,25},{2,10},{10,18},{18,26},{... | collective-permute-start | bytes 239624 | tf_op jit(solution)/shard_map/ppermute | solution.py:360
  8.9 1.3 %collective-permute-start.1 = (bf16[208,192]{1,0:T(8,128)(2,1)S(1)}, bf16[208,192]{1,0:T(8,128)(2,1)S(1)}, u32[]{:S(2)}, u32[]{:S(2)}) collective-permute-start(bf16[208,192]{1,0:T(8,128)(2,1)S(1)} %get-tuple-element.23), channel_id=1, source_target_pairs={{8,0},{16,8},{24,16},{9,1},{17,9},{25,17},{10,2},{18,10},{26,18},{... | collective-permute-start | bytes 239624 | tf_op jit(solution)/shard_map/ppermute | solution.py:360
  10.2 1.0 %collective-permute-done.low_ref.xlow_ref = bf16[208,192]{1,0:T(8,128)(2,1)S(1)} collective-permute-done((bf16[208,192]{1,0:T(8,128)(2,1)S(1)}, bf16[208,192]{1,0:T(8,128)(2,1)S(1)}, u32[]{:S(2)}, u32[]{:S(2)}) %collective-permute-start) | collective-permute-done | bytes 79904 | tf_op jit(solution)/shard_map/ppermute | solution.py:360
  11.2 4.3 %collective-permute-done.1.high_ref.xhigh_ref = bf16[208,192]{1,0:T(8,128)(2,1)S(1)} collective-permute-done((bf16[208,192]{1,0:T(8,128)(2,1)S(1)}, bf16[208,192]{1,0:T(8,128)(2,1)S(1)}, u32[]{:S(2)}, u32[]{:S(2)}) %collective-permute-start.1) | collective-permute-done | bytes 79904 | tf_op jit(solution)/shard_map/ppermute | solution.py:360
  15.5 1.3 %collective-permute-start.2 = (bf16[288,192]{1,0:T(8,128)(2,1)S(1)}, bf16[288,192]{1,0:T(8,128)(2,1)S(1)}, u32[]{:S(2)}, u32[]{:S(2)}) collective-permute-start(bf16[288,192]{1,0:T(8,128)(2,1)S(1)} %get-tuple-element.24), channel_id=1, source_target_pairs={{0,1},{1,2},{2,3},{3,4},{4,5},{5,6},{6,7},{8,9},{9,10},{10,11},{11... | collective-permute-start | bytes 331784 | tf_op jit(solution)/shard_map/ppermute | solution.py:360
  16.8 1.3 %collective-permute-start.3 = (bf16[288,192]{1,0:T(8,128)(2,1)S(1)}, bf16[288,192]{1,0:T(8,128)(2,1)S(1)}, u32[]{:S(2)}, u32[]{:S(2)}) collective-permute-start(bf16[288,192]{1,0:T(8,128)(2,1)S(1)} %get-tuple-element.25), channel_id=1, source_target_pairs={{1,0},{2,1},{3,2},{4,3},{5,4},{6,5},{7,6},{9,8},{10,9},{11,10},{12... | collective-permute-start | bytes 331784 | tf_op jit(solution)/shard_map/ppermute | solution.py:360
  18.1 0.0 copy-start
  18.1 1.7 %copy-done = bf16[192,27,192]{2,0,1:T(8,128)(2,1)S(1)} copy-done((bf16[192,27,192]{2,0,1:T(8,128)(2,1)S(1)}, bf16[192,27,192]{2,0,1:T(8,128)(2,1)}, u32[]{:S(2)}) %copy-start) | copy-done | bytes 1990680
  19.9 0.0 copy-start.5
  19.9 3.7 %shard_map.79.wt_ref = bf16[27,192,192]{2,1,0:T(8,128)(2,1)S(1)} custom-call(bf16[27,192,192]{2,1,0:T(8,128)(2,1)S(1)} %bitcast.23), custom_call_target="tpu_custom_call" | custom-call | flops 63700992 | bytes 3981312 | tf_op jit(solution)/shard_map/pallas_call | solution.py:25
  23.6 0.0 collective-permute-done.2.ylow_ref
  23.6 0.0 collective-permute-done.3.yhigh_ref
  23.6 0.2 shard_map.78
  23.8 2.5 %collective-permute-start.4 = (bf16[1200,128]{1,0:T(8,128)(2,1)S(1)}, bf16[1200,128]{1,0:T(8,128)(2,1)S(1)}, u32[]{:S(2)}, u32[]{:S(2)}) collective-permute-start(bf16[1200,128]{1,0:T(8,128)(2,1)S(1)} %get-tuple-element.31.refs_0_), channel_id=1, source_target_pairs={{0,8},{8,0},{16,24},{24,16},{1,9},{9,1},{17,25},{25,17},{2,10},{10... | collective-permute-start | bytes 921608 | tf_op jit(solution)/shard_map/ppermute | solution.py:353
  26.3 0.0 collective-permute-start.5
  26.3 1.5 %collective-permute-start.6 = (bf16[1200,128]{1,0:T(8,128)(2,1)S(1)}, bf16[1200,128]{1,0:T(8,128)(2,1)S(1)}, u32[]{:S(2)}, u32[]{:S(2)}) collective-permute-start(bf16[1200,128]{1,0:T(8,128)(2,1)S(1)} %get-tuple-element.31.refs_0_), channel_id=1, source_target_pairs={{0,24},{8,16},{16,8},{24,0},{1,25},{9,17},{17,9},{25,1},{2,26},{10... | collective-permute-start | bytes 921608 | tf_op jit(solution)/shard_map/ppermute | solution.py:353
  27.8 0.0 copy-done.5
  27.8 4.6 %shard_map.80 = (bf16[192,512]{1,0:T(8,128)(2,1)}, bf16[10,80,192]{2,1,0:T(8,128)(2,1)S(1)}, bf16[4,48,512]{2,1,0:T(8,128)(2,1)S(1)}) custom-call(bf16[12,96,192]{2,1,0:T(8,128)(2,1)S(1)} %get-tuple-element.26.even_ref, bf16[12,80,192]{2,1,0:T(8,128)(2,1)S(1)} %get-tuple-element.27.odd_ref, bf16[10,80,192]{2,1,0:T(8,128)(2,1)S(1)} %get-tuple-element.28.cot_ref, ...), custom_call_target="tpu_custom_call" | custom-call | flops 1528823808 | bytes 3811328 | tf_op jit(solution)/shard_map/pallas_call | solution.py:25
  32.4 0.0 copy-start.1
  32.4 2.0 %collective-permute-start.7 = (bf16[48,512]{1,0:T(8,128)(2,1)S(1)}, bf16[48,512]{1,0:T(8,128)(2,1)S(1)}, u32[]{:S(2)}, u32[]{:S(2)}) collective-permute-start(bf16[48,512]{1,0:T(8,128)(2,1)S(1)} %get-tuple-element.42), channel_id=1, source_target_pairs={{0,8},{8,0},{16,24},{24,16},{1,9},{9,1},{17,25},{25,17},{2,10},{10... | collective-permute-start | bytes 147464 | tf_op jit(solution)/shard_map/ppermute | solution.py:353
  34.4 0.0 collective-permute-start.8
  34.4 5.3 %collective-permute-done.7.refs_5_ = bf16[48,512]{1,0:T(8,128)(2,1)S(1)} collective-permute-done((bf16[48,512]{1,0:T(8,128)(2,1)S(1)}, bf16[48,512]{1,0:T(8,128)(2,1)S(1)}, u32[]{:S(2)}, u32[]{:S(2)}) %collective-permute-start.7) | collective-permute-done | bytes 49184 | tf_op jit(solution)/shard_map/ppermute | solution.py:353
  39.8 0.6 collective-permute-start.9
  40.4 2.4 %collective-permute-done.8.refs_6_ = bf16[48,512]{1,0:T(8,128)(2,1)S(1)} collective-permute-done((bf16[48,512]{1,0:T(8,128)(2,1)S(1)}, bf16[48,512]{1,0:T(8,128)(2,1)S(1)}, u32[]{:S(2)}, u32[]{:S(2)}) %collective-permute-start.8) | collective-permute-done | bytes 49184 | tf_op jit(solution)/shard_map/ppermute | solution.py:353
  42.8 2.0 %collective-permute-done.9.refs_7_ = bf16[48,512]{1,0:T(8,128)(2,1)S(1)} collective-permute-done((bf16[48,512]{1,0:T(8,128)(2,1)S(1)}, bf16[48,512]{1,0:T(8,128)(2,1)S(1)}, u32[]{:S(2)}, u32[]{:S(2)}) %collective-permute-start.9) | collective-permute-done | bytes 49184 | tf_op jit(solution)/shard_map/ppermute | solution.py:353
  44.8 0.0 collective-permute-done.4.refs_1_
  44.8 0.0 collective-permute-done.5.refs_2_
  44.8 0.0 collective-permute-done.6.refs_3_
  44.8 2.1 %shard_map.82 = (bf16[4,272,128]{2,1,0:T(8,128)(2,1)S(1)}, f32[4,272,128]{2,1,0:T(8,128)S(1)}) custom-call(bf16[1200,128]{1,0:T(8,128)(2,1)S(1)} %get-tuple-element.31.refs_0_, bf16[1200,128]{1,0:T(8,128)(2,1)S(1)} %collective-permute-done.4.refs_1_, bf16[1200,128]{1,0:T(8,128)(2,1)S(1)} %collective-permute-done.5.refs_2_, ...), custom_call_target="tpu_custom_call" | custom-call | flops 1019215872 | bytes 2408448 | tf_op jit(solution)/shard_map/pallas_call | solution.py:25
  46.9 1.3 %collective-permute-start.10 = (bf16[4,272,128]{2,1,0:T(8,128)(2,1)S(1)}, bf16[4,272,128]{2,1,0:T(8,128)(2,1)S(1)}, u32[]{:S(2)}, u32[]{:S(2)}) collective-permute-start(bf16[4,272,128]{2,1,0:T(8,128)(2,1)S(1)} %get-tuple-element.34), channel_id=1, source_target_pairs={{0,1},{1,0},{2,3},{3,2},{4,5},{5,4},{6,7},{7,6},{8,9},{9,8},{10,11... | collective-permute-start | bytes 835592 | tf_op jit(solution)/shard_map/ppermute | solution.py:353
  48.2 1.2 %collective-permute-done.10.recv_ref = bf16[4,272,128]{2,1,0:T(8,128)(2,1)S(1)} collective-permute-done((bf16[4,272,128]{2,1,0:T(8,128)(2,1)S(1)}, bf16[4,272,128]{2,1,0:T(8,128)(2,1)S(1)}, u32[]{:S(2)}, u32[]{:S(2)}) %collective-permute-start.10) | collective-permute-done | bytes 278560 | tf_op jit(solution)/shard_map/ppermute | solution.py:353
  49.4 0.1 shard_map.83
  49.5 5.3 %collective-permute-start.11 = (bf16[272,128]{1,0:T(8,128)(2,1)S(1)}, bf16[272,128]{1,0:T(8,128)(2,1)S(1)}, u32[]{:S(2)}, u32[]{:S(2)}) collective-permute-start(bf16[272,128]{1,0:T(8,128)(2,1)S(1)} %get-tuple-element.39), channel_id=1, source_target_pairs={{0,2},{1,3},{2,0},{3,1},{4,6},{5,7},{6,4},{7,5},{8,10},{9,11},{10,... | collective-permute-start | bytes 208904 | tf_op jit(solution)/shard_map/ppermute | solution.py:353
  54.8 1.4 %collective-permute-start.12 = (bf16[272,128]{1,0:T(8,128)(2,1)S(1)}, bf16[272,128]{1,0:T(8,128)(2,1)S(1)}, u32[]{:S(2)}, u32[]{:S(2)}) collective-permute-start(bf16[272,128]{1,0:T(8,128)(2,1)S(1)} %get-tuple-element.38), channel_id=1, source_target_pairs={{0,4},{1,5},{2,6},{3,7},{4,0},{5,1},{6,2},{7,3},{8,12},{9,13},{10,... | collective-permute-start | bytes 208904 | tf_op jit(solution)/shard_map/ppermute | solution.py:353
  56.2 1.1 %collective-permute-start.13 = (bf16[272,128]{1,0:T(8,128)(2,1)S(1)}, bf16[272,128]{1,0:T(8,128)(2,1)S(1)}, u32[]{:S(2)}, u32[]{:S(2)}) collective-permute-start(bf16[272,128]{1,0:T(8,128)(2,1)S(1)} %get-tuple-element.37), channel_id=1, source_target_pairs={{0,6},{1,7},{2,4},{3,5},{4,2},{5,3},{6,0},{7,1},{8,14},{9,15},{10,... | collective-permute-start | bytes 208904 | tf_op jit(solution)/shard_map/ppermute | solution.py:353
  57.3 0.0 copy-done.1
  57.3 2.7 %shard_map.81 = bf16[192,512]{1,0:T(8,128)(2,1)} custom-call(bf16[10,80,192]{2,1,0:T(8,128)(2,1)S(1)} %get-tuple-element.30.slope_ref, s32[1,512]{1,0:T(1,128)S(1)} %bitcast.29, bf16[27,192,192]{2,1,0:T(8,128)(2,1)S(1)} %bitcast.24), custom_call_target="tpu_custom_call" | custom-call | flops 1019215872 | bytes 2496512 | tf_op jit(solution)/shard_map/pallas_call | solution.py:25
  60.0 0.0 collective-permute-done.11.refs_1_
  60.0 3.3 %collective-permute-done.12.refs_2_ = bf16[272,128]{1,0:T(8,128)(2,1)S(1)} collective-permute-done((bf16[272,128]{1,0:T(8,128)(2,1)S(1)}, bf16[272,128]{1,0:T(8,128)(2,1)S(1)}, u32[]{:S(2)}, u32[]{:S(2)}) %collective-permute-start.12) | collective-permute-done | bytes 69664 | tf_op jit(solution)/shard_map/ppermute | solution.py:353
  63.3 0.0 collective-permute-done.13.refs_3_
  63.3 0.9 %shard_map.84 = f32[27,24,48]{2,1,0:T(8,128)} custom-call(f32[272,128]{1,0:T(8,128)S(1)} %get-tuple-element.35.refs_0_, bf16[272,128]{1,0:T(8,128)(2,1)S(1)} %collective-permute-done.11.refs_1_, bf16[272,128]{1,0:T(8,128)(2,1)S(1)} %collective-permute-done.12.refs_2_, bf16[272,128]{1,0:T(8,128)(2,1)S(1)} %collective-permute-done.13.refs_3_), custom_call_target="tpu_custom_call" | custom-call | bytes 472576 | tf_op jit(solution)/shard_map/pallas_call | solution.py:25
  (3 shorter events, 0.1 us)
Async XLA Ops:
  1.3 0.9 %copy-start.2 = (bf16[1,1,1,192,512]{4,3,2,1,0:T(8,128)(2,1)S(1)}, bf16[1,1,1,192,512]{4,3,2,1,0:T(8,128)(2,1)}, u32[]{:S(2)}) copy-start(bf16[1,1,1,192,512]{4,3,2,1,0:T(8,128)(2,1)} %param.5) | copy-start | bytes 589828
  2.2 0.9 %copy-start.3 = (bf16[1,1,1,192,512]{4,3,2,1,0:T(8,128)(2,1)S(1)}, bf16[1,1,1,192,512]{4,3,2,1,0:T(8,128)(2,1)}, u32[]{:S(2)}) copy-start(bf16[1,1,1,192,512]{4,3,2,1,0:T(8,128)(2,1)} %param.9) | copy-start | bytes 589828
  3.1 0.7 %copy-start.4 = (s32[1,1,1,512]{3,2,1,0:T(1,128)S(1)}, s32[1,1,1,512]{3,2,1,0:T(1,128)}, u32[]{:S(2)}) copy-start(s32[1,1,1,512]{3,2,1,0:T(1,128)} %param.6) | copy-start | bytes 6148
  4.0 7.1 %collective-permute-start = (bf16[208,192]{1,0:T(8,128)(2,1)S(1)}, bf16[208,192]{1,0:T(8,128)(2,1)S(1)}, u32[]{:S(2)}, u32[]{:S(2)}) collective-permute-start(bf16[208,192]{1,0:T(8,128)(2,1)S(1)} %get-tuple-element.22), channel_id=1, source_target_pairs={{0,8},{8,16},{16,24},{1,9},{9,17},{17,25},{2,10},{10,18},{18,26},{... | collective-permute-start | bytes 239624 | tf_op jit(solution)/shard_map/ppermute | solution.py:360
  8.9 6.6 %collective-permute-start.1 = (bf16[208,192]{1,0:T(8,128)(2,1)S(1)}, bf16[208,192]{1,0:T(8,128)(2,1)S(1)}, u32[]{:S(2)}, u32[]{:S(2)}) collective-permute-start(bf16[208,192]{1,0:T(8,128)(2,1)S(1)} %get-tuple-element.23), channel_id=1, source_target_pairs={{8,0},{16,8},{24,16},{9,1},{17,9},{25,17},{10,2},{18,10},{26,18},{... | collective-permute-start | bytes 239624 | tf_op jit(solution)/shard_map/ppermute | solution.py:360
  15.5 8.1 %collective-permute-start.2 = (bf16[288,192]{1,0:T(8,128)(2,1)S(1)}, bf16[288,192]{1,0:T(8,128)(2,1)S(1)}, u32[]{:S(2)}, u32[]{:S(2)}) collective-permute-start(bf16[288,192]{1,0:T(8,128)(2,1)S(1)} %get-tuple-element.24), channel_id=1, source_target_pairs={{0,1},{1,2},{2,3},{3,4},{4,5},{5,6},{6,7},{8,9},{9,10},{10,11},{11... | collective-permute-start | bytes 331784 | tf_op jit(solution)/shard_map/ppermute | solution.py:360
  16.8 6.8 %collective-permute-start.3 = (bf16[288,192]{1,0:T(8,128)(2,1)S(1)}, bf16[288,192]{1,0:T(8,128)(2,1)S(1)}, u32[]{:S(2)}, u32[]{:S(2)}) collective-permute-start(bf16[288,192]{1,0:T(8,128)(2,1)S(1)} %get-tuple-element.25), channel_id=1, source_target_pairs={{1,0},{2,1},{3,2},{4,3},{5,4},{6,5},{7,6},{9,8},{10,9},{11,10},{12... | collective-permute-start | bytes 331784 | tf_op jit(solution)/shard_map/ppermute | solution.py:360
  18.1 1.8 %copy-start = (bf16[192,27,192]{2,0,1:T(8,128)(2,1)S(1)}, bf16[192,27,192]{2,0,1:T(8,128)(2,1)}, u32[]{:S(2)}) copy-start(bf16[192,27,192]{2,0,1:T(8,128)(2,1)} %param.8) | copy-start | bytes 5971972
  19.9 7.9 %copy-start.5 = (s32[1,1,1,512]{3,2,1,0:T(1,128)S(1)}, s32[1,1,1,512]{3,2,1,0:T(1,128)}, u32[]{:S(2)}) copy-start(s32[1,1,1,512]{3,2,1,0:T(1,128)} %param.6) | copy-start | bytes 6148
  23.8 20.9 %collective-permute-start.4 = (bf16[1200,128]{1,0:T(8,128)(2,1)S(1)}, bf16[1200,128]{1,0:T(8,128)(2,1)S(1)}, u32[]{:S(2)}, u32[]{:S(2)}) collective-permute-start(bf16[1200,128]{1,0:T(8,128)(2,1)S(1)} %get-tuple-element.31.refs_0_), channel_id=1, source_target_pairs={{0,8},{8,0},{16,24},{24,16},{1,9},{9,1},{17,25},{25,17},{2,10},{10... | collective-permute-start | bytes 921608 | tf_op jit(solution)/shard_map/ppermute | solution.py:353
  26.3 18.5 %collective-permute-start.5 = (bf16[1200,128]{1,0:T(8,128)(2,1)S(1)}, bf16[1200,128]{1,0:T(8,128)(2,1)S(1)}, u32[]{:S(2)}, u32[]{:S(2)}) collective-permute-start(bf16[1200,128]{1,0:T(8,128)(2,1)S(1)} %get-tuple-element.31.refs_0_), channel_id=1, source_target_pairs={{0,16},{8,24},{16,0},{24,8},{1,17},{9,25},{17,1},{25,9},{2,18},{10... | collective-permute-start | bytes 921608 | tf_op jit(solution)/shard_map/ppermute | solution.py:353
  26.3 18.5 %collective-permute-start.6 = (bf16[1200,128]{1,0:T(8,128)(2,1)S(1)}, bf16[1200,128]{1,0:T(8,128)(2,1)S(1)}, u32[]{:S(2)}, u32[]{:S(2)}) collective-permute-start(bf16[1200,128]{1,0:T(8,128)(2,1)S(1)} %get-tuple-element.31.refs_0_), channel_id=1, source_target_pairs={{0,24},{8,16},{16,8},{24,0},{1,25},{9,17},{17,9},{25,1},{2,26},{10... | collective-permute-start | bytes 921608 | tf_op jit(solution)/shard_map/ppermute | solution.py:353
  32.4 24.8 %copy-start.1 = (bf16[192,27,192]{2,0,1:T(8,128)(2,1)S(1)}, bf16[192,27,192]{2,0,1:T(8,128)(2,1)}, u32[]{:S(2)}) copy-start(bf16[192,27,192]{2,0,1:T(8,128)(2,1)} %param.8) | copy-start | bytes 5971972
  32.4 7.3 %collective-permute-start.7 = (bf16[48,512]{1,0:T(8,128)(2,1)S(1)}, bf16[48,512]{1,0:T(8,128)(2,1)S(1)}, u32[]{:S(2)}, u32[]{:S(2)}) collective-permute-start(bf16[48,512]{1,0:T(8,128)(2,1)S(1)} %get-tuple-element.42), channel_id=1, source_target_pairs={{0,8},{8,0},{16,24},{24,16},{1,9},{9,1},{17,25},{25,17},{2,10},{10... | collective-permute-start | bytes 147464 | tf_op jit(solution)/shard_map/ppermute | solution.py:353
  34.4 8.3 %collective-permute-start.8 = (bf16[48,512]{1,0:T(8,128)(2,1)S(1)}, bf16[48,512]{1,0:T(8,128)(2,1)S(1)}, u32[]{:S(2)}, u32[]{:S(2)}) collective-permute-start(bf16[48,512]{1,0:T(8,128)(2,1)S(1)} %get-tuple-element.41), channel_id=1, source_target_pairs={{0,16},{8,24},{16,0},{24,8},{1,17},{9,25},{17,1},{25,9},{2,18},{10... | collective-permute-start | bytes 147464 | tf_op jit(solution)/shard_map/ppermute | solution.py:353
  39.8 5.0 %collective-permute-start.9 = (bf16[48,512]{1,0:T(8,128)(2,1)S(1)}, bf16[48,512]{1,0:T(8,128)(2,1)S(1)}, u32[]{:S(2)}, u32[]{:S(2)}) collective-permute-start(bf16[48,512]{1,0:T(8,128)(2,1)S(1)} %get-tuple-element.40), channel_id=1, source_target_pairs={{0,24},{8,16},{16,8},{24,0},{1,25},{9,17},{17,9},{25,1},{2,26},{10... | collective-permute-start | bytes 147464 | tf_op jit(solution)/shard_map/ppermute | solution.py:353
  46.9 2.5 %collective-permute-start.10 = (bf16[4,272,128]{2,1,0:T(8,128)(2,1)S(1)}, bf16[4,272,128]{2,1,0:T(8,128)(2,1)S(1)}, u32[]{:S(2)}, u32[]{:S(2)}) collective-permute-start(bf16[4,272,128]{2,1,0:T(8,128)(2,1)S(1)} %get-tuple-element.34), channel_id=1, source_target_pairs={{0,1},{1,0},{2,3},{3,2},{4,5},{5,4},{6,7},{7,6},{8,9},{9,8},{10,11... | collective-permute-start | bytes 835592 | tf_op jit(solution)/shard_map/ppermute | solution.py:353
  49.5 10.5 %collective-permute-start.11 = (bf16[272,128]{1,0:T(8,128)(2,1)S(1)}, bf16[272,128]{1,0:T(8,128)(2,1)S(1)}, u32[]{:S(2)}, u32[]{:S(2)}) collective-permute-start(bf16[272,128]{1,0:T(8,128)(2,1)S(1)} %get-tuple-element.39), channel_id=1, source_target_pairs={{0,2},{1,3},{2,0},{3,1},{4,6},{5,7},{6,4},{7,5},{8,10},{9,11},{10,... | collective-permute-start | bytes 208904 | tf_op jit(solution)/shard_map/ppermute | solution.py:353
  54.8 8.5 %collective-permute-start.12 = (bf16[272,128]{1,0:T(8,128)(2,1)S(1)}, bf16[272,128]{1,0:T(8,128)(2,1)S(1)}, u32[]{:S(2)}, u32[]{:S(2)}) collective-permute-start(bf16[272,128]{1,0:T(8,128)(2,1)S(1)} %get-tuple-element.38), channel_id=1, source_target_pairs={{0,4},{1,5},{2,6},{3,7},{4,0},{5,1},{6,2},{7,3},{8,12},{9,13},{10,... | collective-permute-start | bytes 208904 | tf_op jit(solution)/shard_map/ppermute | solution.py:353
  56.2 7.1 %collective-permute-start.13 = (bf16[272,128]{1,0:T(8,128)(2,1)S(1)}, bf16[272,128]{1,0:T(8,128)(2,1)S(1)}, u32[]{:S(2)}, u32[]{:S(2)}) collective-permute-start(bf16[272,128]{1,0:T(8,128)(2,1)S(1)} %get-tuple-element.37), channel_id=1, source_target_pairs={{0,6},{1,7},{2,4},{3,5},{4,2},{5,3},{6,0},{7,1},{8,14},{9,15},{10,... | collective-permute-start | bytes 208904 | tf_op jit(solution)/shard_map/ppermute | solution.py:353

commit v2 on v1

v2 whole, which is shorter than its diff:
```python
import functools

import jax
import jax.numpy as jnp
from jax import lax
from jax.experimental import pallas as pl
from jax.experimental.pallas import tpu as pltpu
from jax.sharding import PartitionSpec as P

BE = 8
PLANE = BE * BE
VOX = BE * PLANE
BF = jnp.bfloat16
F32 = jnp.float32
NT = (((1,), (1,)), ((), ()))


def call(body, outs, ins, scratch=(), flops=0, smem=()):
    specs = [
        pl.BlockSpec(memory_space=pltpu.SMEM if k in smem else pltpu.VMEM)
        for k in range(len(ins))
    ]
    moved = sum(a.size * a.dtype.itemsize for a in ins)
    moved += sum(a.size * a.dtype.itemsize for a in outs)
    return pl.pallas_call(
        body,
        out_shape=tuple(outs),
        in_specs=specs,
        out_specs=tuple(pl.BlockSpec(memory_space=pltpu.VMEM) for _ in outs),
        scratch_shapes=list(scratch),
        compiler_params=pltpu.CompilerParams(vmem_limit_bytes=48 * 1024 * 1024),
        cost_estimate=pl.CostEstimate(flops=flops, bytes_accessed=moved, transcendentals=0),
    )(*ins)


def shape(dims, dtype):
    return jax.ShapeDtypeStruct(dims, dtype)


X_DATA = 3 * PLANE
Y_XM, Y_COT = 12 * 16, 10 * BE
Y_DATA = Y_XM + Y_COT


def packed_rows(rows, channels):
    half = -(-rows // 32) * 16 if channels % 128 == 64 else 0
    return rows + 16 + half, half


def message(rows, channels):
    if channels % 128 == 64:
        return shape((packed_rows(rows, channels)[0], channels - 64), BF)
    return shape((rows + 16, channels), BF)


def pack(out_ref, data, flag):
    rows, channels = data.shape
    _, half = packed_rows(rows, channels)
    cut = out_ref.shape[1]
    out_ref[0:rows] = data[:, :cut]
    out_ref[rows : rows + 16] = jnp.full((16, cut), flag, jnp.int32).astype(F32).astype(BF)
    if half:
        second = data[half:, cut:]
        if rows < 2 * half:
            second = jnp.concatenate([second, jnp.zeros((2 * half - rows, 64), BF)], axis=0)
        out_ref[rows + 16 :] = jnp.concatenate([data[0:half, cut:], second], axis=1)


def sides(even, odd, axis):
    place = lax.axis_index(axis) & 1
    even, odd = even[...], odd[...]
    return jnp.where(place == 1, even, odd), jnp.where(place == 1, odd, even)


def unpack(came, rows, channels):
    _, half = packed_rows(rows, channels)
    data, flag = came[0:rows], came[rows : rows + 1]
    if half:
        tail = came[rows + 16 :]
        tail = jnp.concatenate([tail[:, :64], tail[: rows - half, 64:]], axis=0)
        data = jnp.concatenate([data, tail], axis=1)
        flag = jnp.concatenate([flag, flag[:, :64]], axis=1)
    return data, flag.reshape(1, 1, channels)


def spot(pos_ref):
    pos = pos_ref[0]
    return pos >> 1, pos & 1


def prep_body(pos_ref, feat_ref, occ_ref, cot_ref, xm_ref, cm_ref, rows_ref, even_ref, odd_ref):
    px, py = spot(pos_ref)
    live = occ_ref[...].astype(F32)
    channels = feat_ref.shape[0]
    rows = feat_ref[...].astype(F32) * live
    rows_ref[...] = rows.astype(BF)
    xm = rows.T.astype(BF)
    cm = (cot_ref[...].astype(F32) * live).T.astype(BF)
    xm_ref[...] = xm
    cm_ref[...] = cm
    up = jnp.concatenate([xm[VOX - 2 * PLANE :], cm[VOX - PLANE :]], axis=0)
    down = jnp.concatenate([xm[: 2 * PLANE], cm[:PLANE]], axis=0)
    odd = lax.axis_index("gx") & 1
    for pair, out in ((0, even_ref), (1, odd_ref)):
        rises = odd == pair
        data = jnp.where(rises, up, down)
        touches = jnp.where(rises, px, 1 - px)
        data = data * jnp.full((1, channels), touches, jnp.int32).astype(F32).astype(BF)
        pack(out, data, py)


def x_planes(came, valid):
    channels = valid.shape[2]
    data, flag = unpack(came, X_DATA, channels)
    xm = data[0 : 2 * PLANE].reshape(2, PLANE, channels) * valid
    cot = data[2 * PLANE :].astype(F32).reshape(1, PLANE, channels) * valid.astype(F32)
    return xm, cot, (1 - flag, flag)


def scalar_rows(value, channels):
    return jnp.full((1, 1, channels), value, jnp.int32).astype(F32).astype(BF)


def strips_body(pos_ref, xm_ref, cm_ref, xeven_ref, xodd_ref, near_ref, even_ref, odd_ref):
    px, py = spot(pos_ref)
    channels = xm_ref.shape[1]
    one = scalar_rows(1, channels)
    own_at = (scalar_rows(1 - py, channels), scalar_rows(py, channels))
    xlow, xhigh = sides(xeven_ref, xodd_ref, "gx")
    xl, cl, at_l = x_planes(xlow, one)
    xh, ch, at_h = x_planes(xhigh, one)
    own = xm_ref[...].reshape(BE, PLANE, channels)
    cot = cm_ref[...].astype(F32).reshape(BE, PLANE, channels)
    strips = []
    for side in (0, 1):
        rows = slice(PLANE - 16, PLANE) if side else slice(0, 16)
        line = slice(PLANE - BE, PLANE) if side else slice(0, BE)
        lines = jnp.concatenate(
            [
                cl[:, line] * at_l[side].astype(F32),
                cot[:, line] * own_at[side].astype(F32),
                ch[:, line] * at_h[side].astype(F32),
            ],
            axis=0,
        )
        strip = [xl[:, rows] * at_l[side], own[:, rows] * own_at[side], xh[:, rows] * at_h[side]]
        strip = jnp.concatenate(strip, axis=0).reshape(Y_XM, channels)
        strips.append(jnp.concatenate([strip, lines.reshape(Y_COT, channels).astype(BF)], axis=0))
    place = lax.axis_index("gy") & 1
    pack(even_ref, jnp.where(place == 0, strips[1], strips[0]), px)
    pack(odd_ref, jnp.where(place == 1, strips[1], strips[0]), px)


def y_rows(came, px, channels):
    data, flag = unpack(came, Y_DATA, channels)
    strip = data[0:Y_XM].reshape(12, 16, channels)
    lines = data[Y_XM:].astype(F32).reshape(10, BE, channels)
    zero_at, one_at = 1 - flag, flag
    here_high = scalar_rows(px, channels)
    here_low = 1 - here_high
    same = zero_at * here_low + one_at * here_high
    xm = jnp.concatenate(
        [
            strip[0:2] * here_low + strip[8:10] * (zero_at * here_high),
            strip[2:10] * same,
            strip[10:12] * here_high + strip[2:4] * (one_at * here_low),
        ],
        axis=0,
    )
    f = lambda v: v.astype(F32)
    cot = jnp.concatenate(
        [
            lines[0:1] * f(here_low) + lines[8:9] * f(zero_at * here_high),
            lines[1:9] * f(same),
            lines[9:10] * f(here_high) + lines[1:2] * f(one_at * here_low),
        ],
        axis=0,
    )
    return xm, cot


def window_body(pos_ref, xm_ref, cm_ref, xeven_ref, xodd_ref, yeven_ref, yodd_ref, even_ref, odd_ref, cot_ref):
    px, py = spot(pos_ref)
    channels = xm_ref.shape[1]
    f = lambda v: v.astype(F32)
    high_x, high_y = scalar_rows(px, channels), scalar_rows(py, channels)
    low_x, low_y = 1 - high_x, 1 - high_y
    xlow, xhigh = sides(xeven_ref, xodd_ref, "gx")
    xl, cl, at_l = x_planes(xlow, low_x)
    xh, ch, at_h = x_planes(xhigh, high_x)
    ylow, yhigh = sides(yeven_ref, yodd_ref, "gy")
    sl, tl = y_rows(ylow, px, channels)
    sh, th = y_rows(yhigh, px, channels)
    own = xm_ref[...].reshape(BE, PLANE, channels)
    cot = cm_ref[...].astype(F32).reshape(BE, PLANE, channels)
    same_l = at_l[0] * low_y + at_l[1] * high_y
    same_h = at_h[0] * low_y + at_h[1] * high_y
    none8 = jnp.zeros((BE, 16, channels), BF)
    own_low = jnp.concatenate([xl[:, 48:64] * at_l[0], none8, xh[:, 48:64] * at_h[0]], axis=0)
    own_high = jnp.concatenate([xl[:, 0:16] * at_l[1], none8, xh[:, 0:16] * at_h[1]], axis=0)
    below = sl * low_y + own_low * high_y
    above = sh * high_y + own_high * low_y
    mid = jnp.concatenate([xl * same_l, own, xh * same_h], axis=0)
    even_ref[:, 0:16] = below
    even_ref[:, 16:80] = mid
    even_ref[:, 80:96] = above
    odd_ref[...] = jnp.concatenate([f(below)[:, 8:16], f(mid), f(above)[:, 0:8]], axis=1).astype(BF)
    none8 = jnp.zeros((BE, BE, channels), F32)
    cot_low = jnp.concatenate([cl[:, 56:64] * f(at_l[0]), none8, ch[:, 56:64] * f(at_h[0])], axis=0)
    cot_high = jnp.concatenate([cl[:, 0:8] * f(at_l[1]), none8, ch[:, 0:8] * f(at_h[1])], axis=0)
    cot_below = tl * f(low_y) + cot_low * f(high_y)
    cot_above = th * f(high_y) + cot_high * f(low_y)
    cot_mid = jnp.concatenate([cl * f(same_l), cot, ch * f(same_h)], axis=0)
    cot_ref[...] = jnp.concatenate([cot_below, cot_mid, cot_above], axis=1).astype(BF)


WIDE = 896


def z_shift(values, by):
    moved = pltpu.roll(values, by % BE, 1)
    place = lax.broadcasted_iota(jnp.int32, values.shape, 1)
    keep = place >= by if by > 0 else place < BE + by
    return jnp.where(keep, moved, 0.0)


def touch_body(w_ref, out_ref):
    out_ref[...] = w_ref[0, 0:16, 0:128]


def forward_body(parts, even_ref, odd_ref, cot_ref, w_ref, act_ref, slope_ref, rows_ref, wide_ref):
    channels = even_ref.shape[2]
    me = lax.axis_index("gx")
    slots = 5

    def taken(first, a, b):
        some = slice(a + first, a + first + slots)
        piece = odd_ref[some] if b == 1 else even_ref[some, 8 * b : 8 * b + 80]
        return piece.reshape(80 * slots, channels)

    for first in range(0, 10, slots):
        columns = [taken(first, a, b) for a in range(3) for b in range(3)]
        columns = jnp.concatenate(columns, axis=1)
        pre = None
        for c in range(3):
            taps = jnp.concatenate([w_ref[3 * ab + c] for ab in range(9)], axis=1)
            total = lax.dot_general(columns, taps, NT, preferred_element_type=F32)
            total = total.reshape(10 * slots, BE, channels)
            if c != 1:
                total = z_shift(total, 1 - c)
            pre = total if pre is None else pre + total
        sigma = 1.0 / (1.0 + jnp.exp(-pre))
        cot = cot_ref[first : first + slots].astype(F32).reshape(10 * slots, BE, channels)
        slope = cot * (sigma * (1.0 + pre * (1.0 - sigma)))
        slope_ref[first : first + slots] = slope.reshape(slots, 80, channels).astype(BF)
        wide_ref[first : first + slots] = (pre * sigma).reshape(slots, 80, channels)
    act_ref[...] = wide_ref[1:9, 8:72].reshape(VOX, channels).astype(BF)
    block = channels // parts
    row = lax.broadcasted_iota(jnp.int32, (channels, channels), 0)
    col = lax.broadcasted_iota(jnp.int32, (channels, channels), 1)
    wanted = jnp.zeros_like(row)
    for k in range(parts):
        start = block * lax.bitwise_xor(me, jnp.int32(k))
        wanted = jnp.where(row >= block * k, row - block * k + start, wanted)
    pick = (col == wanted).astype(F32).astype(BF)
    slope = slope_ref[...].reshape(800, channels)
    lines = lax.dot_general(pick, slope, NT, preferred_element_type=F32).astype(BF)
    for k in range(parts):
        rows_ref[k, :, 0:800] = lines[block * k : block * (k + 1)]
        rows_ref[k, :, 800:] = jnp.zeros((block, WIDE - 800), BF)


def backward_body(slope_ref, act_ref, occ_ref, w_ref, out_ref, grad_ref):
    channels = slope_ref.shape[2]
    live = occ_ref[...].astype(F32)
    out_ref[...] = (act_ref[...].astype(F32).T * live).astype(BF)
    slope = slope_ref[...]
    middle = slope.astype(F32)[:, 8:72].astype(BF)
    columns = []
    for a in range(3):
        for b in range(3):
            if b == 1:
                piece = middle[2 - a : 10 - a]
            else:
                piece = slope[2 - a : 10 - a, 8 * (2 - b) : 8 * (2 - b) + 64]
            columns.append(piece.reshape(VOX, channels))
    columns = jnp.concatenate(columns, axis=1)
    grad = None
    for c in range(3):
        taps = jnp.concatenate([w_ref[3 * ab + c] for ab in range(9)], axis=0)
        total = jnp.dot(columns, taps, preferred_element_type=F32)
        total = total.reshape(PLANE, BE, channels)
        if c != 1:
            total = z_shift(total, c - 1)
        grad = total if grad is None else grad + total
    grad_ref[...] = (grad.reshape(VOX, channels).T * live).astype(BF)


def packing(width):
    full = width // 128
    rest = width - 128 * full
    per = 128 // rest if rest else 0
    return full, rest, per, 9 * full + (-(-9 // per) if rest else 0)


def lines_of(slots, rows):
    return -(-slots * rows // 16) * 16


def kernel_grad_body(parts, chips, *refs):
    bricks, lines = refs[:parts], refs[parts]
    others = refs[parts + 1 : 2 * parts]
    outs = refs[2 * parts :]
    channels = bricks[0].shape[0]
    block = channels // parts
    width = 3 * block
    place = lax.broadcasted_iota(jnp.int32, (block, WIDE), 1) & (BE - 1)
    windows = []
    for k in range(parts):
        g = (lines[0] if k == 0 else others[k - 1][...]).astype(F32)
        back = jnp.where(place < BE - 1, pltpu.roll(g, WIDE - 1, 1), 0.0)
        ahead = jnp.where(place > 0, pltpu.roll(g, 1, 1), 0.0)
        columns = jnp.concatenate([back, g, ahead], axis=0).T[0:800].reshape(10, 80, width)
        windows.append((columns.astype(BF), columns[:, 8:72].astype(BF)))
    left = jnp.concatenate([brick[...] for brick in bricks], axis=1)
    full, rest, per, slots = packing(width)
    leftover = []
    store = outs[-1]
    for a in range(3):
        for b in range(3):
            right = []
            for window, middle in windows:
                if b == 1:
                    piece = middle[2 - a : 10 - a]
                else:
                    piece = window[2 - a : 10 - a, 8 * (2 - b) : 8 * (2 - b) + 64]
                right.append(piece.reshape(VOX, width))
            total = jnp.dot(left, jnp.concatenate(right, axis=0), preferred_element_type=F32)
            for n in range(full):
                store[(3 * a + b) * full + n] = total[:, 128 * n : 128 * n + 128]
            if rest:
                leftover.append(total[:, 128 * full :])
    if rest:
        for n in range(slots - 9 * full):
            some = leftover[n * per : (n + 1) * per]
            spare = 128 - rest * len(some)
            if spare:
                some = some + [jnp.zeros((channels, spare), F32)]
            store[9 * full + n] = jnp.concatenate(some, axis=1)
    if len(outs) == 1:
        return
    send_ref, keep_ref, _ = outs
    rows = channels // (2 * chips)
    count = lines_of(slots, rows)
    core = lax.axis_index("gy") & 1
    pad = [jnp.zeros((count - slots * rows, 128), F32)] if count > slots * rows else []
    for chip in range(chips):
        for whose, out in ((1 - core, send_ref), (core, keep_ref)):
            start = pl.multiple_of(rows * (2 * chip + whose), 8)
            piece = store[:, pl.ds(start, rows), :].reshape(slots * rows, 128)
            out[chip] = jnp.concatenate([piece] + pad, axis=0).astype(out.dtype)


def pair_body(chips, keep_ref, recv_ref, own_ref, send_ref):
    me = lax.axis_index("gy") >> 1
    own_ref[...] = keep_ref[me] + recv_ref[me].astype(F32)
    for k in range(1, chips):
        it = lax.bitwise_xor(me, jnp.int32(k))
        send_ref[k - 1] = (keep_ref[it] + recv_ref[it].astype(F32)).astype(BF)


def last_body(slots, width, scale, *refs):
    out_ref = refs[-1]
    total = refs[0][...]
    for other in refs[1:-1]:
        total = total + other[...].astype(F32)
    total = total * scale
    rows, block = out_ref.shape[1], width // 3
    full, rest, per, _ = packing(width)
    for ab in range(9):
        parts = [total[rows * (ab * full + n) : rows * (ab * full + n + 1)] for n in range(full)]
        if rest:
            at = rows * (9 * full + ab // per)
            lane = rest * (ab % per)
            parts.append(total[at : at + rows, lane : lane + rest])
        line = parts[0] if len(parts) == 1 else jnp.concatenate(parts, axis=1)
        for c in range(3):
            out_ref[3 * ab + c] = line[:, block * c : block * (c + 1)]


def xor_step(value, axis, step):
    count = lax.axis_size(axis)
    return lax.ppermute(value, axis, [(i, i ^ step) for i in range(count)])


def swap_pairs(even, odd, axis):
    count = lax.axis_size(axis)
    later = [(i, i + 1) for i in range(1, count - 1, 2)]
    odd = lax.ppermute(odd, axis, later + [(j, i) for i, j in later])
    return xor_step(even, axis, 1), odd


def shards(features, occupancy, brick_pos, weight, cotangent):
    channels = features.shape[3]
    parts, line = lax.axis_size("gx"), lax.axis_size("gy")
    chips = line // 2
    block, rows = channels // parts, channels // line
    feat = features.reshape(channels, VOX)
    cot = cotangent.reshape(channels, VOX)
    occ = occupancy.reshape(1, VOX)
    pos = brick_pos.reshape(1)
    taps = weight.transpose(1, 0, 2)

    brick, plain = shape((VOX, channels), BF), shape((channels, VOX), BF)
    face, strip = message(X_DATA, channels), message(Y_DATA, channels)
    xm, cm, masked, even, odd = call(
        prep_body,
        [brick, brick, plain, face, face],
        [pos, feat, occ, cot],
        smem=(0,),
    )
    xeven, xodd = swap_pairs(even, odd, "gx")
    bricks = {k: xor_step(masked, "gx", k) for k in reversed(range(1, parts))}
    bricks = [masked] + [bricks[k] for k in range(1, parts)]
    (near,) = call(touch_body, [shape((16, 128), BF)], [taps])
    even, odd = call(strips_body, [strip, strip], [pos, xm, cm, xeven, xodd, near], smem=(0,))
    yeven, yodd = swap_pairs(even, odd, "gy")
    even, odd, wide_cot = call(
        window_body,
        [shape((12, 96, channels), BF), shape((12, 80, channels), BF), shape((10, 80, channels), BF)],
        [pos, xm, cm, xeven, xodd, yeven, yodd],
        smem=(0,),
    )
    flops = 2 * VOX * 27 * channels * channels
    act, slope, lines = call(
        functools.partial(forward_body, parts),
        [brick, shape((10, 80, channels), BF), shape((parts, block, WIDE), BF)],
        [even, odd, wide_cot, taps],
        scratch=[pltpu.VMEM((10, 80, channels), F32)],
        flops=flops * 3 // 2,
    )
    others = {k: xor_step(lines[k], "gx", k) for k in reversed(range(1, parts))}
    others = [others[k] for k in range(1, parts)]
    output, x_grad = call(backward_body, [plain, plain], [slope, act, occ, taps], flops=flops)

    width = 3 * block
    slots = packing(width)[3]
    count = lines_of(slots, rows)
    body = functools.partial(kernel_grad_body, parts, chips)
    table = (slots, channels, 128)
    if rows % 8 == 0:
        send, keep = call(
            body,
            [shape((chips, count, 128), BF), shape((chips, count, 128), F32)],
            bricks + [lines] + others,
            scratch=[pltpu.VMEM(table, F32)],
            flops=flops,
        )
    else:
        (store,) = call(body, [shape(table, F32)], bricks + [lines] + others, flops=flops)
        store = store.reshape(slots, chips, 2, rows, 128).transpose(2, 1, 0, 3, 4)
        store = store.reshape(2, chips, slots * rows, 128)
        store = jnp.pad(store, ((0, 0), (0, 0), (0, count - slots * rows), (0, 0)))
        core = lax.axis_index("gy") & 1
        keep = lax.dynamic_index_in_dim(store, core, 0, False)
        send = lax.dynamic_index_in_dim(store, 1 - core, 0, False).astype(BF)
    recv = xor_step(send, "gy", 1)
    own, sends = call(
        functools.partial(pair_body, chips),
        [shape((count, 128), F32), shape((chips - 1, count, 128), BF)],
        [keep, recv],
    )
    came = [xor_step(sends[k - 1], "gy", 2 * k) for k in reversed(range(1, chips))]
    (w_grad,) = call(
        functools.partial(last_body, slots, width, 1.0 / (parts * line)),
        [shape((27, rows, block), F32)],
        [own] + came,
    )
    return (
        output.reshape(features.shape),
        x_grad.reshape(features.shape),
        w_grad.transpose(2, 0, 1),
    )


def solution(mesh):
    placed = (
        P("gx", "gy", None, None, None),
        P("gx", "gy", None, None),
        P("gx", "gy", None),
        P(),
        P("gx", "gy", None, None, None),
    )
    return jax.shard_map(
        shards,
        mesh=mesh,
        in_specs=placed,
        out_specs=(
            P("gx", "gy", None, None, None),
            P("gx", "gy", None, None, None),
            P("gx", None, "gy"),
        ),
        check_vma=False,
    )
```

time: 64.6 us -> 47.8 us (0.74)
  waiting for transfers between devices: 19.5 us -> 9.5 us
  Pallas kernels: 14.6 us -> 9.75 us
  starting transfers between devices: 24.4 us -> 22.5 us
    ppermute x4 -> x2, starting transfers between devices: 8.73 us -> 1.45 us  [swap_pairs(): odd = lax.ppermute(odd, axis, later + [(j, i) for i, j in later])]
    ppermute x10 -> x12, starting transfers between devices: 15.7 us -> 21.1 us  [xor_step(): return lax.ppermute(value, axis, [(i, i ^ step) for i in range(count)])]
    ppermute x4 -> x2, waiting for transfers between devices: 5.3 us -> 0.01 us  [swap_pairs(): odd = lax.ppermute(odd, axis, later + [(j, i) for i, j in later])]
    pallas_call x9, Pallas kernels: 14.6 us -> 9.75 us  [call(): pl.pallas_call(body, out_shape=tuple(outs), in_specs=specs, out_specs=tup...]
    ppermute x10 -> x12, waiting for transfers between devices: 14.2 us -> 9.5 us  [xor_step(): return lax.ppermute(value, axis, [(i, i ^ step) for i in range(count)])]
  transfers between devices with their start and end apart: 14 -> 14, of which waited for: 7 -> 5; matrix products, arithmetic and copies ran while one was open for 0% -> 0% of each run, Pallas kernels for 17% -> 12%
where the time goes in v2:
time: 47.8 us; the launch traced here: 47.5 us
  starting transfers between devices  22.5 us (47%)
  Pallas kernels  9.75 us (20%)
  waiting for transfers between devices  9.5 us (20%)
  local copies, waits for them, and re-layouts  4.32 us (9%)
  between operations  1.4 us (3%)
    ppermute x12, starting transfers between devices, xor_step(): return lax.ppermute(value, axis, [(i, i ^ step) for i in range(count)])  21.1 us
    pallas_call x9, Pallas kernels, call(): pl.pallas_call(body, out_shape=tuple(outs), in_specs=specs, out_specs=tup...  9.75 us
    ppermute x12, waiting for transfers between devices, xor_step(): return lax.ppermute(value, axis, [(i, i ^ step) for i in range(count)])  9.5 us
    unnamed x12, local copies, waits for them, and re-layouts  4.28 us
    ppermute x2, starting transfers between devices, swap_pairs(): odd = lax.ppermute(odd, axis, later + [(j, i) for i, j in later])  1.45 us
  transfers between devices with their start and end apart: 14, of which 5 were waited for; matrix products, arithmetic and copies ran while one was open for 0% of the time, Pallas kernels for 12%

profile of v2, /device:TPU:0, one launch (start us, length us, event | category | flops | bytes accessed | tf_op | source)
XLA Modules:
  0.0 47.5 jit_solution(6461340998971927930)
XLA Ops:
  1.3 0.0 copy-start.2
  1.3 0.9 %copy-done.2 = bf16[1,1,1,192,512]{4,3,2,1,0:T(8,128)(2,1)S(1)} copy-done((bf16[1,1,1,192,512]{4,3,2,1,0:T(8,128)(2,1)S(1)}, bf16[1,1,1,192,512]{4,3,2,1,0:T(8,128)(2,1)}, u32[]{:S(2)}) %copy-start.2) | copy-done | bytes 196632
  2.2 0.0 copy-start.3
  2.2 0.9 %copy-done.3 = bf16[1,1,1,192,512]{4,3,2,1,0:T(8,128)(2,1)S(1)} copy-done((bf16[1,1,1,192,512]{4,3,2,1,0:T(8,128)(2,1)S(1)}, bf16[1,1,1,192,512]{4,3,2,1,0:T(8,128)(2,1)}, u32[]{:S(2)}) %copy-start.3) | copy-done | bytes 196632
  3.1 0.0 copy-start.4
  3.1 0.7 %copy-done.4 = s32[1,1,1,512]{3,2,1,0:T(1,128)S(1)} copy-done((s32[1,1,1,512]{3,2,1,0:T(1,128)S(1)}, s32[1,1,1,512]{3,2,1,0:T(1,128)}, u32[]{:S(2)}) %copy-start.4) | copy-done | bytes 2072
  3.8 0.3 shard_map.76
  4.1 3.0 %collective-permute-start = (bf16[304,128]{1,0:T(8,128)(2,1)S(1)}, bf16[304,128]{1,0:T(8,128)(2,1)S(1)}, u32[]{:S(2)}, u32[]{:S(2)}) collective-permute-start(bf16[304,128]{1,0:T(8,128)(2,1)S(1)} %get-tuple-element.24), channel_id=1, source_target_pairs={{0,8},{8,0},{16,24},{24,16},{1,9},{9,1},{17,25},{25,17},{2,10},{10... | collective-permute-start | bytes 233480 | tf_op jit(solution)/shard_map/ppermute | solution.py:393
  7.1 0.7 %collective-permute-start.1 = (bf16[304,128]{1,0:T(8,128)(2,1)S(1)}, bf16[304,128]{1,0:T(8,128)(2,1)S(1)}, u32[]{:S(2)}, u32[]{:S(2)}) collective-permute-start(bf16[304,128]{1,0:T(8,128)(2,1)S(1)} %get-tuple-element.25), channel_id=1, source_target_pairs={{8,16},{16,8},{9,17},{17,9},{10,18},{18,10},{11,19},{19,11},{12,20... | collective-permute-start | bytes 233480 | tf_op jit(solution)/shard_map/ppermute | solution.py:399
  7.8 0.0 copy-start
  7.8 1.7 %copy-done = bf16[192,27,192]{2,0,1:T(8,128)(2,1)S(1)} copy-done((bf16[192,27,192]{2,0,1:T(8,128)(2,1)S(1)}, bf16[192,27,192]{2,0,1:T(8,128)(2,1)}, u32[]{:S(2)}) %copy-start) | copy-done | bytes 1990680
  9.5 0.0 copy-start.1
  9.5 0.0 collective-permute-done.xeven_ref
  9.5 0.0 collective-permute-done.1.xodd_ref
  9.5 0.2 shard_map.78
  9.7 0.0 collective-permute-start.2
  9.7 0.8 %collective-permute-start.3 = (bf16[432,128]{1,0:T(8,128)(2,1)S(1)}, bf16[432,128]{1,0:T(8,128)(2,1)S(1)}, u32[]{:S(2)}, u32[]{:S(2)}) collective-permute-start(bf16[432,128]{1,0:T(8,128)(2,1)S(1)} %get-tuple-element.27), channel_id=1, source_target_pairs={{1,2},{3,4},{5,6},{2,1},{4,3},{6,5},{9,10},{11,12},{13,14},{10,9},... | collective-permute-start | bytes 331784 | tf_op jit(solution)/shard_map/ppermute | solution.py:399
  10.5 4.7 %collective-permute-start.4 = (bf16[192,512]{1,0:T(8,128)(2,1)S(1)}, bf16[192,512]{1,0:T(8,128)(2,1)S(1)}, u32[]{:S(2)}, u32[]{:S(2)}) collective-permute-start(bf16[192,512]{1,0:T(8,128)(2,1)S(1)} %get-tuple-element.35.refs_0_), channel_id=1, source_target_pairs={{0,8},{8,0},{16,24},{24,16},{1,9},{9,1},{17,25},{25,17},{2,10},{10... | collective-permute-start | bytes 589832 | tf_op jit(solution)/shard_map/ppermute | solution.py:393
  15.3 1.5 %collective-permute-start.5 = (bf16[192,512]{1,0:T(8,128)(2,1)S(1)}, bf16[192,512]{1,0:T(8,128)(2,1)S(1)}, u32[]{:S(2)}, u32[]{:S(2)}) collective-permute-start(bf16[192,512]{1,0:T(8,128)(2,1)S(1)} %get-tuple-element.35.refs_0_), channel_id=1, source_target_pairs={{0,16},{8,24},{16,0},{24,8},{1,17},{9,25},{17,1},{25,9},{2,18},{10... | collective-permute-start | bytes 589832 | tf_op jit(solution)/shard_map/ppermute | solution.py:393
  16.8 1.4 %collective-permute-start.6 = (bf16[192,512]{1,0:T(8,128)(2,1)S(1)}, bf16[192,512]{1,0:T(8,128)(2,1)S(1)}, u32[]{:S(2)}, u32[]{:S(2)}) collective-permute-start(bf16[192,512]{1,0:T(8,128)(2,1)S(1)} %get-tuple-element.35.refs_0_), channel_id=1, source_target_pairs={{0,24},{8,16},{16,8},{24,0},{1,25},{9,17},{17,9},{25,1},{2,26},{10... | collective-permute-start | bytes 589832 | tf_op jit(solution)/shard_map/ppermute | solution.py:393
  18.2 0.0 collective-permute-done.2.yeven_ref
  18.2 0.0 collective-permute-done.3.yodd_ref
  18.2 0.2 shard_map.79
  18.4 0.0 copy-done.1
  18.4 3.0 %shard_map.80 = (bf16[512,192]{1,0:T(8,128)(2,1)S(1)}, bf16[10,80,192]{2,1,0:T(8,128)(2,1)S(1)}, bf16[4,48,896]{2,1,0:T(8,128)(2,1)S(1)}) custom-call(bf16[12,96,192]{2,1,0:T(8,128)(2,1)S(1)} %get-tuple-element.28.even_ref, bf16[12,80,192]{2,1,0:T(8,128)(2,1)S(1)} %get-tuple-element.29.odd_ref, bf16[10,80,192]{2,1,0:T(8,128)(2,1)S(1)} %get-tuple-element.30.cot_ref, ...), custom_call_target="tpu_custom_call" | custom-call | flops 1528823808 | bytes 3956736 | tf_op jit(solution)/shard_map/pallas_call | solution.py:25
  21.4 0.0 copy-start.5
  21.5 0.6 %collective-permute-start.7 = (bf16[48,896]{1,0:T(8,128)(2,1)S(1)}, bf16[48,896]{1,0:T(8,128)(2,1)S(1)}, u32[]{:S(2)}, u32[]{:S(2)}) collective-permute-start(bf16[48,896]{1,0:T(8,128)(2,1)S(1)} %get-tuple-element.43), channel_id=1, source_target_pairs={{0,8},{8,0},{16,24},{24,16},{1,9},{9,1},{17,25},{25,17},{2,10},{10... | collective-permute-start | bytes 258056 | tf_op jit(solution)/shard_map/ppermute | solution.py:393
  22.1 1.5 %collective-permute-start.8 = (bf16[48,896]{1,0:T(8,128)(2,1)S(1)}, bf16[48,896]{1,0:T(8,128)(2,1)S(1)}, u32[]{:S(2)}, u32[]{:S(2)}) collective-permute-start(bf16[48,896]{1,0:T(8,128)(2,1)S(1)} %get-tuple-element.42), channel_id=1, source_target_pairs={{0,16},{8,24},{16,0},{24,8},{1,17},{9,25},{17,1},{25,9},{2,18},{10... | collective-permute-start | bytes 258056 | tf_op jit(solution)/shard_map/ppermute | solution.py:393
  23.6 0.0 collective-permute-done.4.refs_1_
  23.6 1.4 %collective-permute-start.9 = (bf16[48,896]{1,0:T(8,128)(2,1)S(1)}, bf16[48,896]{1,0:T(8,128)(2,1)S(1)}, u32[]{:S(2)}, u32[]{:S(2)}) collective-permute-start(bf16[48,896]{1,0:T(8,128)(2,1)S(1)} %get-tuple-element.41), channel_id=1, source_target_pairs={{0,24},{8,16},{16,8},{24,0},{1,25},{9,17},{17,9},{25,1},{2,26},{10... | collective-permute-start | bytes 258056 | tf_op jit(solution)/shard_map/ppermute | solution.py:393
  25.0 0.0 collective-permute-done.5.refs_2_
  25.0 1.2 %collective-permute-done.6.refs_3_ = bf16[192,512]{1,0:T(8,128)(2,1)S(1)} collective-permute-done((bf16[192,512]{1,0:T(8,128)(2,1)S(1)}, bf16[192,512]{1,0:T(8,128)(2,1)S(1)}, u32[]{:S(2)}, u32[]{:S(2)}) %collective-permute-start.6) | collective-permute-done | bytes 196640 | tf_op jit(solution)/shard_map/ppermute | solution.py:393
  26.2 0.8 %collective-permute-done.7.refs_5_ = bf16[48,896]{1,0:T(8,128)(2,1)S(1)} collective-permute-done((bf16[48,896]{1,0:T(8,128)(2,1)S(1)}, bf16[48,896]{1,0:T(8,128)(2,1)S(1)}, u32[]{:S(2)}, u32[]{:S(2)}) %collective-permute-start.7) | collective-permute-done | bytes 86048 | tf_op jit(solution)/shard_map/ppermute | solution.py:393
  27.0 3.3 %collective-permute-done.8.refs_6_ = bf16[48,896]{1,0:T(8,128)(2,1)S(1)} collective-permute-done((bf16[48,896]{1,0:T(8,128)(2,1)S(1)}, bf16[48,896]{1,0:T(8,128)(2,1)S(1)}, u32[]{:S(2)}, u32[]{:S(2)}) %collective-permute-start.8) | collective-permute-done | bytes 86048 | tf_op jit(solution)/shard_map/ppermute | solution.py:393
  30.3 0.0 collective-permute-done.9.refs_7_
  30.3 2.7 %shard_map.82 = (bf16[4,272,128]{2,1,0:T(8,128)(2,1)S(1)}, f32[4,272,128]{2,1,0:T(8,128)S(1)}) custom-call(bf16[192,512]{1,0:T(8,128)(2,1)S(1)} %get-tuple-element.35.refs_0_, bf16[192,512]{1,0:T(8,128)(2,1)S(1)} %collective-permute-done.4.refs_1_, bf16[192,512]{1,0:T(8,128)(2,1)S(1)} %collective-permute-done.5.refs_2_, ...), custom_call_target="tpu_custom_call" | custom-call | flops 1019215872 | bytes 2224128 | tf_op jit(solution)/shard_map/pallas_call | solution.py:25
  33.0 1.4 %collective-permute-start.10 = (bf16[4,272,128]{2,1,0:T(8,128)(2,1)S(1)}, bf16[4,272,128]{2,1,0:T(8,128)(2,1)S(1)}, u32[]{:S(2)}, u32[]{:S(2)}) collective-permute-start(bf16[4,272,128]{2,1,0:T(8,128)(2,1)S(1)} %get-tuple-element.38), channel_id=1, source_target_pairs={{0,1},{1,0},{2,3},{3,2},{4,5},{5,4},{6,7},{7,6},{8,9},{9,8},{10,11... | collective-permute-start | bytes 835592 | tf_op jit(solution)/shard_map/ppermute | solution.py:393
  34.5 1.2 %collective-permute-done.10.recv_ref = bf16[4,272,128]{2,1,0:T(8,128)(2,1)S(1)} collective-permute-done((bf16[4,272,128]{2,1,0:T(8,128)(2,1)S(1)}, bf16[4,272,128]{2,1,0:T(8,128)(2,1)S(1)}, u32[]{:S(2)}, u32[]{:S(2)}) %collective-permute-start.10) | collective-permute-done | bytes 278560 | tf_op jit(solution)/shard_map/ppermute | solution.py:393
  35.7 0.1 shard_map.83
  35.7 3.7 %collective-permute-start.11 = (bf16[272,128]{1,0:T(8,128)(2,1)S(1)}, bf16[272,128]{1,0:T(8,128)(2,1)S(1)}, u32[]{:S(2)}, u32[]{:S(2)}) collective-permute-start(bf16[272,128]{1,0:T(8,128)(2,1)S(1)} %get-tuple-element.46), channel_id=1, source_target_pairs={{0,6},{1,7},{2,4},{3,5},{4,2},{5,3},{6,0},{7,1},{8,14},{9,15},{10,... | collective-permute-start | bytes 208904 | tf_op jit(solution)/shard_map/ppermute | solution.py:393
  39.5 1.6 %collective-permute-start.12 = (bf16[272,128]{1,0:T(8,128)(2,1)S(1)}, bf16[272,128]{1,0:T(8,128)(2,1)S(1)}, u32[]{:S(2)}, u32[]{:S(2)}) collective-permute-start(bf16[272,128]{1,0:T(8,128)(2,1)S(1)} %get-tuple-element.45), channel_id=1, source_target_pairs={{0,4},{1,5},{2,6},{3,7},{4,0},{5,1},{6,2},{7,3},{8,12},{9,13},{10,... | collective-permute-start | bytes 208904 | tf_op jit(solution)/shard_map/ppermute | solution.py:393
  41.0 0.1 collective-permute-start.13
  41.1 0.0 copy-done.5
  41.1 2.4 %shard_map.81 = (bf16[192,512]{1,0:T(8,128)(2,1)}, bf16[192,512]{1,0:T(8,128)(2,1)}) custom-call(bf16[10,80,192]{2,1,0:T(8,128)(2,1)S(1)} %get-tuple-element.31.slope_ref, bf16[512,192]{1,0:T(8,128)(2,1)S(1)} %get-tuple-element.32.act_ref, s32[1,512]{1,0:T(1,128)S(1)} %bitcast.29, bf16[27,192,192]{2,1,0:T(8,128)(2,1)S(1)} %bitcast.25), custom_call_target="tpu_custom_call" | custom-call | flops 1019215872 | bytes 2889728 | tf_op jit(solution)/shard_map/pallas_call | solution.py:25
  43.5 0.0 collective-permute-done.11.refs_1_
  43.5 3.0 %collective-permute-done.12.refs_2_ = bf16[272,128]{1,0:T(8,128)(2,1)S(1)} collective-permute-done((bf16[272,128]{1,0:T(8,128)(2,1)S(1)}, bf16[272,128]{1,0:T(8,128)(2,1)S(1)}, u32[]{:S(2)}, u32[]{:S(2)}) %collective-permute-start.12) | collective-permute-done | bytes 69664 | tf_op jit(solution)/shard_map/ppermute | solution.py:393
  46.5 0.0 collective-permute-done.13.refs_3_
  46.5 0.9 %shard_map.84 = f32[27,24,48]{2,1,0:T(8,128)} custom-call(f32[272,128]{1,0:T(8,128)S(1)} %get-tuple-element.39.refs_0_, bf16[272,128]{1,0:T(8,128)(2,1)S(1)} %collective-permute-done.11.refs_1_, bf16[272,128]{1,0:T(8,128)(2,1)S(1)} %collective-permute-done.12.refs_2_, bf16[272,128]{1,0:T(8,128)(2,1)S(1)} %collective-permute-done.13.refs_3_), custom_call_target="tpu_custom_call" | custom-call | bytes 472576 | tf_op jit(solution)/shard_map/pallas_call | solution.py:25
  (3 shorter events, 0.0 us)
Async XLA Ops:
  1.3 0.9 %copy-start.2 = (bf16[1,1,1,192,512]{4,3,2,1,0:T(8,128)(2,1)S(1)}, bf16[1,1,1,192,512]{4,3,2,1,0:T(8,128)(2,1)}, u32[]{:S(2)}) copy-start(bf16[1,1,1,192,512]{4,3,2,1,0:T(8,128)(2,1)} %param.5) | copy-start | bytes 589828
  2.2 0.9 %copy-start.3 = (bf16[1,1,1,192,512]{4,3,2,1,0:T(8,128)(2,1)S(1)}, bf16[1,1,1,192,512]{4,3,2,1,0:T(8,128)(2,1)}, u32[]{:S(2)}) copy-start(bf16[1,1,1,192,512]{4,3,2,1,0:T(8,128)(2,1)} %param.9) | copy-start | bytes 589828
  3.1 0.7 %copy-start.4 = (s32[1,1,1,512]{3,2,1,0:T(1,128)S(1)}, s32[1,1,1,512]{3,2,1,0:T(1,128)}, u32[]{:S(2)}) copy-start(s32[1,1,1,512]{3,2,1,0:T(1,128)} %param.6) | copy-start | bytes 6148
  4.1 5.4 %collective-permute-start = (bf16[304,128]{1,0:T(8,128)(2,1)S(1)}, bf16[304,128]{1,0:T(8,128)(2,1)S(1)}, u32[]{:S(2)}, u32[]{:S(2)}) collective-permute-start(bf16[304,128]{1,0:T(8,128)(2,1)S(1)} %get-tuple-element.24), channel_id=1, source_target_pairs={{0,8},{8,0},{16,24},{24,16},{1,9},{9,1},{17,25},{25,17},{2,10},{10... | collective-permute-start | bytes 233480 | tf_op jit(solution)/shard_map/ppermute | solution.py:393
  7.1 2.4 %collective-permute-start.1 = (bf16[304,128]{1,0:T(8,128)(2,1)S(1)}, bf16[304,128]{1,0:T(8,128)(2,1)S(1)}, u32[]{:S(2)}, u32[]{:S(2)}) collective-permute-start(bf16[304,128]{1,0:T(8,128)(2,1)S(1)} %get-tuple-element.25), channel_id=1, source_target_pairs={{8,16},{16,8},{9,17},{17,9},{10,18},{18,10},{11,19},{19,11},{12,20... | collective-permute-start | bytes 233480 | tf_op jit(solution)/shard_map/ppermute | solution.py:399
  7.8 1.8 %copy-start = (bf16[192,27,192]{2,0,1:T(8,128)(2,1)S(1)}, bf16[192,27,192]{2,0,1:T(8,128)(2,1)}, u32[]{:S(2)}) copy-start(bf16[192,27,192]{2,0,1:T(8,128)(2,1)} %param.8) | copy-start | bytes 5971972
  9.5 8.9 %copy-start.1 = (bf16[192,27,192]{2,0,1:T(8,128)(2,1)S(1)}, bf16[192,27,192]{2,0,1:T(8,128)(2,1)}, u32[]{:S(2)}) copy-start(bf16[192,27,192]{2,0,1:T(8,128)(2,1)} %param.8) | copy-start | bytes 5971972
  9.7 8.5 %collective-permute-start.2 = (bf16[432,128]{1,0:T(8,128)(2,1)S(1)}, bf16[432,128]{1,0:T(8,128)(2,1)S(1)}, u32[]{:S(2)}, u32[]{:S(2)}) collective-permute-start(bf16[432,128]{1,0:T(8,128)(2,1)S(1)} %get-tuple-element.26), channel_id=1, source_target_pairs={{0,1},{1,0},{2,3},{3,2},{4,5},{5,4},{6,7},{7,6},{8,9},{9,8},{10,11... | collective-permute-start | bytes 331784 | tf_op jit(solution)/shard_map/ppermute | solution.py:393
  9.7 8.5 %collective-permute-start.3 = (bf16[432,128]{1,0:T(8,128)(2,1)S(1)}, bf16[432,128]{1,0:T(8,128)(2,1)S(1)}, u32[]{:S(2)}, u32[]{:S(2)}) collective-permute-start(bf16[432,128]{1,0:T(8,128)(2,1)S(1)} %get-tuple-element.27), channel_id=1, source_target_pairs={{1,2},{3,4},{5,6},{2,1},{4,3},{6,5},{9,10},{11,12},{13,14},{10,9},... | collective-permute-start | bytes 331784 | tf_op jit(solution)/shard_map/ppermute | solution.py:399
  10.5 13.1 %collective-permute-start.4 = (bf16[192,512]{1,0:T(8,128)(2,1)S(1)}, bf16[192,512]{1,0:T(8,128)(2,1)S(1)}, u32[]{:S(2)}, u32[]{:S(2)}) collective-permute-start(bf16[192,512]{1,0:T(8,128)(2,1)S(1)} %get-tuple-element.35.refs_0_), channel_id=1, source_target_pairs={{0,8},{8,0},{16,24},{24,16},{1,9},{9,1},{17,25},{25,17},{2,10},{10... | collective-permute-start | bytes 589832 | tf_op jit(solution)/shard_map/ppermute | solution.py:393
  15.3 9.7 %collective-permute-start.5 = (bf16[192,512]{1,0:T(8,128)(2,1)S(1)}, bf16[192,512]{1,0:T(8,128)(2,1)S(1)}, u32[]{:S(2)}, u32[]{:S(2)}) collective-permute-start(bf16[192,512]{1,0:T(8,128)(2,1)S(1)} %get-tuple-element.35.refs_0_), channel_id=1, source_target_pairs={{0,16},{8,24},{16,0},{24,8},{1,17},{9,25},{17,1},{25,9},{2,18},{10... | collective-permute-start | bytes 589832 | tf_op jit(solution)/shard_map/ppermute | solution.py:393
  16.8 9.4 %collective-permute-start.6 = (bf16[192,512]{1,0:T(8,128)(2,1)S(1)}, bf16[192,512]{1,0:T(8,128)(2,1)S(1)}, u32[]{:S(2)}, u32[]{:S(2)}) collective-permute-start(bf16[192,512]{1,0:T(8,128)(2,1)S(1)} %get-tuple-element.35.refs_0_), channel_id=1, source_target_pairs={{0,24},{8,16},{16,8},{24,0},{1,25},{9,17},{17,9},{25,1},{2,26},{10... | collective-permute-start | bytes 589832 | tf_op jit(solution)/shard_map/ppermute | solution.py:393
  21.4 19.7 %copy-start.5 = (s32[1,1,1,512]{3,2,1,0:T(1,128)S(1)}, s32[1,1,1,512]{3,2,1,0:T(1,128)}, u32[]{:S(2)}) copy-start(s32[1,1,1,512]{3,2,1,0:T(1,128)} %param.6) | copy-start | bytes 6148
  21.5 5.5 %collective-permute-start.7 = (bf16[48,896]{1,0:T(8,128)(2,1)S(1)}, bf16[48,896]{1,0:T(8,128)(2,1)S(1)}, u32[]{:S(2)}, u32[]{:S(2)}) collective-permute-start(bf16[48,896]{1,0:T(8,128)(2,1)S(1)} %get-tuple-element.43), channel_id=1, source_target_pairs={{0,8},{8,0},{16,24},{24,16},{1,9},{9,1},{17,25},{25,17},{2,10},{10... | collective-permute-start | bytes 258056 | tf_op jit(solution)/shard_map/ppermute | solution.py:393
  22.1 8.2 %collective-permute-start.8 = (bf16[48,896]{1,0:T(8,128)(2,1)S(1)}, bf16[48,896]{1,0:T(8,128)(2,1)S(1)}, u32[]{:S(2)}, u32[]{:S(2)}) collective-permute-start(bf16[48,896]{1,0:T(8,128)(2,1)S(1)} %get-tuple-element.42), channel_id=1, source_target_pairs={{0,16},{8,24},{16,0},{24,8},{1,17},{9,25},{17,1},{25,9},{2,18},{10... | collective-permute-start | bytes 258056 | tf_op jit(solution)/shard_map/ppermute | solution.py:393
  23.6 6.7 %collective-permute-start.9 = (bf16[48,896]{1,0:T(8,128)(2,1)S(1)}, bf16[48,896]{1,0:T(8,128)(2,1)S(1)}, u32[]{:S(2)}, u32[]{:S(2)}) collective-permute-start(bf16[48,896]{1,0:T(8,128)(2,1)S(1)} %get-tuple-element.41), channel_id=1, source_target_pairs={{0,24},{8,16},{16,8},{24,0},{1,25},{9,17},{17,9},{25,1},{2,26},{10... | collective-permute-start | bytes 258056 | tf_op jit(solution)/shard_map/ppermute | solution.py:393
  33.0 2.6 %collective-permute-start.10 = (bf16[4,272,128]{2,1,0:T(8,128)(2,1)S(1)}, bf16[4,272,128]{2,1,0:T(8,128)(2,1)S(1)}, u32[]{:S(2)}, u32[]{:S(2)}) collective-permute-start(bf16[4,272,128]{2,1,0:T(8,128)(2,1)S(1)} %get-tuple-element.38), channel_id=1, source_target_pairs={{0,1},{1,0},{2,3},{3,2},{4,5},{5,4},{6,7},{7,6},{8,9},{9,8},{10,11... | collective-permute-start | bytes 835592 | tf_op jit(solution)/shard_map/ppermute | solution.py:393
  35.7 7.8 %collective-permute-start.11 = (bf16[272,128]{1,0:T(8,128)(2,1)S(1)}, bf16[272,128]{1,0:T(8,128)(2,1)S(1)}, u32[]{:S(2)}, u32[]{:S(2)}) collective-permute-start(bf16[272,128]{1,0:T(8,128)(2,1)S(1)} %get-tuple-element.46), channel_id=1, source_target_pairs={{0,6},{1,7},{2,4},{3,5},{4,2},{5,3},{6,0},{7,1},{8,14},{9,15},{10,... | collective-permute-start | bytes 208904 | tf_op jit(solution)/shard_map/ppermute | solution.py:393
  39.5 7.1 %collective-permute-start.12 = (bf16[272,128]{1,0:T(8,128)(2,1)S(1)}, bf16[272,128]{1,0:T(8,128)(2,1)S(1)}, u32[]{:S(2)}, u32[]{:S(2)}) collective-permute-start(bf16[272,128]{1,0:T(8,128)(2,1)S(1)} %get-tuple-element.45), channel_id=1, source_target_pairs={{0,4},{1,5},{2,6},{3,7},{4,0},{5,1},{6,2},{7,3},{8,12},{9,13},{10,... | collective-permute-start | bytes 208904 | tf_op jit(solution)/shard_map/ppermute | solution.py:393
  41.0 5.5 %collective-permute-start.13 = (bf16[272,128]{1,0:T(8,128)(2,1)S(1)}, bf16[272,128]{1,0:T(8,128)(2,1)S(1)}, u32[]{:S(2)}, u32[]{:S(2)}) collective-permute-start(bf16[272,128]{1,0:T(8,128)(2,1)S(1)} %get-tuple-element.44), channel_id=1, source_target_pairs={{0,2},{1,3},{2,0},{3,1},{4,6},{5,7},{6,4},{7,5},{8,10},{9,11},{10,... | collective-permute-start | bytes 208904 | tf_op jit(solution)/shard_map/ppermute | solution.py:393

commit v3 on v2

--- a/solution.py
+++ b/solution.py
@@ -15,13 +15,14 @@
 NT = (((1,), (1,)), ((), ()))
 
 
-def call(body, outs, ins, scratch=(), flops=0, smem=()):
-    specs = [
-        pl.BlockSpec(memory_space=pltpu.SMEM if k in smem else pltpu.VMEM)
-        for k in range(len(ins))
+def call(body, outs, ins, scratch=(), flops=0, smem=(), far=(), short=False):
+    space = {k: pltpu.SMEM for k in smem} | {k: pltpu.HBM for k in far}
+    specs = [pl.BlockSpec(memory_space=space.get(k, pltpu.VMEM)) for k in range(len(ins))]
+    ins = [
+        pltpu.with_memory_space_constraint(a, pltpu.HBM) if k in far else a
+        for k, a in enumerate(ins)
     ]
-    moved = sum(a.size * a.dtype.itemsize for a in ins)
-    moved += sum(a.size * a.dtype.itemsize for a in outs)
+    moved = 0 if short else sum(a.size * a.dtype.itemsize for a in [*ins, *outs])
     return pl.pallas_call(
         body,
         out_shape=tuple(outs),
@@ -88,7 +89,13 @@
     return pos >> 1, pos & 1
 
 
-def prep_body(pos_ref, feat_ref, occ_ref, cot_ref, xm_ref, cm_ref, rows_ref, even_ref, odd_ref):
+def prep_body(pos_ref, feat_hbm, occ_hbm, cot_hbm, xm_ref, cm_ref, rows_ref, even_ref, odd_ref, feat_ref, occ_ref, cot_ref, sems):
+    arrays = ((occ_hbm, occ_ref), (feat_hbm, feat_ref), (cot_hbm, cot_ref))
+    copies = [pltpu.make_async_copy(a, b, sems.at[k]) for k, (a, b) in enumerate(arrays)]
+    for copy in copies:
+        copy.start()
+    for copy in copies:
+        copy.wait()
     px, py = spot(pos_ref)
     live = occ_ref[...].astype(F32)
     channels = feat_ref.shape[0]
@@ -121,7 +128,7 @@
     return jnp.full((1, 1, channels), value, jnp.int32).astype(F32).astype(BF)
 
 
-def strips_body(pos_ref, xm_ref, cm_ref, xeven_ref, xodd_ref, near_ref, even_ref, odd_ref):
+def strips_body(pos_ref, xm_ref, cm_ref, xeven_ref, xodd_ref, even_ref, odd_ref):
     px, py = spot(pos_ref)
     channels = xm_ref.shape[1]
     one = scalar_rows(1, channels)
@@ -179,7 +186,7 @@
     return xm, cot
 
 
-def window_body(pos_ref, xm_ref, cm_ref, xeven_ref, xodd_ref, yeven_ref, yodd_ref, even_ref, odd_ref, cot_ref):
+def window_body(pos_ref, xm_ref, cm_ref, xeven_ref, xodd_ref, yeven_ref, yodd_ref, near_ref, even_ref, odd_ref, cot_ref):
     px, py = spot(pos_ref)
     channels = xm_ref.shape[1]
     f = lambda v: v.astype(F32)
@@ -307,39 +314,43 @@
     return -(-slots * rows // 16) * 16
 
 
-def kernel_grad_body(parts, chips, *refs):
-    bricks, lines = refs[:parts], refs[parts]
-    others = refs[parts + 1 : 2 * parts]
-    outs = refs[2 * parts :]
-    channels = bricks[0].shape[0]
-    block = channels // parts
+def kernel_grad_body(last, chips, *refs):
+    brick_ref, line_ref = refs[:2]
+    outs = refs[2:]
+    before = None
+    if outs[0].shape[0] == 9 and len(outs) > 1:
+        before, outs = outs[0], outs[1:]
+    channels = brick_ref.shape[0]
+    block = line_ref.shape[0]
     width = 3 * block
     place = lax.broadcasted_iota(jnp.int32, (block, WIDE), 1) & (BE - 1)
-    windows = []
-    for k in range(parts):
-        g = (lines[0] if k == 0 else others[k - 1][...]).astype(F32)
-        back = jnp.where(place < BE - 1, pltpu.roll(g, WIDE - 1, 1), 0.0)
-        ahead = jnp.where(place > 0, pltpu.roll(g, 1, 1), 0.0)
-        columns = jnp.concatenate([back, g, ahead], axis=0).T[0:800].reshape(10, 80, width)
-        windows.append((columns.astype(BF), columns[:, 8:72].astype(BF)))
-    left = jnp.concatenate([brick[...] for brick in bricks], axis=1)
+    g = line_ref[...].astype(F32)
+    back = jnp.where(place < BE - 1, pltpu.roll(g, WIDE - 1, 1), 0.0)
+    ahead = jnp.where(place > 0, pltpu.roll(g, 1, 1), 0.0)
+    columns = jnp.concatenate([back, g, ahead], axis=0).T[0:800].reshape(10, 80, width)
+    window, middle = columns.astype(BF), columns[:, 8:72].astype(BF)
+    left = brick_ref[...]
     full, rest, per, slots = packing(width)
     leftover = []
     store = outs[-1]
     for a in range(3):
         for b in range(3):
-            right = []
-            for window, middle in windows:
-                if b == 1:
-                    piece = middle[2 - a : 10 - a]
-                else:
-                    piece = window[2 - a : 10 - a, 8 * (2 - b) : 8 * (2 - b) + 64]
-                right.append(piece.reshape(VOX, width))
-            total = jnp.dot(left, jnp.concatenate(right, axis=0), preferred_element_type=F32)
+            if b == 1:
+                piece = middle[2 - a : 10 - a]
+            else:
+                piece = window[2 - a : 10 - a, 8 * (2 - b) : 8 * (2 - b) + 64]
+            total = jnp.dot(left, piece.reshape(VOX, width), preferred_element_type=F32)
+            if before is not None:
+                total = total + before[3 * a + b]
+            if not last:
+                store[3 * a + b] = total
+                continue
             for n in range(full):
                 store[(3 * a + b) * full + n] = total[:, 128 * n : 128 * n + 128]
             if rest:
                 leftover.append(total[:, 128 * full :])
+    if not last:
+        return
     if rest:
         for n in range(slots - 9 * full):
             some = leftover[n * per : (n + 1) * per]
@@ -417,19 +428,29 @@
         prep_body,
         [brick, brick, plain, face, face],
         [pos, feat, occ, cot],
+        scratch=[
+            pltpu.VMEM((channels, VOX), BF),
+            pltpu.VMEM((1, VOX), jnp.int32),
+            pltpu.VMEM((channels, VOX), BF),
+            pltpu.SemaphoreType.DMA((3,)),
+        ],
         smem=(0,),
+        far=(1, 2, 3),
+        short=True,
     )
     xeven, xodd = swap_pairs(even, odd, "gx")
-    bricks = {k: xor_step(masked, "gx", k) for k in reversed(range(1, parts))}
-    bricks = [masked] + [bricks[k] for k in range(1, parts)]
-    (near,) = call(touch_body, [shape((16, 128), BF)], [taps])
-    even, odd = call(strips_body, [strip, strip], [pos, xm, cm, xeven, xodd, near], smem=(0,))
+    bricks = {k: xor_step(masked, "gx", k) for k in reversed(range(2, parts))}
+    even, odd = call(strips_body, [strip, strip], [pos, xm, cm, xeven, xodd], smem=(0,), short=True)
+    even, odd, taps, again = lax.optimization_barrier((even, odd, taps, masked))
+    bricks = [masked, xor_step(again, "gx", 1)] + [bricks[k] for k in range(2, parts)]
+    (near,) = call(touch_body, [shape((16, 128), BF)], [taps], flops=10**10)
     yeven, yodd = swap_pairs(even, odd, "gy")
     even, odd, wide_cot = call(
         window_body,
         [shape((12, 96, channels), BF), shape((12, 80, channels), BF), shape((10, 80, channels), BF)],
-        [pos, xm, cm, xeven, xodd, yeven, yodd],
+        [pos, xm, cm, xeven, xodd, yeven, yodd, near],
         smem=(0,),
+        short=True,
     )
     flops = 2 * VOX * 27 * channels * channels
     act, slope, lines = call(
@@ -437,7 +458,7 @@
         [brick, shape((10, 80, channels), BF), shape((parts, block, WIDE), BF)],
         [even, odd, wide_cot, taps],
         scratch=[pltpu.VMEM((10, 80, channels), F32)],
-        flops=flops * 3 // 2,
+        short=True,
     )
     others = {k: xor_step(lines[k], "gx", k) for k in reversed(range(1, parts))}
     others = [others[k] for k in range(1, parts)]
@@ -446,18 +467,24 @@
     width = 3 * block
     slots = packing(width)[3]
     count = lines_of(slots, rows)
-    body = functools.partial(kernel_grad_body, parts, chips)
     table = (slots, channels, 128)
+    lines = [lines[0]] + others
+    so_far = []
+    for k in [0, *reversed(range(2, parts))]:
+        body = functools.partial(kernel_grad_body, False, chips)
+        so_far = call(body, [shape((9, channels, width), F32)], [bricks[k], lines[k], *so_far], flops=flops // parts)
+    body = functools.partial(kernel_grad_body, True, chips)
+    ins = [bricks[1], lines[1], *so_far]
     if rows % 8 == 0:
         send, keep = call(
             body,
             [shape((chips, count, 128), BF), shape((chips, count, 128), F32)],
-            bricks + [lines] + others,
+            ins,
             scratch=[pltpu.VMEM(table, F32)],
-            flops=flops,
+            flops=flops // parts,
         )
     else:
-        (store,) = call(body, [shape(table, F32)], bricks + [lines] + others, flops=flops)
+        (store,) = call(body, [shape(table, F32)], ins, flops=flops // parts)
         store = store.reshape(slots, chips, 2, rows, 128).transpose(2, 1, 0, 3, 4)
         store = store.reshape(2, chips, slots * rows, 128)
         store = jnp.pad(store, ((0, 0), (0, 0), (0, count - slots * rows), (0, 0)))
@@ -470,7 +497,7 @@
         [shape((count, 128), F32), shape((chips - 1, count, 128), BF)],
         [keep, recv],
     )
-    came = [xor_step(sends[k - 1], "gy", 2 * k) for k in reversed(range(1, chips))]
+    came = [xor_step(sends[k - 1], "gy", 2 * k) for k in range(1, chips)]
     (w_grad,) = call(
         functools.partial(last_body, slots, width, 1.0 / (parts * line)),
         [shape((27, rows, block), F32)],

time: 47.8 us -> 44.5 us (0.931)
  waiting for transfers between devices: 9.5 us -> 6.93 us
  local copies, waits for them, and re-layouts: 4.32 us -> 2.09 us
  Pallas kernels: 9.75 us -> 11.8 us
  starting transfers between devices: 22.5 us -> 22 us
    ppermute x12, waiting for transfers between devices: 9.5 us -> 6.92 us  [xor_step(): return lax.ppermute(value, axis, [(i, i ^ step) for i in range(count)])]
    unnamed x12 -> x6, local copies, waits for them, and re-layouts: 4.28 us -> 2.05 us
    pallas_call x9 -> x12, Pallas kernels: 9.75 us -> 11.8 us  [call(): pl.pallas_call(body, out_shape=tuple(outs), in_specs=specs, out_specs=tup...]
  transfers between devices with their start and end apart: 14 -> 14, of which waited for: 5 -> 4; matrix products, arithmetic and copies ran while one was open for 0% -> 0% of each run, Pallas kernels for 12% -> 19%
where the time goes in v3:
time: 44.5 us; the launch traced here: 44.3 us
  starting transfers between devices  22 us (49%)
  Pallas kernels  11.8 us (27%)
  waiting for transfers between devices  6.93 us (16%)
  local copies, waits for them, and re-layouts  2.09 us (5%)
  between operations  1.41 us (3%)
    ppermute x12, starting transfers between devices, xor_step(): return lax.ppermute(value, axis, [(i, i ^ step) for i in range(count)])  20.7 us
    pallas_call x12, Pallas kernels, call(): pl.pallas_call(body, out_shape=tuple(outs), in_specs=specs, out_specs=tup...  11.8 us
    ppermute x12, waiting for transfers between devices, xor_step(): return lax.ppermute(value, axis, [(i, i ^ step) for i in range(count)])  6.92 us
    unnamed x6, local copies, waits for them, and re-layouts  2.05 us
    ppermute x2, starting transfers between devices, swap_pairs(): odd = lax.ppermute(odd, axis, later + [(j, i) for i, j in later])  1.32 us
  transfers between devices with their start and end apart: 14, of which 4 were waited for; matrix products, arithmetic and copies ran while one was open for 0% of the time, Pallas kernels for 19%

profile of v3, /device:TPU:0, one launch (start us, length us, event | category | flops | bytes accessed | tf_op | source)
XLA Modules:
  0.0 44.3 jit_solution(586520720100568430)
XLA Ops:
  1.3 1.4 %shard_map.76 = (bf16[512,192]{1,0:T(8,128)(2,1)S(1)}, bf16[512,192]{1,0:T(8,128)(2,1)S(1)}, bf16[192,512]{1,0:T(8,128)(2,1)S(1)}, bf16[304,128]{1,0:T(8,128)(2,1)S(1)}, bf16[304,128]{1,0:T(8,128)(2,1)S(1)}) custom-call(s32[1]{0:T(128)} %bitcast.22.pos_ref, bf16[192,512]{1,0:T(8,128)(2,1)} %bitcast.31, s32[1,512]{1,0:T(1,128)} %bitcast.28, ...), custom_call_target="tpu_custom_call" | custom-call | tf_op jit(solution)/shard_map/pallas_call | solution.py:26
  2.6 3.0 %collective-permute-start = (bf16[304,128]{1,0:T(8,128)(2,1)S(1)}, bf16[304,128]{1,0:T(8,128)(2,1)S(1)}, u32[]{:S(2)}, u32[]{:S(2)}) collective-permute-start(bf16[304,128]{1,0:T(8,128)(2,1)S(1)} %get-tuple-element.28), channel_id=1, source_target_pairs={{0,8},{8,0},{16,24},{24,16},{1,9},{9,1},{17,25},{25,17},{2,10},{10... | collective-permute-start | bytes 233480 | tf_op jit(solution)/shard_map/ppermute | solution.py:404
  5.6 0.7 %collective-permute-start.1 = (bf16[304,128]{1,0:T(8,128)(2,1)S(1)}, bf16[304,128]{1,0:T(8,128)(2,1)S(1)}, u32[]{:S(2)}, u32[]{:S(2)}) collective-permute-start(bf16[304,128]{1,0:T(8,128)(2,1)S(1)} %get-tuple-element.29), channel_id=1, source_target_pairs={{8,16},{16,8},{9,17},{17,9},{10,18},{18,10},{11,19},{19,11},{12,20... | collective-permute-start | bytes 233480 | tf_op jit(solution)/shard_map/ppermute | solution.py:410
  6.3 1.6 %collective-permute-start.8 = (bf16[192,512]{1,0:T(8,128)(2,1)S(1)}, bf16[192,512]{1,0:T(8,128)(2,1)S(1)}, u32[]{:S(2)}, u32[]{:S(2)}) collective-permute-start(bf16[192,512]{1,0:T(8,128)(2,1)S(1)} %get-tuple-element.43.refs_0_), channel_id=1, source_target_pairs={{0,24},{8,16},{16,8},{24,0},{1,25},{9,17},{17,9},{25,1},{2,26},{10... | collective-permute-start | bytes 589832 | tf_op jit(solution)/shard_map/ppermute | solution.py:404
  7.9 4.2 %collective-permute-start.6 = (bf16[192,512]{1,0:T(8,128)(2,1)S(1)}, bf16[192,512]{1,0:T(8,128)(2,1)S(1)}, u32[]{:S(2)}, u32[]{:S(2)}) collective-permute-start(bf16[192,512]{1,0:T(8,128)(2,1)S(1)} %get-tuple-element.43.refs_0_), channel_id=1, source_target_pairs={{0,16},{8,24},{16,0},{24,8},{1,17},{9,25},{17,1},{25,9},{2,18},{10... | collective-permute-start | bytes 589832 | tf_op jit(solution)/shard_map/ppermute | solution.py:404
  12.1 0.0 collective-permute-done.xeven_ref
  12.1 0.0 collective-permute-done.1.xodd_ref
  12.1 0.2 shard_map.77
  12.2 0.0 collective-permute-start.2
  12.3 0.7 %collective-permute-start.3 = (bf16[432,128]{1,0:T(8,128)(2,1)S(1)}, bf16[432,128]{1,0:T(8,128)(2,1)S(1)}, u32[]{:S(2)}, u32[]{:S(2)}) collective-permute-start(bf16[432,128]{1,0:T(8,128)(2,1)S(1)} %get-tuple-element.34), channel_id=1, source_target_pairs={{1,2},{3,4},{5,6},{2,1},{4,3},{6,5},{9,10},{11,12},{13,14},{10,9},... | collective-permute-start | bytes 331784 | tf_op jit(solution)/shard_map/ppermute | solution.py:410
  12.9 0.0 copy-start
  12.9 1.7 %copy-done = bf16[192,27,192]{2,0,1:T(8,128)(2,1)S(1)} copy-done((bf16[192,27,192]{2,0,1:T(8,128)(2,1)S(1)}, bf16[192,27,192]{2,0,1:T(8,128)(2,1)}, u32[]{:S(2)}) %copy-start) | copy-done | bytes 1990680
  14.7 0.0 copy-start.1
  14.7 1.3 %collective-permute-start.4 = (bf16[192,512]{1,0:T(8,128)(2,1)S(1)}, bf16[192,512]{1,0:T(8,128)(2,1)S(1)}, u32[]{:S(2)}, u32[]{:S(2)}) collective-permute-start(bf16[192,512]{1,0:T(8,128)(2,1)S(1)} %get-tuple-element.43.refs_0_), channel_id=1, source_target_pairs={{0,8},{8,0},{16,24},{24,16},{1,9},{9,1},{17,25},{25,17},{2,10},{10... | collective-permute-start | bytes 589832 | tf_op jit(solution)/shard_map/ppermute | solution.py:404
  15.9 0.0 collective-permute-done.2.yeven_ref
  15.9 0.0 collective-permute-done.3.yodd_ref
  15.9 0.2 shard_map.79
  16.1 0.3 copy-done.1
  16.4 3.0 %shard_map.80 = (bf16[512,192]{1,0:T(8,128)(2,1)S(1)}, bf16[10,80,192]{2,1,0:T(8,128)(2,1)S(1)}, bf16[4,48,896]{2,1,0:T(8,128)(2,1)S(1)}) custom-call(bf16[12,96,192]{2,1,0:T(8,128)(2,1)S(1)} %get-tuple-element.36.even_ref, bf16[12,80,192]{2,1,0:T(8,128)(2,1)S(1)} %get-tuple-element.37.odd_ref, bf16[10,80,192]{2,1,0:T(8,128)(2,1)S(1)} %get-tuple-element.38.cot_ref, ...), custom_call_target="tpu_custom_call" | custom-call | tf_op jit(solution)/shard_map/pallas_call | solution.py:26
  19.5 3.2 %collective-permute-start.9 = (bf16[48,896]{1,0:T(8,128)(2,1)S(1)}, bf16[48,896]{1,0:T(8,128)(2,1)S(1)}, u32[]{:S(2)}, u32[]{:S(2)}) collective-permute-start(bf16[48,896]{1,0:T(8,128)(2,1)S(1)} %get-tuple-element.50), channel_id=1, source_target_pairs={{0,24},{8,16},{16,8},{24,0},{1,25},{9,17},{17,9},{25,1},{2,26},{10... | collective-permute-start | bytes 258056 | tf_op jit(solution)/shard_map/ppermute | solution.py:404
  22.8 0.1 collective-permute-start.7
  22.9 0.0 collective-permute-done.8.refs_0_
  22.9 1.4 %collective-permute-start.5 = (bf16[48,896]{1,0:T(8,128)(2,1)S(1)}, bf16[48,896]{1,0:T(8,128)(2,1)S(1)}, u32[]{:S(2)}, u32[]{:S(2)}) collective-permute-start(bf16[48,896]{1,0:T(8,128)(2,1)S(1)} %get-tuple-element.52), channel_id=1, source_target_pairs={{0,8},{8,0},{16,24},{24,16},{1,9},{9,1},{17,25},{25,17},{2,10},{10... | collective-permute-start | bytes 258056 | tf_op jit(solution)/shard_map/ppermute | solution.py:404
  24.3 0.9 %shard_map.82.refs_2_ = f32[9,192,144]{2,1,0:T(8,128)S(1)} custom-call(bf16[192,512]{1,0:T(8,128)(2,1)S(1)} %get-tuple-element.43.refs_0_, bf16[48,896]{1,0:T(8,128)(2,1)S(1)} %get-tuple-element.49.refs_1_), custom_call_target="tpu_custom_call" | custom-call | flops 254803968 | bytes 1277952 | tf_op jit(solution)/shard_map/pallas_call | solution.py:26
  25.2 0.9 %collective-permute-done.9.refs_1_ = bf16[48,896]{1,0:T(8,128)(2,1)S(1)} collective-permute-done((bf16[48,896]{1,0:T(8,128)(2,1)S(1)}, bf16[48,896]{1,0:T(8,128)(2,1)S(1)}, u32[]{:S(2)}, u32[]{:S(2)}) %collective-permute-start.9) | collective-permute-done | bytes 86048 | tf_op jit(solution)/shard_map/ppermute | solution.py:404
  26.1 0.9 %shard_map.83.refs_2_ = f32[9,192,144]{2,1,0:T(8,128)S(1)} custom-call(bf16[192,512]{1,0:T(8,128)(2,1)S(1)} %collective-permute-done.8.refs_0_, bf16[48,896]{1,0:T(8,128)(2,1)S(1)} %collective-permute-done.9.refs_1_, f32[9,192,144]{2,1,0:T(8,128)S(1)} %shard_map.82.refs_2_), custom_call_target="tpu_custom_call" | custom-call | flops 254803968 | bytes 2273280 | tf_op jit(solution)/shard_map/pallas_call | solution.py:26
  27.0 0.0 collective-permute-done.6.refs_0_
  27.0 1.4 %collective-permute-done.7.refs_1_ = bf16[48,896]{1,0:T(8,128)(2,1)S(1)} collective-permute-done((bf16[48,896]{1,0:T(8,128)(2,1)S(1)}, bf16[48,896]{1,0:T(8,128)(2,1)S(1)}, u32[]{:S(2)}, u32[]{:S(2)}) %collective-permute-start.7) | collective-permute-done | bytes 86048 | tf_op jit(solution)/shard_map/ppermute | solution.py:404
  28.4 0.9 %shard_map.84.refs_2_ = f32[9,192,144]{2,1,0:T(8,128)S(1)} custom-call(bf16[192,512]{1,0:T(8,128)(2,1)S(1)} %collective-permute-done.6.refs_0_, bf16[48,896]{1,0:T(8,128)(2,1)S(1)} %collective-permute-done.7.refs_1_, f32[9,192,144]{2,1,0:T(8,128)S(1)} %shard_map.83.refs_2_), custom_call_target="tpu_custom_call" | custom-call | flops 254803968 | bytes 2273280 | tf_op jit(solution)/shard_map/pallas_call | solution.py:26
  29.3 0.0 copy-start.2
  29.3 0.0 collective-permute-done.4.refs_0_
  29.3 0.0 collective-permute-done.5.refs_1_
  29.4 1.0 %shard_map.85 = (bf16[4,272,128]{2,1,0:T(8,128)(2,1)S(1)}, f32[4,272,128]{2,1,0:T(8,128)S(1)}) custom-call(bf16[192,512]{1,0:T(8,128)(2,1)S(1)} %collective-permute-done.4.refs_0_, bf16[48,896]{1,0:T(8,128)(2,1)S(1)} %collective-permute-done.5.refs_1_, f32[9,192,144]{2,1,0:T(8,128)S(1)} %shard_map.84.refs_2_), custom_call_target="tpu_custom_call" | custom-call | flops 254803968 | bytes 2113536 | tf_op jit(solution)/shard_map/pallas_call | solution.py:26
  30.4 0.5 %collective-permute-start.10 = (bf16[4,272,128]{2,1,0:T(8,128)(2,1)S(1)}, bf16[4,272,128]{2,1,0:T(8,128)(2,1)S(1)}, u32[]{:S(2)}, u32[]{:S(2)}) collective-permute-start(bf16[4,272,128]{2,1,0:T(8,128)(2,1)S(1)} %get-tuple-element.46), channel_id=1, source_target_pairs={{0,1},{1,0},{2,3},{3,2},{4,5},{5,4},{6,7},{7,6},{8,9},{9,8},{10,11... | collective-permute-start | bytes 835592 | tf_op jit(solution)/shard_map/ppermute | solution.py:404
  30.9 1.2 %collective-permute-done.10.recv_ref = bf16[4,272,128]{2,1,0:T(8,128)(2,1)S(1)} collective-permute-done((bf16[4,272,128]{2,1,0:T(8,128)(2,1)S(1)}, bf16[4,272,128]{2,1,0:T(8,128)(2,1)S(1)}, u32[]{:S(2)}, u32[]{:S(2)}) %collective-permute-start.10) | collective-permute-done | bytes 278560 | tf_op jit(solution)/shard_map/ppermute | solution.py:404
  32.1 0.1 shard_map.86
  32.2 4.2 %collective-permute-start.13 = (bf16[272,128]{1,0:T(8,128)(2,1)S(1)}, bf16[272,128]{1,0:T(8,128)(2,1)S(1)}, u32[]{:S(2)}, u32[]{:S(2)}) collective-permute-start(bf16[272,128]{1,0:T(8,128)(2,1)S(1)} %get-tuple-element.53), channel_id=1, source_target_pairs={{0,6},{1,7},{2,4},{3,5},{4,2},{5,3},{6,0},{7,1},{8,14},{9,15},{10,... | collective-permute-start | bytes 208904 | tf_op jit(solution)/shard_map/ppermute | solution.py:404
  36.4 1.0 %collective-permute-start.12 = (bf16[272,128]{1,0:T(8,128)(2,1)S(1)}, bf16[272,128]{1,0:T(8,128)(2,1)S(1)}, u32[]{:S(2)}, u32[]{:S(2)}) collective-permute-start(bf16[272,128]{1,0:T(8,128)(2,1)S(1)} %get-tuple-element.54), channel_id=1, source_target_pairs={{0,4},{1,5},{2,6},{3,7},{4,0},{5,1},{6,2},{7,3},{8,12},{9,13},{10,... | collective-permute-start | bytes 208904 | tf_op jit(solution)/shard_map/ppermute | solution.py:404
  37.4 0.1 collective-permute-start.11
  37.5 0.0 copy-done.2
  37.5 2.4 %shard_map.81 = (bf16[192,512]{1,0:T(8,128)(2,1)}, bf16[192,512]{1,0:T(8,128)(2,1)}) custom-call(bf16[10,80,192]{2,1,0:T(8,128)(2,1)S(1)} %get-tuple-element.39.slope_ref, bf16[512,192]{1,0:T(8,128)(2,1)S(1)} %get-tuple-element.40.act_ref, s32[1,512]{1,0:T(1,128)S(1)} %bitcast.29, bf16[27,192,192]{2,1,0:T(8,128)(2,1)S(1)} %bitcast.27), custom_call_target="tpu_custom_call" | custom-call | flops 1019215872 | bytes 2889728 | tf_op jit(solution)/shard_map/pallas_call | solution.py:26
  39.9 0.0 collective-permute-done.13.refs_3_
  39.9 3.4 %collective-permute-done.12.refs_2_ = bf16[272,128]{1,0:T(8,128)(2,1)S(1)} collective-permute-done((bf16[272,128]{1,0:T(8,128)(2,1)S(1)}, bf16[272,128]{1,0:T(8,128)(2,1)S(1)}, u32[]{:S(2)}, u32[]{:S(2)}) %collective-permute-start.12) | collective-permute-done | bytes 69664 | tf_op jit(solution)/shard_map/ppermute | solution.py:404
  43.3 0.0 collective-permute-done.11.refs_1_
  43.3 0.9 %shard_map.87 = f32[27,24,48]{2,1,0:T(8,128)} custom-call(f32[272,128]{1,0:T(8,128)S(1)} %get-tuple-element.47.refs_0_, bf16[272,128]{1,0:T(8,128)(2,1)S(1)} %collective-permute-done.11.refs_1_, bf16[272,128]{1,0:T(8,128)(2,1)S(1)} %collective-permute-done.12.refs_2_, bf16[272,128]{1,0:T(8,128)(2,1)S(1)} %collective-permute-done.13.refs_3_), custom_call_target="tpu_custom_call" | custom-call | bytes 472576 | tf_op jit(solution)/shard_map/pallas_call | solution.py:26
  (3 shorter events, 0.0 us)
Async XLA Ops:
  2.6 9.4 %collective-permute-start = (bf16[304,128]{1,0:T(8,128)(2,1)S(1)}, bf16[304,128]{1,0:T(8,128)(2,1)S(1)}, u32[]{:S(2)}, u32[]{:S(2)}) collective-permute-start(bf16[304,128]{1,0:T(8,128)(2,1)S(1)} %get-tuple-element.28), channel_id=1, source_target_pairs={{0,8},{8,0},{16,24},{24,16},{1,9},{9,1},{17,25},{25,17},{2,10},{10... | collective-permute-start | bytes 233480 | tf_op jit(solution)/shard_map/ppermute | solution.py:404
  5.6 6.4 %collective-permute-start.1 = (bf16[304,128]{1,0:T(8,128)(2,1)S(1)}, bf16[304,128]{1,0:T(8,128)(2,1)S(1)}, u32[]{:S(2)}, u32[]{:S(2)}) collective-permute-start(bf16[304,128]{1,0:T(8,128)(2,1)S(1)} %get-tuple-element.29), channel_id=1, source_target_pairs={{8,16},{16,8},{9,17},{17,9},{10,18},{18,10},{11,19},{19,11},{12,20... | collective-permute-start | bytes 233480 | tf_op jit(solution)/shard_map/ppermute | solution.py:410
  6.3 16.6 %collective-permute-start.8 = (bf16[192,512]{1,0:T(8,128)(2,1)S(1)}, bf16[192,512]{1,0:T(8,128)(2,1)S(1)}, u32[]{:S(2)}, u32[]{:S(2)}) collective-permute-start(bf16[192,512]{1,0:T(8,128)(2,1)S(1)} %get-tuple-element.43.refs_0_), channel_id=1, source_target_pairs={{0,24},{8,16},{16,8},{24,0},{1,25},{9,17},{17,9},{25,1},{2,26},{10... | collective-permute-start | bytes 589832 | tf_op jit(solution)/shard_map/ppermute | solution.py:404
  7.9 19.1 %collective-permute-start.6 = (bf16[192,512]{1,0:T(8,128)(2,1)S(1)}, bf16[192,512]{1,0:T(8,128)(2,1)S(1)}, u32[]{:S(2)}, u32[]{:S(2)}) collective-permute-start(bf16[192,512]{1,0:T(8,128)(2,1)S(1)} %get-tuple-element.43.refs_0_), channel_id=1, source_target_pairs={{0,16},{8,24},{16,0},{24,8},{1,17},{9,25},{17,1},{25,9},{2,18},{10... | collective-permute-start | bytes 589832 | tf_op jit(solution)/shard_map/ppermute | solution.py:404
  12.2 3.7 %collective-permute-start.2 = (bf16[432,128]{1,0:T(8,128)(2,1)S(1)}, bf16[432,128]{1,0:T(8,128)(2,1)S(1)}, u32[]{:S(2)}, u32[]{:S(2)}) collective-permute-start(bf16[432,128]{1,0:T(8,128)(2,1)S(1)} %get-tuple-element.33), channel_id=1, source_target_pairs={{0,1},{1,0},{2,3},{3,2},{4,5},{5,4},{6,7},{7,6},{8,9},{9,8},{10,11... | collective-permute-start | bytes 331784 | tf_op jit(solution)/shard_map/ppermute | solution.py:404
  12.3 3.7 %collective-permute-start.3 = (bf16[432,128]{1,0:T(8,128)(2,1)S(1)}, bf16[432,128]{1,0:T(8,128)(2,1)S(1)}, u32[]{:S(2)}, u32[]{:S(2)}) collective-permute-start(bf16[432,128]{1,0:T(8,128)(2,1)S(1)} %get-tuple-element.34), channel_id=1, source_target_pairs={{1,2},{3,4},{5,6},{2,1},{4,3},{6,5},{9,10},{11,12},{13,14},{10,9},... | collective-permute-start | bytes 331784 | tf_op jit(solution)/shard_map/ppermute | solution.py:410
  12.9 1.8 %copy-start = (bf16[192,27,192]{2,0,1:T(8,128)(2,1)S(1)}, bf16[192,27,192]{2,0,1:T(8,128)(2,1)}, u32[]{:S(2)}) copy-start(bf16[192,27,192]{2,0,1:T(8,128)(2,1)} %param.8) | copy-start | bytes 5971972
  14.7 1.7 %copy-start.1 = (bf16[192,27,192]{2,0,1:T(8,128)(2,1)S(1)}, bf16[192,27,192]{2,0,1:T(8,128)(2,1)}, u32[]{:S(2)}) copy-start(bf16[192,27,192]{2,0,1:T(8,128)(2,1)} %param.8) | copy-start | bytes 5971972
  14.7 14.7 %collective-permute-start.4 = (bf16[192,512]{1,0:T(8,128)(2,1)S(1)}, bf16[192,512]{1,0:T(8,128)(2,1)S(1)}, u32[]{:S(2)}, u32[]{:S(2)}) collective-permute-start(bf16[192,512]{1,0:T(8,128)(2,1)S(1)} %get-tuple-element.43.refs_0_), channel_id=1, source_target_pairs={{0,8},{8,0},{16,24},{24,16},{1,9},{9,1},{17,25},{25,17},{2,10},{10... | collective-permute-start | bytes 589832 | tf_op jit(solution)/shard_map/ppermute | solution.py:404
  19.5 6.6 %collective-permute-start.9 = (bf16[48,896]{1,0:T(8,128)(2,1)S(1)}, bf16[48,896]{1,0:T(8,128)(2,1)S(1)}, u32[]{:S(2)}, u32[]{:S(2)}) collective-permute-start(bf16[48,896]{1,0:T(8,128)(2,1)S(1)} %get-tuple-element.50), channel_id=1, source_target_pairs={{0,24},{8,16},{16,8},{24,0},{1,25},{9,17},{17,9},{25,1},{2,26},{10... | collective-permute-start | bytes 258056 | tf_op jit(solution)/shard_map/ppermute | solution.py:404
  22.8 5.7 %collective-permute-start.7 = (bf16[48,896]{1,0:T(8,128)(2,1)S(1)}, bf16[48,896]{1,0:T(8,128)(2,1)S(1)}, u32[]{:S(2)}, u32[]{:S(2)}) collective-permute-start(bf16[48,896]{1,0:T(8,128)(2,1)S(1)} %get-tuple-element.51), channel_id=1, source_target_pairs={{0,16},{8,24},{16,0},{24,8},{1,17},{9,25},{17,1},{25,9},{2,18},{10... | collective-permute-start | bytes 258056 | tf_op jit(solution)/shard_map/ppermute | solution.py:404
  22.9 6.4 %collective-permute-start.5 = (bf16[48,896]{1,0:T(8,128)(2,1)S(1)}, bf16[48,896]{1,0:T(8,128)(2,1)S(1)}, u32[]{:S(2)}, u32[]{:S(2)}) collective-permute-start(bf16[48,896]{1,0:T(8,128)(2,1)S(1)} %get-tuple-element.52), channel_id=1, source_target_pairs={{0,8},{8,0},{16,24},{24,16},{1,9},{9,1},{17,25},{25,17},{2,10},{10... | collective-permute-start | bytes 258056 | tf_op jit(solution)/shard_map/ppermute | solution.py:404
  29.3 8.2 %copy-start.2 = (s32[1,1,1,512]{3,2,1,0:T(1,128)S(1)}, s32[1,1,1,512]{3,2,1,0:T(1,128)}, u32[]{:S(2)}) copy-start(s32[1,1,1,512]{3,2,1,0:T(1,128)} %param.6) | copy-start | bytes 6148
  30.4 1.7 %collective-permute-start.10 = (bf16[4,272,128]{2,1,0:T(8,128)(2,1)S(1)}, bf16[4,272,128]{2,1,0:T(8,128)(2,1)S(1)}, u32[]{:S(2)}, u32[]{:S(2)}) collective-permute-start(bf16[4,272,128]{2,1,0:T(8,128)(2,1)S(1)} %get-tuple-element.46), channel_id=1, source_target_pairs={{0,1},{1,0},{2,3},{3,2},{4,5},{5,4},{6,7},{7,6},{8,9},{9,8},{10,11... | collective-permute-start | bytes 835592 | tf_op jit(solution)/shard_map/ppermute | solution.py:404
  32.2 7.8 %collective-permute-start.13 = (bf16[272,128]{1,0:T(8,128)(2,1)S(1)}, bf16[272,128]{1,0:T(8,128)(2,1)S(1)}, u32[]{:S(2)}, u32[]{:S(2)}) collective-permute-start(bf16[272,128]{1,0:T(8,128)(2,1)S(1)} %get-tuple-element.53), channel_id=1, source_target_pairs={{0,6},{1,7},{2,4},{3,5},{4,2},{5,3},{6,0},{7,1},{8,14},{9,15},{10,... | collective-permute-start | bytes 208904 | tf_op jit(solution)/shard_map/ppermute | solution.py:404
  36.4 7.0 %collective-permute-start.12 = (bf16[272,128]{1,0:T(8,128)(2,1)S(1)}, bf16[272,128]{1,0:T(8,128)(2,1)S(1)}, u32[]{:S(2)}, u32[]{:S(2)}) collective-permute-start(bf16[272,128]{1,0:T(8,128)(2,1)S(1)} %get-tuple-element.54), channel_id=1, source_target_pairs={{0,4},{1,5},{2,6},{3,7},{4,0},{5,1},{6,2},{7,3},{8,12},{9,13},{10,... | collective-permute-start | bytes 208904 | tf_op jit(solution)/shard_map/ppermute | solution.py:404
  37.4 5.9 %collective-permute-start.11 = (bf16[272,128]{1,0:T(8,128)(2,1)S(1)}, bf16[272,128]{1,0:T(8,128)(2,1)S(1)}, u32[]{:S(2)}, u32[]{:S(2)}) collective-permute-start(bf16[272,128]{1,0:T(8,128)(2,1)S(1)} %get-tuple-element.55), channel_id=1, source_target_pairs={{0,2},{1,3},{2,0},{3,1},{4,6},{5,7},{6,4},{7,5},{8,10},{9,11},{10,... | collective-permute-start | bytes 208904 | tf_op jit(solution)/shard_map/ppermute | solution.py:404

commit v4 on v3

--- a/solution.py
+++ b/solution.py
@@ -15,8 +15,8 @@
 NT = (((1,), (1,)), ((), ()))
 
 
-def call(body, outs, ins, scratch=(), flops=0, smem=(), far=(), short=False):
-    space = {k: pltpu.SMEM for k in smem} | {k: pltpu.HBM for k in far}
+def call(body, outs, ins, scratch=(), flops=0, far=(), anywhere=(), short=False):
+    space = {k: pl.ANY for k in anywhere} | {k: pltpu.HBM for k in far}
     specs = [pl.BlockSpec(memory_space=space.get(k, pltpu.VMEM)) for k in range(len(ins))]
     ins = [
         pltpu.with_memory_space_constraint(a, pltpu.HBM) if k in far else a
@@ -59,7 +59,7 @@
     _, half = packed_rows(rows, channels)
     cut = out_ref.shape[1]
     out_ref[0:rows] = data[:, :cut]
-    out_ref[rows : rows + 16] = jnp.full((16, cut), flag, jnp.int32).astype(F32).astype(BF)
+    out_ref[rows : rows + 16] = flag[:, :cut] + jnp.zeros((16, cut), BF)
     if half:
         second = data[half:, cut:]
         if rows < 2 * half:
@@ -84,36 +84,38 @@
     return data, flag.reshape(1, 1, channels)
 
 
-def spot(pos_ref):
-    pos = pos_ref[0]
-    return pos >> 1, pos & 1
-
-
-def prep_body(pos_ref, feat_hbm, occ_hbm, cot_hbm, xm_ref, cm_ref, rows_ref, even_ref, odd_ref, feat_ref, occ_ref, cot_ref, sems):
-    arrays = ((occ_hbm, occ_ref), (feat_hbm, feat_ref), (cot_hbm, cot_ref))
+def spot(spot_ref):
+    return spot_ref[0:1], spot_ref[16:17]
+
+
+def prep_body(
+    pos_hbm, feat_hbm, occ_hbm, cot_hbm, xm_ref, cm_ref, rows_ref, even_ref, odd_ref, spot_ref, pos_ref, feat_ref, occ_ref, cot_ref, sems
+):
+    arrays = ((pos_hbm, pos_ref), (occ_hbm, occ_ref), (feat_hbm, feat_ref), (cot_hbm, cot_ref))
     copies = [pltpu.make_async_copy(a, b, sems.at[k]) for k, (a, b) in enumerate(arrays)]
     for copy in copies:
         copy.start()
-    for copy in copies:
+    channels = feat_ref.shape[0]
+    for copy in copies[:3]:
         copy.wait()
-    px, py = spot(pos_ref)
+    pos = jnp.full((1, channels), pos_ref[0, 0, 0], jnp.int32)
+    px, py = [place.astype(F32).astype(BF) for place in (pos >> 1, pos & 1)]
+    spot_ref[0:16] = px + jnp.zeros((16, channels), BF)
+    spot_ref[16:32] = py + jnp.zeros((16, channels), BF)
     live = occ_ref[...].astype(F32)
-    channels = feat_ref.shape[0]
     rows = feat_ref[...].astype(F32) * live
     rows_ref[...] = rows.astype(BF)
     xm = rows.T.astype(BF)
+    xm_ref[...] = xm
+    copies[3].wait()
     cm = (cot_ref[...].astype(F32) * live).T.astype(BF)
-    xm_ref[...] = xm
     cm_ref[...] = cm
     up = jnp.concatenate([xm[VOX - 2 * PLANE :], cm[VOX - PLANE :]], axis=0)
     down = jnp.concatenate([xm[: 2 * PLANE], cm[:PLANE]], axis=0)
     odd = lax.axis_index("gx") & 1
     for pair, out in ((0, even_ref), (1, odd_ref)):
         rises = odd == pair
-        data = jnp.where(rises, up, down)
-        touches = jnp.where(rises, px, 1 - px)
-        data = data * jnp.full((1, channels), touches, jnp.int32).astype(F32).astype(BF)
-        pack(out, data, py)
+        pack(out, jnp.where(rises, up * px, down * (1 - px)), py)
 
 
 def x_planes(came, valid):
@@ -124,15 +126,11 @@
     return xm, cot, (1 - flag, flag)
 
 
-def scalar_rows(value, channels):
-    return jnp.full((1, 1, channels), value, jnp.int32).astype(F32).astype(BF)
-
-
-def strips_body(pos_ref, xm_ref, cm_ref, xeven_ref, xodd_ref, even_ref, odd_ref):
-    px, py = spot(pos_ref)
+def strips_body(spot_ref, xm_ref, cm_ref, xeven_ref, xodd_ref, fetched_ref, even_ref, odd_ref):
+    px, py = spot(spot_ref)
     channels = xm_ref.shape[1]
-    one = scalar_rows(1, channels)
-    own_at = (scalar_rows(1 - py, channels), scalar_rows(py, channels))
+    one = jnp.ones((1, 1, channels), BF)
+    own_at = ((1 - py).reshape(1, 1, channels), py.reshape(1, 1, channels))
     xlow, xhigh = sides(xeven_ref, xodd_ref, "gx")
     xl, cl, at_l = x_planes(xlow, one)
     xh, ch, at_h = x_planes(xhigh, one)
@@ -163,7 +161,7 @@
     strip = data[0:Y_XM].reshape(12, 16, channels)
     lines = data[Y_XM:].astype(F32).reshape(10, BE, channels)
     zero_at, one_at = 1 - flag, flag
-    here_high = scalar_rows(px, channels)
+    here_high = px.reshape(1, 1, channels)
     here_low = 1 - here_high
     same = zero_at * here_low + one_at * here_high
     xm = jnp.concatenate(
@@ -186,11 +184,11 @@
     return xm, cot
 
 
-def window_body(pos_ref, xm_ref, cm_ref, xeven_ref, xodd_ref, yeven_ref, yodd_ref, near_ref, even_ref, odd_ref, cot_ref):
-    px, py = spot(pos_ref)
+def window_body(spot_ref, xm_ref, cm_ref, xeven_ref, xodd_ref, yeven_ref, yodd_ref, brick_ref, even_ref, odd_ref, cot_ref):
+    px, py = spot(spot_ref)
     channels = xm_ref.shape[1]
     f = lambda v: v.astype(F32)
-    high_x, high_y = scalar_rows(px, channels), scalar_rows(py, channels)
+    high_x, high_y = px.reshape(1, 1, channels), py.reshape(1, 1, channels)
     low_x, low_y = 1 - high_x, 1 - high_y
     xlow, xhigh = sides(xeven_ref, xodd_ref, "gx")
     xl, cl, at_l = x_planes(xlow, low_x)
@@ -231,8 +229,16 @@
     return jnp.where(keep, moved, 0.0)
 
 
-def touch_body(w_ref, out_ref):
-    out_ref[...] = w_ref[0, 0:16, 0:128]
+def fetch_body(w_hbm, out_ref, done_ref, sem):
+    copies = [
+        pltpu.make_async_copy(w_hbm.at[pl.ds(9 * k, 9)], out_ref.at[pl.ds(9 * k, 9)], sem.at[k])
+        for k in range(3)
+    ]
+    for copy in copies:
+        copy.start()
+    for copy in copies:
+        copy.wait()
+    done_ref[...] = jnp.zeros_like(done_ref)
 
 
 def forward_body(parts, even_ref, odd_ref, cot_ref, w_ref, act_ref, slope_ref, rows_ref, wide_ref):
@@ -419,37 +425,46 @@
     feat = features.reshape(channels, VOX)
     cot = cotangent.reshape(channels, VOX)
     occ = occupancy.reshape(1, VOX)
-    pos = brick_pos.reshape(1)
     taps = weight.transpose(1, 0, 2)
 
     brick, plain = shape((VOX, channels), BF), shape((channels, VOX), BF)
     face, strip = message(X_DATA, channels), message(Y_DATA, channels)
-    xm, cm, masked, even, odd = call(
+    xm, cm, masked, even, odd, place = call(
         prep_body,
-        [brick, brick, plain, face, face],
-        [pos, feat, occ, cot],
+        [brick, brick, plain, face, face, shape((32, channels), BF)],
+        [brick_pos, feat, occ, cot],
         scratch=[
+            pltpu.SMEM((1, 1, 1), jnp.int32),
             pltpu.VMEM((channels, VOX), BF),
             pltpu.VMEM((1, VOX), jnp.int32),
             pltpu.VMEM((channels, VOX), BF),
-            pltpu.SemaphoreType.DMA((3,)),
+            pltpu.SemaphoreType.DMA((4,)),
         ],
-        smem=(0,),
+        anywhere=(0,),
         far=(1, 2, 3),
         short=True,
     )
     xeven, xodd = swap_pairs(even, odd, "gx")
-    bricks = {k: xor_step(masked, "gx", k) for k in reversed(range(2, parts))}
-    even, odd = call(strips_body, [strip, strip], [pos, xm, cm, xeven, xodd], smem=(0,), short=True)
-    even, odd, taps, again = lax.optimization_barrier((even, odd, taps, masked))
-    bricks = [masked, xor_step(again, "gx", 1)] + [bricks[k] for k in range(2, parts)]
-    (near,) = call(touch_body, [shape((16, 128), BF)], [taps], flops=10**10)
+    first = parts - 1
+    bricks = {0: masked, first: xor_step(masked, "gx", first)}
+    taps, fetched = call(
+        fetch_body,
+        [shape(taps.shape, BF), shape((16, 128), BF)],
+        [taps],
+        scratch=[pltpu.SemaphoreType.DMA((3,))],
+        flops=10**9,
+        far=(0,),
+    )
+    even, odd = call(strips_body, [strip, strip], [place, xm, cm, xeven, xodd, fetched], short=True)
+    even, odd, again = lax.optimization_barrier((even, odd, masked))
     yeven, yodd = swap_pairs(even, odd, "gy")
+    for k in reversed(range(1, parts)):
+        if k != first:
+            bricks[k] = xor_step(again, "gx", k)
     even, odd, wide_cot = call(
         window_body,
         [shape((12, 96, channels), BF), shape((12, 80, channels), BF), shape((10, 80, channels), BF)],
-        [pos, xm, cm, xeven, xodd, yeven, yodd, near],
-        smem=(0,),
+        [place, xm, cm, xeven, xodd, yeven, yodd, bricks[first]],
         short=True,
     )
     flops = 2 * VOX * 27 * channels * channels
@@ -470,11 +485,13 @@
     table = (slots, channels, 128)
     lines = [lines[0]] + others
     so_far = []
-    for k in [0, *reversed(range(2, parts))]:
-        body = functools.partial(kernel_grad_body, False, chips)
-        so_far = call(body, [shape((9, channels, width), F32)], [bricks[k], lines[k], *so_far], flops=flops // parts)
-    body = functools.partial(kernel_grad_body, True, chips)
-    ins = [bricks[1], lines[1], *so_far]
+    order = [0, *reversed(range(1, parts))]
+    for k in order:
+        last = k == order[-1]
+        body = functools.partial(kernel_grad_body, last, chips)
+        ins = [bricks[k], lines[k], *so_far]
+        if not last:
+            so_far = call(body, [shape((9, channels, width), F32)], ins, flops=flops // parts)
     if rows % 8 == 0:
         send, keep = call(
             body,
@@ -497,7 +514,7 @@
         [shape((count, 128), F32), shape((chips - 1, count, 128), BF)],
         [keep, recv],
     )
-    came = [xor_step(sends[k - 1], "gy", 2 * k) for k in range(1, chips)]
+    came = [xor_step(sends[k - 1], "gy", 2 * k) for k in reversed(range(1, chips))]
     (w_grad,) = call(
         functools.partial(last_body, slots, width, 1.0 / (parts * line)),
         [shape((27, rows, block), F32)],

time: 44.5 us -> 44.2 us (level)
  local copies, waits for them, and re-layouts: 2.09 us -> 0.05 us
  Pallas kernels: 11.8 us -> 13.6 us
  waiting for transfers between devices: 6.93 us -> 6.22 us
  starting transfers between devices: 22 us -> 22.7 us
    unnamed x6 -> x2, local copies, waits for them, and re-layouts: 2.05 us -> 0.01 us
    pallas_call x12, Pallas kernels: 11.8 us -> 13.6 us  [call(): pl.pallas_call(body, out_shape=tuple(outs), in_specs=specs, out_specs=tup...]
    ppermute x12, starting transfers between devices: 20.7 us -> 21.4 us  [xor_step(): return lax.ppermute(value, axis, [(i, i ^ step) for i in range(count)])]
    ppermute x12, waiting for transfers between devices: 6.92 us -> 6.22 us  [xor_step(): return lax.ppermute(value, axis, [(i, i ^ step) for i in range(count)])]
  transfers between devices with their start and end apart: 14 -> 14, of which waited for: 4 -> 5; matrix products, arithmetic and copies ran while one was open for 0% -> 0% of each run, Pallas kernels for 19% -> 23%
where the time goes in v4:
time: 44.2 us; the launch traced here: 44 us
  starting transfers between devices  22.7 us (51%)
  Pallas kernels  13.6 us (31%)
  waiting for transfers between devices  6.22 us (14%)
  between operations  1.42 us (3%)
    ppermute x12, starting transfers between devices, xor_step(): return lax.ppermute(value, axis, [(i, i ^ step) for i in range(count)])  21.4 us
    pallas_call x12, Pallas kernels, call(): pl.pallas_call(body, out_shape=tuple(outs), in_specs=specs, out_specs=tup...  13.6 us
    ppermute x12, waiting for transfers between devices, xor_step(): return lax.ppermute(value, axis, [(i, i ^ step) for i in range(count)])  6.22 us
    ppermute x2, starting transfers between devices, swap_pairs(): odd = lax.ppermute(odd, axis, later + [(j, i) for i, j in later])  1.32 us
  transfers between devices with their start and end apart: 14, of which 5 were waited for; matrix products, arithmetic and copies ran while one was open for 0% of the time, Pallas kernels for 23%

profile of v4, /device:TPU:0, one launch (start us, length us, event | category | flops | bytes accessed | tf_op | source)
XLA Modules:
  0.0 44.0 jit_solution(16979368094971978720)
XLA Ops:
  1.3 1.3 %shard_map.76 = (bf16[512,192]{1,0:T(8,128)(2,1)S(1)}, bf16[512,192]{1,0:T(8,128)(2,1)S(1)}, bf16[192,512]{1,0:T(8,128)(2,1)S(1)}, bf16[304,128]{1,0:T(8,128)(2,...) custom-call(s32[1,1,1]{2,1,0:T(1,128)S(6)} %copy.8.pos_hbm, bf16[192,512]{1,0:T(8,128)(2,1)} %bitcast.24, ...), custom_call_target="tpu_custom_call" | custom-call | tf_op jit(solution)/shard_map/pallas_call | solution.py:26
  2.6 3.0 %collective-permute-start = (bf16[304,128]{1,0:T(8,128)(2,1)S(1)}, bf16[304,128]{1,0:T(8,128)(2,1)S(1)}, u32[]{:S(2)}, u32[]{:S(2)}) collective-permute-start(bf16[304,128]{1,0:T(8,128)(2,1)S(1)} %get-tuple-element.31), channel_id=1, source_target_pairs={{0,8},{8,0},{16,24},{24,16},{1,9},{9,1},{17,25},{25,17},{2,10},{10... | collective-permute-start | bytes 233480 | tf_op jit(solution)/shard_map/ppermute | solution.py:410
  5.6 0.7 %collective-permute-start.1 = (bf16[304,128]{1,0:T(8,128)(2,1)S(1)}, bf16[304,128]{1,0:T(8,128)(2,1)S(1)}, u32[]{:S(2)}, u32[]{:S(2)}) collective-permute-start(bf16[304,128]{1,0:T(8,128)(2,1)S(1)} %get-tuple-element.32), channel_id=1, source_target_pairs={{8,16},{16,8},{9,17},{17,9},{10,18},{18,10},{11,19},{19,11},{12,20... | collective-permute-start | bytes 233480 | tf_op jit(solution)/shard_map/ppermute | solution.py:416
  6.3 1.6 %collective-permute-start.4 = (bf16[192,512]{1,0:T(8,128)(2,1)S(1)}, bf16[192,512]{1,0:T(8,128)(2,1)S(1)}, u32[]{:S(2)}, u32[]{:S(2)}) collective-permute-start(bf16[192,512]{1,0:T(8,128)(2,1)S(1)} %get-tuple-element.47.refs_0_), channel_id=1, source_target_pairs={{0,24},{8,16},{16,8},{24,0},{1,25},{9,17},{17,9},{25,1},{2,26},{10... | collective-permute-start | bytes 589832 | tf_op jit(solution)/shard_map/ppermute | solution.py:410
  7.8 1.7 %shard_map.77 = (bf16[27,192,192]{2,1,0:T(8,128)(2,1)S(1)}, bf16[16,128]{1,0:T(8,128)(2,1)S(1)}) custom-call(bf16[27,192,192]{2,1,0:T(8,128)(2,1)} %bitcast.26), custom_call_target="tpu_custom_call" | custom-call | flops 1000000000 | bytes 3985408 | tf_op jit(solution)/shard_map/pallas_call | solution.py:26
  9.6 0.0 collective-permute-done.xeven_ref
  9.6 0.0 collective-permute-done.1.xodd_ref
  9.6 0.2 shard_map.78
  9.8 0.0 collective-permute-start.2
  9.8 0.7 %collective-permute-start.3 = (bf16[432,128]{1,0:T(8,128)(2,1)S(1)}, bf16[432,128]{1,0:T(8,128)(2,1)S(1)}, u32[]{:S(2)}, u32[]{:S(2)}) collective-permute-start(bf16[432,128]{1,0:T(8,128)(2,1)S(1)} %get-tuple-element.38), channel_id=1, source_target_pairs={{1,2},{3,4},{5,6},{2,1},{4,3},{6,5},{9,10},{11,12},{13,14},{10,9},... | collective-permute-start | bytes 331784 | tf_op jit(solution)/shard_map/ppermute | solution.py:416
  10.5 3.8 %collective-permute-start.5 = (bf16[192,512]{1,0:T(8,128)(2,1)S(1)}, bf16[192,512]{1,0:T(8,128)(2,1)S(1)}, u32[]{:S(2)}, u32[]{:S(2)}) collective-permute-start(bf16[192,512]{1,0:T(8,128)(2,1)S(1)} %get-tuple-element.47.refs_0_), channel_id=1, source_target_pairs={{0,8},{8,0},{16,24},{24,16},{1,9},{9,1},{17,25},{25,17},{2,10},{10... | collective-permute-start | bytes 589832 | tf_op jit(solution)/shard_map/ppermute | solution.py:410
  14.2 2.0 %collective-permute-start.7 = (bf16[192,512]{1,0:T(8,128)(2,1)S(1)}, bf16[192,512]{1,0:T(8,128)(2,1)S(1)}, u32[]{:S(2)}, u32[]{:S(2)}) collective-permute-start(bf16[192,512]{1,0:T(8,128)(2,1)S(1)} %get-tuple-element.47.refs_0_), channel_id=1, source_target_pairs={{0,16},{8,24},{16,0},{24,8},{1,17},{9,25},{17,1},{25,9},{2,18},{10... | collective-permute-start | bytes 589832 | tf_op jit(solution)/shard_map/ppermute | solution.py:410
  16.2 0.0 collective-permute-done.2.yeven_ref
  16.2 0.0 collective-permute-done.3.yodd_ref
  16.2 0.0 collective-permute-done.4.brick_ref.refs_0_
  16.2 0.2 shard_map.79
  16.4 3.0 %shard_map.80 = (bf16[512,192]{1,0:T(8,128)(2,1)S(1)}, bf16[10,80,192]{2,1,0:T(8,128)(2,1)S(1)}, bf16[4,48,896]{2,1,0:T(8,128)(2,1)S(1)}) custom-call(bf16[12,96,192]{2,1,0:T(8,128)(2,1)S(1)} %get-tuple-element.39.even_ref, bf16[12,80,192]{2,1,0:T(8,128)(2,1)S(1)} %get-tuple-element.40.odd_ref, bf16[10,80,192]{2,1,0:T(8,128)(2,1)S(1)} %get-tuple-element.41.cot_ref, ...), custom_call_target="tpu_custom_call" | custom-call | tf_op jit(solution)/shard_map/pallas_call | solution.py:26
  19.5 1.5 %collective-permute-start.9 = (bf16[48,896]{1,0:T(8,128)(2,1)S(1)}, bf16[48,896]{1,0:T(8,128)(2,1)S(1)}, u32[]{:S(2)}, u32[]{:S(2)}) collective-permute-start(bf16[48,896]{1,0:T(8,128)(2,1)S(1)} %get-tuple-element.54), channel_id=1, source_target_pairs={{0,24},{8,16},{16,8},{24,0},{1,25},{9,17},{17,9},{25,1},{2,26},{10... | collective-permute-start | bytes 258056 | tf_op jit(solution)/shard_map/ppermute | solution.py:410
  21.0 2.0 %collective-permute-start.8 = (bf16[48,896]{1,0:T(8,128)(2,1)S(1)}, bf16[48,896]{1,0:T(8,128)(2,1)S(1)}, u32[]{:S(2)}, u32[]{:S(2)}) collective-permute-start(bf16[48,896]{1,0:T(8,128)(2,1)S(1)} %get-tuple-element.55), channel_id=1, source_target_pairs={{0,16},{8,24},{16,0},{24,8},{1,17},{9,25},{17,1},{25,9},{2,18},{10... | collective-permute-start | bytes 258056 | tf_op jit(solution)/shard_map/ppermute | solution.py:410
  23.0 0.1 collective-permute-start.6
  23.1 0.9 %shard_map.82.refs_2_ = f32[9,192,144]{2,1,0:T(8,128)S(1)} custom-call(bf16[192,512]{1,0:T(8,128)(2,1)S(1)} %get-tuple-element.47.refs_0_, bf16[48,896]{1,0:T(8,128)(2,1)S(1)} %get-tuple-element.53.refs_1_), custom_call_target="tpu_custom_call" | custom-call | flops 254803968 | bytes 1277952 | tf_op jit(solution)/shard_map/pallas_call | solution.py:26
  24.0 1.1 %collective-permute-done.9.refs_1_ = bf16[48,896]{1,0:T(8,128)(2,1)S(1)} collective-permute-done((bf16[48,896]{1,0:T(8,128)(2,1)S(1)}, bf16[48,896]{1,0:T(8,128)(2,1)S(1)}, u32[]{:S(2)}, u32[]{:S(2)}) %collective-permute-start.9) | collective-permute-done | bytes 86048 | tf_op jit(solution)/shard_map/ppermute | solution.py:410
  25.0 0.9 %shard_map.83.refs_2_ = f32[9,192,144]{2,1,0:T(8,128)S(1)} custom-call(bf16[192,512]{1,0:T(8,128)(2,1)S(1)} %collective-permute-done.4.brick_ref.refs_0_, bf16[48,896]{1,0:T(8,128)(2,1)S(1)} %collective-permute-done.9.refs_1_, f32[9,192,144]{2,1,0:T(8,128)S(1)} %shard_map.82.refs_2_), custom_call_target="tpu_custom_call" | custom-call | flops 254803968 | bytes 2273280 | tf_op jit(solution)/shard_map/pallas_call | solution.py:26
  25.9 0.0 collective-permute-done.7.refs_0_
  25.9 0.4 collective-permute-done.8.refs_1_
  26.3 0.9 %shard_map.84.refs_2_ = f32[9,192,144]{2,1,0:T(8,128)S(1)} custom-call(bf16[192,512]{1,0:T(8,128)(2,1)S(1)} %collective-permute-done.7.refs_0_, bf16[48,896]{1,0:T(8,128)(2,1)S(1)} %collective-permute-done.8.refs_1_, f32[9,192,144]{2,1,0:T(8,128)S(1)} %shard_map.83.refs_2_), custom_call_target="tpu_custom_call" | custom-call | flops 254803968 | bytes 2273280 | tf_op jit(solution)/shard_map/pallas_call | solution.py:26
  27.2 0.0 copy-start
  27.2 0.0 collective-permute-done.5.refs_0_
  27.2 0.3 collective-permute-done.6.refs_1_
  27.5 1.0 %shard_map.85 = (bf16[4,272,128]{2,1,0:T(8,128)(2,1)S(1)}, f32[4,272,128]{2,1,0:T(8,128)S(1)}) custom-call(bf16[192,512]{1,0:T(8,128)(2,1)S(1)} %collective-permute-done.5.refs_0_, bf16[48,896]{1,0:T(8,128)(2,1)S(1)} %collective-permute-done.6.refs_1_, f32[9,192,144]{2,1,0:T(8,128)S(1)} %shard_map.84.refs_2_), custom_call_target="tpu_custom_call" | custom-call | flops 254803968 | bytes 2113536 | tf_op jit(solution)/shard_map/pallas_call | solution.py:26
  28.5 1.7 %collective-permute-start.10 = (bf16[4,272,128]{2,1,0:T(8,128)(2,1)S(1)}, bf16[4,272,128]{2,1,0:T(8,128)(2,1)S(1)}, u32[]{:S(2)}, u32[]{:S(2)}) collective-permute-start(bf16[4,272,128]{2,1,0:T(8,128)(2,1)S(1)} %get-tuple-element.50), channel_id=1, source_target_pairs={{0,1},{1,0},{2,3},{3,2},{4,5},{5,4},{6,7},{7,6},{8,9},{9,8},{10,11... | collective-permute-start | bytes 835592 | tf_op jit(solution)/shard_map/ppermute | solution.py:410
  30.2 1.2 %collective-permute-done.10.recv_ref = bf16[4,272,128]{2,1,0:T(8,128)(2,1)S(1)} collective-permute-done((bf16[4,272,128]{2,1,0:T(8,128)(2,1)S(1)}, bf16[4,272,128]{2,1,0:T(8,128)(2,1)S(1)}, u32[]{:S(2)}, u32[]{:S(2)}) %collective-permute-start.10) | collective-permute-done | bytes 278560 | tf_op jit(solution)/shard_map/ppermute | solution.py:410
  31.4 0.1 shard_map.86
  31.5 4.5 %collective-permute-start.11 = (bf16[272,128]{1,0:T(8,128)(2,1)S(1)}, bf16[272,128]{1,0:T(8,128)(2,1)S(1)}, u32[]{:S(2)}, u32[]{:S(2)}) collective-permute-start(bf16[272,128]{1,0:T(8,128)(2,1)S(1)} %get-tuple-element.59), channel_id=1, source_target_pairs={{0,6},{1,7},{2,4},{3,5},{4,2},{5,3},{6,0},{7,1},{8,14},{9,15},{10,... | collective-permute-start | bytes 208904 | tf_op jit(solution)/shard_map/ppermute | solution.py:410
  36.1 1.1 %collective-permute-start.12 = (bf16[272,128]{1,0:T(8,128)(2,1)S(1)}, bf16[272,128]{1,0:T(8,128)(2,1)S(1)}, u32[]{:S(2)}, u32[]{:S(2)}) collective-permute-start(bf16[272,128]{1,0:T(8,128)(2,1)S(1)} %get-tuple-element.58), channel_id=1, source_target_pairs={{0,4},{1,5},{2,6},{3,7},{4,0},{5,1},{6,2},{7,3},{8,12},{9,13},{10,... | collective-permute-start | bytes 208904 | tf_op jit(solution)/shard_map/ppermute | solution.py:410
  37.2 0.1 collective-permute-start.13
  37.3 0.0 copy-done
  37.3 2.4 %shard_map.81 = (bf16[192,512]{1,0:T(8,128)(2,1)}, bf16[192,512]{1,0:T(8,128)(2,1)}) custom-call(bf16[10,80,192]{2,1,0:T(8,128)(2,1)S(1)} %get-tuple-element.43.slope_ref, bf16[512,192]{1,0:T(8,128)(2,1)S(1)} %get-tuple-element.44.act_ref, s32[1,512]{1,0:T(1,128)S(1)} %bitcast.22, bf16[27,192,192]{2,1,0:T(8,128)(2,1)S(1)} %get-tuple-element.42.w_ref), custom_call_target="tpu_custom_call" | custom-call | flops 1019215872 | bytes 2889728 | tf_op jit(solution)/shard_map/pallas_call | solution.py:26
  39.7 0.0 collective-permute-done.11.refs_1_
  39.7 3.3 %collective-permute-done.12.refs_2_ = bf16[272,128]{1,0:T(8,128)(2,1)S(1)} collective-permute-done((bf16[272,128]{1,0:T(8,128)(2,1)S(1)}, bf16[272,128]{1,0:T(8,128)(2,1)S(1)}, u32[]{:S(2)}, u32[]{:S(2)}) %collective-permute-start.12) | collective-permute-done | bytes 69664 | tf_op jit(solution)/shard_map/ppermute | solution.py:410
  43.0 0.0 collective-permute-done.13.refs_3_
  43.0 0.9 %shard_map.87 = f32[27,24,48]{2,1,0:T(8,128)} custom-call(f32[272,128]{1,0:T(8,128)S(1)} %get-tuple-element.51.refs_0_, bf16[272,128]{1,0:T(8,128)(2,1)S(1)} %collective-permute-done.11.refs_1_, bf16[272,128]{1,0:T(8,128)(2,1)S(1)} %collective-permute-done.12.refs_2_, bf16[272,128]{1,0:T(8,128)(2,1)S(1)} %collective-permute-done.13.refs_3_), custom_call_target="tpu_custom_call" | custom-call | bytes 472576 | tf_op jit(solution)/shard_map/pallas_call | solution.py:26
  (2 shorter events, 0.0 us)
Async XLA Ops:
  2.6 7.0 %collective-permute-start = (bf16[304,128]{1,0:T(8,128)(2,1)S(1)}, bf16[304,128]{1,0:T(8,128)(2,1)S(1)}, u32[]{:S(2)}, u32[]{:S(2)}) collective-permute-start(bf16[304,128]{1,0:T(8,128)(2,1)S(1)} %get-tuple-element.31), channel_id=1, source_target_pairs={{0,8},{8,0},{16,24},{24,16},{1,9},{9,1},{17,25},{25,17},{2,10},{10... | collective-permute-start | bytes 233480 | tf_op jit(solution)/shard_map/ppermute | solution.py:410
  5.6 4.0 %collective-permute-start.1 = (bf16[304,128]{1,0:T(8,128)(2,1)S(1)}, bf16[304,128]{1,0:T(8,128)(2,1)S(1)}, u32[]{:S(2)}, u32[]{:S(2)}) collective-permute-start(bf16[304,128]{1,0:T(8,128)(2,1)S(1)} %get-tuple-element.32), channel_id=1, source_target_pairs={{8,16},{16,8},{9,17},{17,9},{10,18},{18,10},{11,19},{19,11},{12,20... | collective-permute-start | bytes 233480 | tf_op jit(solution)/shard_map/ppermute | solution.py:416
  6.3 9.9 %collective-permute-start.4 = (bf16[192,512]{1,0:T(8,128)(2,1)S(1)}, bf16[192,512]{1,0:T(8,128)(2,1)S(1)}, u32[]{:S(2)}, u32[]{:S(2)}) collective-permute-start(bf16[192,512]{1,0:T(8,128)(2,1)S(1)} %get-tuple-element.47.refs_0_), channel_id=1, source_target_pairs={{0,24},{8,16},{16,8},{24,0},{1,25},{9,17},{17,9},{25,1},{2,26},{10... | collective-permute-start | bytes 589832 | tf_op jit(solution)/shard_map/ppermute | solution.py:410
  9.8 6.5 %collective-permute-start.2 = (bf16[432,128]{1,0:T(8,128)(2,1)S(1)}, bf16[432,128]{1,0:T(8,128)(2,1)S(1)}, u32[]{:S(2)}, u32[]{:S(2)}) collective-permute-start(bf16[432,128]{1,0:T(8,128)(2,1)S(1)} %get-tuple-element.37), channel_id=1, source_target_pairs={{0,1},{1,0},{2,3},{3,2},{4,5},{5,4},{6,7},{7,6},{8,9},{9,8},{10,11... | collective-permute-start | bytes 331784 | tf_op jit(solution)/shard_map/ppermute | solution.py:410
  9.8 6.4 %collective-permute-start.3 = (bf16[432,128]{1,0:T(8,128)(2,1)S(1)}, bf16[432,128]{1,0:T(8,128)(2,1)S(1)}, u32[]{:S(2)}, u32[]{:S(2)}) collective-permute-start(bf16[432,128]{1,0:T(8,128)(2,1)S(1)} %get-tuple-element.38), channel_id=1, source_target_pairs={{1,2},{3,4},{5,6},{2,1},{4,3},{6,5},{9,10},{11,12},{13,14},{10,9},... | collective-permute-start | bytes 331784 | tf_op jit(solution)/shard_map/ppermute | solution.py:416
  10.5 16.8 %collective-permute-start.5 = (bf16[192,512]{1,0:T(8,128)(2,1)S(1)}, bf16[192,512]{1,0:T(8,128)(2,1)S(1)}, u32[]{:S(2)}, u32[]{:S(2)}) collective-permute-start(bf16[192,512]{1,0:T(8,128)(2,1)S(1)} %get-tuple-element.47.refs_0_), channel_id=1, source_target_pairs={{0,8},{8,0},{16,24},{24,16},{1,9},{9,1},{17,25},{25,17},{2,10},{10... | collective-permute-start | bytes 589832 | tf_op jit(solution)/shard_map/ppermute | solution.py:410
  14.2 11.7 %collective-permute-start.7 = (bf16[192,512]{1,0:T(8,128)(2,1)S(1)}, bf16[192,512]{1,0:T(8,128)(2,1)S(1)}, u32[]{:S(2)}, u32[]{:S(2)}) collective-permute-start(bf16[192,512]{1,0:T(8,128)(2,1)S(1)} %get-tuple-element.47.refs_0_), channel_id=1, source_target_pairs={{0,16},{8,24},{16,0},{24,8},{1,17},{9,25},{17,1},{25,9},{2,18},{10... | collective-permute-start | bytes 589832 | tf_op jit(solution)/shard_map/ppermute | solution.py:410
  19.5 5.5 %collective-permute-start.9 = (bf16[48,896]{1,0:T(8,128)(2,1)S(1)}, bf16[48,896]{1,0:T(8,128)(2,1)S(1)}, u32[]{:S(2)}, u32[]{:S(2)}) collective-permute-start(bf16[48,896]{1,0:T(8,128)(2,1)S(1)} %get-tuple-element.54), channel_id=1, source_target_pairs={{0,24},{8,16},{16,8},{24,0},{1,25},{9,17},{17,9},{25,1},{2,26},{10... | collective-permute-start | bytes 258056 | tf_op jit(solution)/shard_map/ppermute | solution.py:410
  21.0 5.3 %collective-permute-start.8 = (bf16[48,896]{1,0:T(8,128)(2,1)S(1)}, bf16[48,896]{1,0:T(8,128)(2,1)S(1)}, u32[]{:S(2)}, u32[]{:S(2)}) collective-permute-start(bf16[48,896]{1,0:T(8,128)(2,1)S(1)} %get-tuple-element.55), channel_id=1, source_target_pairs={{0,16},{8,24},{16,0},{24,8},{1,17},{9,25},{17,1},{25,9},{2,18},{10... | collective-permute-start | bytes 258056 | tf_op jit(solution)/shard_map/ppermute | solution.py:410
  23.0 4.5 %collective-permute-start.6 = (bf16[48,896]{1,0:T(8,128)(2,1)S(1)}, bf16[48,896]{1,0:T(8,128)(2,1)S(1)}, u32[]{:S(2)}, u32[]{:S(2)}) collective-permute-start(bf16[48,896]{1,0:T(8,128)(2,1)S(1)} %get-tuple-element.56), channel_id=1, source_target_pairs={{0,8},{8,0},{16,24},{24,16},{1,9},{9,1},{17,25},{25,17},{2,10},{10... | collective-permute-start | bytes 258056 | tf_op jit(solution)/shard_map/ppermute | solution.py:410
  27.2 10.1 %copy-start = (s32[1,1,1,512]{3,2,1,0:T(1,128)S(1)}, s32[1,1,1,512]{3,2,1,0:T(1,128)}, u32[]{:S(2)}) copy-start(s32[1,1,1,512]{3,2,1,0:T(1,128)} %param.6) | copy-start | bytes 6148
  28.5 2.9 %collective-permute-start.10 = (bf16[4,272,128]{2,1,0:T(8,128)(2,1)S(1)}, bf16[4,272,128]{2,1,0:T(8,128)(2,1)S(1)}, u32[]{:S(2)}, u32[]{:S(2)}) collective-permute-start(bf16[4,272,128]{2,1,0:T(8,128)(2,1)S(1)} %get-tuple-element.50), channel_id=1, source_target_pairs={{0,1},{1,0},{2,3},{3,2},{4,5},{5,4},{6,7},{7,6},{8,9},{9,8},{10,11... | collective-permute-start | bytes 835592 | tf_op jit(solution)/shard_map/ppermute | solution.py:410
  31.5 8.2 %collective-permute-start.11 = (bf16[272,128]{1,0:T(8,128)(2,1)S(1)}, bf16[272,128]{1,0:T(8,128)(2,1)S(1)}, u32[]{:S(2)}, u32[]{:S(2)}) collective-permute-start(bf16[272,128]{1,0:T(8,128)(2,1)S(1)} %get-tuple-element.59), channel_id=1, source_target_pairs={{0,6},{1,7},{2,4},{3,5},{4,2},{5,3},{6,0},{7,1},{8,14},{9,15},{10,... | collective-permute-start | bytes 208904 | tf_op jit(solution)/shard_map/ppermute | solution.py:410
  36.1 7.0 %collective-permute-start.12 = (bf16[272,128]{1,0:T(8,128)(2,1)S(1)}, bf16[272,128]{1,0:T(8,128)(2,1)S(1)}, u32[]{:S(2)}, u32[]{:S(2)}) collective-permute-start(bf16[272,128]{1,0:T(8,128)(2,1)S(1)} %get-tuple-element.58), channel_id=1, source_target_pairs={{0,4},{1,5},{2,6},{3,7},{4,0},{5,1},{6,2},{7,3},{8,12},{9,13},{10,... | collective-permute-start | bytes 208904 | tf_op jit(solution)/shard_map/ppermute | solution.py:410
  37.2 5.8 %collective-permute-start.13 = (bf16[272,128]{1,0:T(8,128)(2,1)S(1)}, bf16[272,128]{1,0:T(8,128)(2,1)S(1)}, u32[]{:S(2)}, u32[]{:S(2)}) collective-permute-start(bf16[272,128]{1,0:T(8,128)(2,1)S(1)} %get-tuple-element.57), channel_id=1, source_target_pairs={{0,2},{1,3},{2,0},{3,1},{4,6},{5,7},{6,4},{7,5},{8,10},{9,11},{10,... | collective-permute-start | bytes 208904 | tf_op jit(solution)/shard_map/ppermute | solution.py:410

commit v5 on v4

--- a/solution.py
+++ b/solution.py
@@ -184,7 +184,7 @@
     return xm, cot
 
 
-def window_body(spot_ref, xm_ref, cm_ref, xeven_ref, xodd_ref, yeven_ref, yodd_ref, brick_ref, even_ref, odd_ref, cot_ref):
+def window_body(spot_ref, xm_ref, cm_ref, xeven_ref, xodd_ref, yeven_ref, yodd_ref, even_ref, odd_ref, cot_ref):
     px, py = spot(spot_ref)
     channels = xm_ref.shape[1]
     f = lambda v: v.astype(F32)
@@ -241,8 +241,9 @@
     done_ref[...] = jnp.zeros_like(done_ref)
 
 
-def forward_body(parts, even_ref, odd_ref, cot_ref, w_ref, act_ref, slope_ref, rows_ref, wide_ref):
+def forward_body(parts, even_ref, odd_ref, cot_ref, w_ref, act_ref, slope_ref, *refs):
     channels = even_ref.shape[2]
+    rows_refs, wide_ref = refs[:-1], refs[-1]
     me = lax.axis_index("gx")
     slots = 5
 
@@ -279,8 +280,15 @@
     slope = slope_ref[...].reshape(800, channels)
     lines = lax.dot_general(pick, slope, NT, preferred_element_type=F32).astype(BF)
     for k in range(parts):
-        rows_ref[k, :, 0:800] = lines[block * k : block * (k + 1)]
-        rows_ref[k, :, 800:] = jnp.zeros((block, WIDE - 800), BF)
+        rows_refs[k][:, 0:800] = lines[block * k : block * (k + 1)]
+        rows_refs[k][:, 800:] = jnp.zeros((block, WIDE - 800), BF)
+
+
+def window_forward_body(parts, *refs):
+    halo, w_ref, outs, scratch = refs[:7], refs[7], refs[9:-4], refs[-4:]
+    windows, wide_ref = scratch[:3], scratch[3]
+    window_body(*halo, *windows)
+    forward_body(parts, *windows, w_ref, *outs, wide_ref)
 
 
 def backward_body(slope_ref, act_ref, occ_ref, w_ref, out_ref, grad_ref):
@@ -333,8 +341,8 @@
     g = line_ref[...].astype(F32)
     back = jnp.where(place < BE - 1, pltpu.roll(g, WIDE - 1, 1), 0.0)
     ahead = jnp.where(place > 0, pltpu.roll(g, 1, 1), 0.0)
-    columns = jnp.concatenate([back, g, ahead], axis=0).T[0:800].reshape(10, 80, width)
-    window, middle = columns.astype(BF), columns[:, 8:72].astype(BF)
+    columns = jnp.concatenate([back, g, ahead], axis=0).astype(BF).T[0:800].reshape(10, 80, width)
+    window, middle = columns, columns.astype(F32)[:, 8:72].astype(BF)
     left = brick_ref[...]
     full, rest, per, slots = packing(width)
     leftover = []
@@ -378,12 +386,12 @@
             out[chip] = jnp.concatenate([piece] + pad, axis=0).astype(out.dtype)
 
 
-def pair_body(chips, keep_ref, recv_ref, own_ref, send_ref):
+def pair_body(chips, keep_ref, recv_ref, own_ref, *send_refs):
     me = lax.axis_index("gy") >> 1
     own_ref[...] = keep_ref[me] + recv_ref[me].astype(F32)
     for k in range(1, chips):
         it = lax.bitwise_xor(me, jnp.int32(k))
-        send_ref[k - 1] = (keep_ref[it] + recv_ref[it].astype(F32)).astype(BF)
+        send_refs[k - 1][...] = (keep_ref[it] + recv_ref[it].astype(F32)).astype(BF)
 
 
 def last_body(slots, width, scale, *refs):
@@ -461,18 +469,17 @@
     for k in reversed(range(1, parts)):
         if k != first:
             bricks[k] = xor_step(again, "gx", k)
-    even, odd, wide_cot = call(
-        window_body,
-        [shape((12, 96, channels), BF), shape((12, 80, channels), BF), shape((10, 80, channels), BF)],
-        [place, xm, cm, xeven, xodd, yeven, yodd, bricks[first]],
-        short=True,
-    )
     flops = 2 * VOX * 27 * channels * channels
-    act, slope, lines = call(
-        functools.partial(forward_body, parts),
-        [brick, shape((10, 80, channels), BF), shape((parts, block, WIDE), BF)],
-        [even, odd, wide_cot, taps],
-        scratch=[pltpu.VMEM((10, 80, channels), F32)],
+    act, slope, *lines = call(
+        functools.partial(window_forward_body, parts),
+        [brick, shape((10, 80, channels), BF), *[shape((block, WIDE), BF)] * parts],
+        [place, xm, cm, xeven, xodd, yeven, yodd, taps, bricks[first]],
+        scratch=[
+            pltpu.VMEM((12, 96, channels), BF),
+            pltpu.VMEM((12, 80, channels), BF),
+            pltpu.VMEM((10, 80, channels), BF),
+            pltpu.VMEM((10, 80, channels), F32),
+        ],
         short=True,
     )
     others = {k: xor_step(lines[k], "gx", k) for k in reversed(range(1, parts))}
@@ -509,9 +516,9 @@
         keep = lax.dynamic_index_in_dim(store, core, 0, False)
         send = lax.dynamic_index_in_dim(store, 1 - core, 0, False).astype(BF)
     recv = xor_step(send, "gy", 1)
-    own, sends = call(
+    own, *sends = call(
         functools.partial(pair_body, chips),
-        [shape((count, 128), F32), shape((chips - 1, count, 128), BF)],
+        [shape((count, 128), F32), *[shape((count, 128), BF)] * (chips - 1)],
         [keep, recv],
     )
     came = [xor_step(sends[k - 1], "gy", 2 * k) for k in reversed(range(1, chips))]

time: 44.2 us -> 44.1 us (level)
    pallas_call x12 -> x11, Pallas kernels: 13.6 us -> 13.4 us  [call(): pl.pallas_call(body, out_shape=tuple(outs), in_specs=specs, out_specs=tup...]
where the time goes in v5:
time: 44.1 us; the launch traced here: 43.9 us
  starting transfers between devices  22.6 us (51%)
  Pallas kernels  13.4 us (30%)
  waiting for transfers between devices  6.43 us (15%)
  between operations  1.41 us (3%)
    ppermute x12, starting transfers between devices, xor_step(): return lax.ppermute(value, axis, [(i, i ^ step) for i in range(count)])  21.3 us
    pallas_call x11, Pallas kernels, call(): pl.pallas_call(body, out_shape=tuple(outs), in_specs=specs, out_specs=tup...  13.4 us
    ppermute x12, waiting for transfers between devices, xor_step(): return lax.ppermute(value, axis, [(i, i ^ step) for i in range(count)])  6.42 us
    ppermute x2, starting transfers between devices, swap_pairs(): odd = lax.ppermute(odd, axis, later + [(j, i) for i, j in later])  1.32 us
  transfers between devices with their start and end apart: 14, of which 5 were waited for; matrix products, arithmetic and copies ran while one was open for 0% of the time, Pallas kernels for 23%

profile of v5, /device:TPU:0, one launch (start us, length us, event | category | flops | bytes accessed | tf_op | source)
XLA Modules:
  0.0 43.9 jit_solution(10198676584977734249)
XLA Ops:
  1.3 1.3 %shard_map.76 = (bf16[512,192]{1,0:T(8,128)(2,1)S(1)}, bf16[512,192]{1,0:T(8,128)(2,1)S(1)}, bf16[192,512]{1,0:T(8,128)(2,1)S(1)}, bf16[304,128]{1,0:T(8,128)(2,...) custom-call(s32[1,1,1]{2,1,0:T(1,128)S(6)} %copy.8.pos_hbm, bf16[192,512]{1,0:T(8,128)(2,1)} %bitcast.10, ...), custom_call_target="tpu_custom_call" | custom-call | tf_op jit(solution)/shard_map/pallas_call | solution.py:26
  2.6 3.0 %collective-permute-start = (bf16[304,128]{1,0:T(8,128)(2,1)S(1)}, bf16[304,128]{1,0:T(8,128)(2,1)S(1)}, u32[]{:S(2)}, u32[]{:S(2)}) collective-permute-start(bf16[304,128]{1,0:T(8,128)(2,1)S(1)} %get-tuple-element.33), channel_id=1, source_target_pairs={{0,8},{8,0},{16,24},{24,16},{1,9},{9,1},{17,25},{25,17},{2,10},{10... | collective-permute-start | bytes 233480 | tf_op jit(solution)/shard_map/ppermute | solution.py:418
  5.6 0.7 %collective-permute-start.1 = (bf16[304,128]{1,0:T(8,128)(2,1)S(1)}, bf16[304,128]{1,0:T(8,128)(2,1)S(1)}, u32[]{:S(2)}, u32[]{:S(2)}) collective-permute-start(bf16[304,128]{1,0:T(8,128)(2,1)S(1)} %get-tuple-element.34), channel_id=1, source_target_pairs={{8,16},{16,8},{9,17},{17,9},{10,18},{18,10},{11,19},{19,11},{12,20... | collective-permute-start | bytes 233480 | tf_op jit(solution)/shard_map/ppermute | solution.py:424
  6.3 1.6 %collective-permute-start.4 = (bf16[192,512]{1,0:T(8,128)(2,1)S(1)}, bf16[192,512]{1,0:T(8,128)(2,1)S(1)}, u32[]{:S(2)}, u32[]{:S(2)}) collective-permute-start(bf16[192,512]{1,0:T(8,128)(2,1)S(1)} %get-tuple-element.46.refs_0_), channel_id=1, source_target_pairs={{0,24},{8,16},{16,8},{24,0},{1,25},{9,17},{17,9},{25,1},{2,26},{10... | collective-permute-start | bytes 589832 | tf_op jit(solution)/shard_map/ppermute | solution.py:418
  7.8 1.7 %shard_map.77 = (bf16[27,192,192]{2,1,0:T(8,128)(2,1)S(1)}, bf16[16,128]{1,0:T(8,128)(2,1)S(1)}) custom-call(bf16[27,192,192]{2,1,0:T(8,128)(2,1)} %bitcast.12), custom_call_target="tpu_custom_call" | custom-call | flops 1000000000 | bytes 3985408 | tf_op jit(solution)/shard_map/pallas_call | solution.py:26
  9.6 0.0 collective-permute-done.xeven_ref.refs_3_
  9.6 0.0 collective-permute-done.1.xodd_ref.refs_4_
  9.6 0.2 shard_map.78
  9.8 0.0 collective-permute-start.2
  9.8 0.7 %collective-permute-start.3 = (bf16[432,128]{1,0:T(8,128)(2,1)S(1)}, bf16[432,128]{1,0:T(8,128)(2,1)S(1)}, u32[]{:S(2)}, u32[]{:S(2)}) collective-permute-start(bf16[432,128]{1,0:T(8,128)(2,1)S(1)} %get-tuple-element.40), channel_id=1, source_target_pairs={{1,2},{3,4},{5,6},{2,1},{4,3},{6,5},{9,10},{11,12},{13,14},{10,9},... | collective-permute-start | bytes 331784 | tf_op jit(solution)/shard_map/ppermute | solution.py:424
  10.5 5.7 %collective-permute-start.7 = (bf16[192,512]{1,0:T(8,128)(2,1)S(1)}, bf16[192,512]{1,0:T(8,128)(2,1)S(1)}, u32[]{:S(2)}, u32[]{:S(2)}) collective-permute-start(bf16[192,512]{1,0:T(8,128)(2,1)S(1)} %get-tuple-element.46.refs_0_), channel_id=1, source_target_pairs={{0,16},{8,24},{16,0},{24,8},{1,17},{9,25},{17,1},{25,9},{2,18},{10... | collective-permute-start | bytes 589832 | tf_op jit(solution)/shard_map/ppermute | solution.py:418
  16.1 0.0 collective-permute-start.5
  16.1 0.0 collective-permute-done.2.refs_5_
  16.1 0.0 collective-permute-done.3.refs_6_
  16.2 0.0 collective-permute-done.4.refs_8_.refs_0_
  16.2 3.2 %shard_map.79 = (bf16[512,192]{1,0:T(8,128)(2,1)S(1)}, bf16[10,80,192]{2,1,0:T(8,128)(2,1)S(1)}, bf16[48,896]{1,0:T(8,128)(2,1)S(1)}, bf16[48,896]{1,0:T(8,128)(...) custom-call(bf16[32,192]{1,0:T(8,128)(2,1)S(1)} %get-tuple-element.30.spot_ref.refs_0_, ...), custom_call_target="tpu_custom_call" | custom-call | tf_op jit(solution)/shard_map/pallas_call | solution.py:26
  19.4 1.6 %collective-permute-start.9 = (bf16[48,896]{1,0:T(8,128)(2,1)S(1)}, bf16[48,896]{1,0:T(8,128)(2,1)S(1)}, u32[]{:S(2)}, u32[]{:S(2)}) collective-permute-start(bf16[48,896]{1,0:T(8,128)(2,1)S(1)} %get-tuple-element.49), channel_id=1, source_target_pairs={{0,24},{8,16},{16,8},{24,0},{1,25},{9,17},{17,9},{25,1},{2,26},{10... | collective-permute-start | bytes 258056 | tf_op jit(solution)/shard_map/ppermute | solution.py:418
  21.0 1.9 %collective-permute-start.8 = (bf16[48,896]{1,0:T(8,128)(2,1)S(1)}, bf16[48,896]{1,0:T(8,128)(2,1)S(1)}, u32[]{:S(2)}, u32[]{:S(2)}) collective-permute-start(bf16[48,896]{1,0:T(8,128)(2,1)S(1)} %get-tuple-element.48), channel_id=1, source_target_pairs={{0,16},{8,24},{16,0},{24,8},{1,17},{9,25},{17,1},{25,9},{2,18},{10... | collective-permute-start | bytes 258056 | tf_op jit(solution)/shard_map/ppermute | solution.py:418
  22.9 0.0 collective-permute-start.6
  22.9 0.8 %shard_map.81.refs_2_ = f32[9,192,144]{2,1,0:T(8,128)S(1)} custom-call(bf16[192,512]{1,0:T(8,128)(2,1)S(1)} %get-tuple-element.46.refs_0_, bf16[48,896]{1,0:T(8,128)(2,1)S(1)} %get-tuple-element.50.refs_1_), custom_call_target="tpu_custom_call" | custom-call | flops 254803968 | bytes 1277952 | tf_op jit(solution)/shard_map/pallas_call | solution.py:26
  23.8 1.1 %collective-permute-done.9.refs_1_ = bf16[48,896]{1,0:T(8,128)(2,1)S(1)} collective-permute-done((bf16[48,896]{1,0:T(8,128)(2,1)S(1)}, bf16[48,896]{1,0:T(8,128)(2,1)S(1)}, u32[]{:S(2)}, u32[]{:S(2)}) %collective-permute-start.9) | collective-permute-done | bytes 86048 | tf_op jit(solution)/shard_map/ppermute | solution.py:418
  24.8 0.8 %shard_map.82.refs_2_ = f32[9,192,144]{2,1,0:T(8,128)S(1)} custom-call(bf16[192,512]{1,0:T(8,128)(2,1)S(1)} %collective-permute-done.4.refs_8_.refs_0_, bf16[48,896]{1,0:T(8,128)(2,1)S(1)} %collective-permute-done.9.refs_1_, f32[9,192,144]{2,1,0:T(8,128)S(1)} %shard_map.81.refs_2_), custom_call_target="tpu_custom_call" | custom-call | flops 254803968 | bytes 2273280 | tf_op jit(solution)/shard_map/pallas_call | solution.py:26
  25.7 0.0 collective-permute-done.7.refs_0_
  25.7 0.5 %collective-permute-done.8.refs_1_ = bf16[48,896]{1,0:T(8,128)(2,1)S(1)} collective-permute-done((bf16[48,896]{1,0:T(8,128)(2,1)S(1)}, bf16[48,896]{1,0:T(8,128)(2,1)S(1)}, u32[]{:S(2)}, u32[]{:S(2)}) %collective-permute-start.8) | collective-permute-done | bytes 86048 | tf_op jit(solution)/shard_map/ppermute | solution.py:418
  26.2 0.8 %shard_map.83.refs_2_ = f32[9,192,144]{2,1,0:T(8,128)S(1)} custom-call(bf16[192,512]{1,0:T(8,128)(2,1)S(1)} %collective-permute-done.7.refs_0_, bf16[48,896]{1,0:T(8,128)(2,1)S(1)} %collective-permute-done.8.refs_1_, f32[9,192,144]{2,1,0:T(8,128)S(1)} %shard_map.82.refs_2_), custom_call_target="tpu_custom_call" | custom-call | flops 254803968 | bytes 2273280 | tf_op jit(solution)/shard_map/pallas_call | solution.py:26
  27.1 0.0 copy-start
  27.1 0.0 collective-permute-done.5.refs_0_
  27.1 0.3 collective-permute-done.6.refs_1_
  27.4 1.0 %shard_map.84 = (bf16[4,272,128]{2,1,0:T(8,128)(2,1)S(1)}, f32[4,272,128]{2,1,0:T(8,128)S(1)}) custom-call(bf16[192,512]{1,0:T(8,128)(2,1)S(1)} %collective-permute-done.5.refs_0_, bf16[48,896]{1,0:T(8,128)(2,1)S(1)} %collective-permute-done.6.refs_1_, f32[9,192,144]{2,1,0:T(8,128)S(1)} %shard_map.83.refs_2_), custom_call_target="tpu_custom_call" | custom-call | flops 254803968 | bytes 2113536 | tf_op jit(solution)/shard_map/pallas_call | solution.py:26
  28.5 1.7 %collective-permute-start.10 = (bf16[4,272,128]{2,1,0:T(8,128)(2,1)S(1)}, bf16[4,272,128]{2,1,0:T(8,128)(2,1)S(1)}, u32[]{:S(2)}, u32[]{:S(2)}) collective-permute-start(bf16[4,272,128]{2,1,0:T(8,128)(2,1)S(1)} %get-tuple-element.52), channel_id=1, source_target_pairs={{0,1},{1,0},{2,3},{3,2},{4,5},{5,4},{6,7},{7,6},{8,9},{9,8},{10,11... | collective-permute-start | bytes 835592 | tf_op jit(solution)/shard_map/ppermute | solution.py:418
  30.2 1.2 %collective-permute-done.10.recv_ref = bf16[4,272,128]{2,1,0:T(8,128)(2,1)S(1)} collective-permute-done((bf16[4,272,128]{2,1,0:T(8,128)(2,1)S(1)}, bf16[4,272,128]{2,1,0:T(8,128)(2,1)S(1)}, u32[]{:S(2)}, u32[]{:S(2)}) %collective-permute-start.10) | collective-permute-done | bytes 278560 | tf_op jit(solution)/shard_map/ppermute | solution.py:418
  31.3 0.1 shard_map.85
  31.4 4.5 %collective-permute-start.11 = (bf16[272,128]{1,0:T(8,128)(2,1)S(1)}, bf16[272,128]{1,0:T(8,128)(2,1)S(1)}, u32[]{:S(2)}, u32[]{:S(2)}) collective-permute-start(bf16[272,128]{1,0:T(8,128)(2,1)S(1)} %get-tuple-element.54), channel_id=1, source_target_pairs={{0,6},{1,7},{2,4},{3,5},{4,2},{5,3},{6,0},{7,1},{8,14},{9,15},{10,... | collective-permute-start | bytes 208904 | tf_op jit(solution)/shard_map/ppermute | solution.py:418
  35.9 1.1 %collective-permute-start.12 = (bf16[272,128]{1,0:T(8,128)(2,1)S(1)}, bf16[272,128]{1,0:T(8,128)(2,1)S(1)}, u32[]{:S(2)}, u32[]{:S(2)}) collective-permute-start(bf16[272,128]{1,0:T(8,128)(2,1)S(1)} %get-tuple-element.55), channel_id=1, source_target_pairs={{0,4},{1,5},{2,6},{3,7},{4,0},{5,1},{6,2},{7,3},{8,12},{9,13},{10,... | collective-permute-start | bytes 208904 | tf_op jit(solution)/shard_map/ppermute | solution.py:418
  37.1 0.1 collective-permute-start.13
  37.2 0.0 copy-done
  37.2 2.4 %shard_map.80 = (bf16[192,512]{1,0:T(8,128)(2,1)}, bf16[192,512]{1,0:T(8,128)(2,1)}) custom-call(bf16[10,80,192]{2,1,0:T(8,128)(2,1)S(1)} %get-tuple-element.42.slope_ref, bf16[512,192]{1,0:T(8,128)(2,1)S(1)} %get-tuple-element.43.act_ref, s32[1,512]{1,0:T(1,128)S(1)} %bitcast.8, bf16[27,192,192]{2,1,0:T(8,128)(2,1)S(1)} %get-tuple-element.41.refs_7_.w_ref), custom_call_target="tpu_custom_call" | custom-call | flops 1019215872 | bytes 2889728 | tf_op jit(solution)/shard_map/pallas_call | solution.py:26
  39.6 0.0 collective-permute-done.11.refs_1_
  39.6 3.3 %collective-permute-done.12.refs_2_ = bf16[272,128]{1,0:T(8,128)(2,1)S(1)} collective-permute-done((bf16[272,128]{1,0:T(8,128)(2,1)S(1)}, bf16[272,128]{1,0:T(8,128)(2,1)S(1)}, u32[]{:S(2)}, u32[]{:S(2)}) %collective-permute-start.12) | collective-permute-done | bytes 69664 | tf_op jit(solution)/shard_map/ppermute | solution.py:418
  42.9 0.0 collective-permute-done.13.refs_3_
  42.9 0.9 %shard_map.86 = f32[27,24,48]{2,1,0:T(8,128)} custom-call(f32[272,128]{1,0:T(8,128)S(1)} %get-tuple-element.53.refs_0_, bf16[272,128]{1,0:T(8,128)(2,1)S(1)} %collective-permute-done.11.refs_1_, bf16[272,128]{1,0:T(8,128)(2,1)S(1)} %collective-permute-done.12.refs_2_, bf16[272,128]{1,0:T(8,128)(2,1)S(1)} %collective-permute-done.13.refs_3_), custom_call_target="tpu_custom_call" | custom-call | bytes 472576 | tf_op jit(solution)/shard_map/pallas_call | solution.py:26
Async XLA Ops:
  2.6 7.0 %collective-permute-start = (bf16[304,128]{1,0:T(8,128)(2,1)S(1)}, bf16[304,128]{1,0:T(8,128)(2,1)S(1)}, u32[]{:S(2)}, u32[]{:S(2)}) collective-permute-start(bf16[304,128]{1,0:T(8,128)(2,1)S(1)} %get-tuple-element.33), channel_id=1, source_target_pairs={{0,8},{8,0},{16,24},{24,16},{1,9},{9,1},{17,25},{25,17},{2,10},{10... | collective-permute-start | bytes 233480 | tf_op jit(solution)/shard_map/ppermute | solution.py:418
  5.6 4.0 %collective-permute-start.1 = (bf16[304,128]{1,0:T(8,128)(2,1)S(1)}, bf16[304,128]{1,0:T(8,128)(2,1)S(1)}, u32[]{:S(2)}, u32[]{:S(2)}) collective-permute-start(bf16[304,128]{1,0:T(8,128)(2,1)S(1)} %get-tuple-element.34), channel_id=1, source_target_pairs={{8,16},{16,8},{9,17},{17,9},{10,18},{18,10},{11,19},{19,11},{12,20... | collective-permute-start | bytes 233480 | tf_op jit(solution)/shard_map/ppermute | solution.py:424
  6.3 9.9 %collective-permute-start.4 = (bf16[192,512]{1,0:T(8,128)(2,1)S(1)}, bf16[192,512]{1,0:T(8,128)(2,1)S(1)}, u32[]{:S(2)}, u32[]{:S(2)}) collective-permute-start(bf16[192,512]{1,0:T(8,128)(2,1)S(1)} %get-tuple-element.46.refs_0_), channel_id=1, source_target_pairs={{0,24},{8,16},{16,8},{24,0},{1,25},{9,17},{17,9},{25,1},{2,26},{10... | collective-permute-start | bytes 589832 | tf_op jit(solution)/shard_map/ppermute | solution.py:418
  9.8 6.4 %collective-permute-start.2 = (bf16[432,128]{1,0:T(8,128)(2,1)S(1)}, bf16[432,128]{1,0:T(8,128)(2,1)S(1)}, u32[]{:S(2)}, u32[]{:S(2)}) collective-permute-start(bf16[432,128]{1,0:T(8,128)(2,1)S(1)} %get-tuple-element.39), channel_id=1, source_target_pairs={{0,1},{1,0},{2,3},{3,2},{4,5},{5,4},{6,7},{7,6},{8,9},{9,8},{10,11... | collective-permute-start | bytes 331784 | tf_op jit(solution)/shard_map/ppermute | solution.py:418
  9.8 6.4 %collective-permute-start.3 = (bf16[432,128]{1,0:T(8,128)(2,1)S(1)}, bf16[432,128]{1,0:T(8,128)(2,1)S(1)}, u32[]{:S(2)}, u32[]{:S(2)}) collective-permute-start(bf16[432,128]{1,0:T(8,128)(2,1)S(1)} %get-tuple-element.40), channel_id=1, source_target_pairs={{1,2},{3,4},{5,6},{2,1},{4,3},{6,5},{9,10},{11,12},{13,14},{10,9},... | collective-permute-start | bytes 331784 | tf_op jit(solution)/shard_map/ppermute | solution.py:424
  10.5 15.2 %collective-permute-start.7 = (bf16[192,512]{1,0:T(8,128)(2,1)S(1)}, bf16[192,512]{1,0:T(8,128)(2,1)S(1)}, u32[]{:S(2)}, u32[]{:S(2)}) collective-permute-start(bf16[192,512]{1,0:T(8,128)(2,1)S(1)} %get-tuple-element.46.refs_0_), channel_id=1, source_target_pairs={{0,16},{8,24},{16,0},{24,8},{1,17},{9,25},{17,1},{25,9},{2,18},{10... | collective-permute-start | bytes 589832 | tf_op jit(solution)/shard_map/ppermute | solution.py:418
  16.1 11.0 %collective-permute-start.5 = (bf16[192,512]{1,0:T(8,128)(2,1)S(1)}, bf16[192,512]{1,0:T(8,128)(2,1)S(1)}, u32[]{:S(2)}, u32[]{:S(2)}) collective-permute-start(bf16[192,512]{1,0:T(8,128)(2,1)S(1)} %get-tuple-element.46.refs_0_), channel_id=1, source_target_pairs={{0,8},{8,0},{16,24},{24,16},{1,9},{9,1},{17,25},{25,17},{2,10},{10... | collective-permute-start | bytes 589832 | tf_op jit(solution)/shard_map/ppermute | solution.py:418
  19.4 5.5 %collective-permute-start.9 = (bf16[48,896]{1,0:T(8,128)(2,1)S(1)}, bf16[48,896]{1,0:T(8,128)(2,1)S(1)}, u32[]{:S(2)}, u32[]{:S(2)}) collective-permute-start(bf16[48,896]{1,0:T(8,128)(2,1)S(1)} %get-tuple-element.49), channel_id=1, source_target_pairs={{0,24},{8,16},{16,8},{24,0},{1,25},{9,17},{17,9},{25,1},{2,26},{10... | collective-permute-start | bytes 258056 | tf_op jit(solution)/shard_map/ppermute | solution.py:418
  21.0 5.3 %collective-permute-start.8 = (bf16[48,896]{1,0:T(8,128)(2,1)S(1)}, bf16[48,896]{1,0:T(8,128)(2,1)S(1)}, u32[]{:S(2)}, u32[]{:S(2)}) collective-permute-start(bf16[48,896]{1,0:T(8,128)(2,1)S(1)} %get-tuple-element.48), channel_id=1, source_target_pairs={{0,16},{8,24},{16,0},{24,8},{1,17},{9,25},{17,1},{25,9},{2,18},{10... | collective-permute-start | bytes 258056 | tf_op jit(solution)/shard_map/ppermute | solution.py:418
  22.9 4.5 %collective-permute-start.6 = (bf16[48,896]{1,0:T(8,128)(2,1)S(1)}, bf16[48,896]{1,0:T(8,128)(2,1)S(1)}, u32[]{:S(2)}, u32[]{:S(2)}) collective-permute-start(bf16[48,896]{1,0:T(8,128)(2,1)S(1)} %get-tuple-element.47), channel_id=1, source_target_pairs={{0,8},{8,0},{16,24},{24,16},{1,9},{9,1},{17,25},{25,17},{2,10},{10... | collective-permute-start | bytes 258056 | tf_op jit(solution)/shard_map/ppermute | solution.py:418
  27.1 10.1 %copy-start = (s32[1,1,1,512]{3,2,1,0:T(1,128)S(1)}, s32[1,1,1,512]{3,2,1,0:T(1,128)}, u32[]{:S(2)}) copy-start(s32[1,1,1,512]{3,2,1,0:T(1,128)} %param.6) | copy-start | bytes 6148
  28.5 2.9 %collective-permute-start.10 = (bf16[4,272,128]{2,1,0:T(8,128)(2,1)S(1)}, bf16[4,272,128]{2,1,0:T(8,128)(2,1)S(1)}, u32[]{:S(2)}, u32[]{:S(2)}) collective-permute-start(bf16[4,272,128]{2,1,0:T(8,128)(2,1)S(1)} %get-tuple-element.52), channel_id=1, source_target_pairs={{0,1},{1,0},{2,3},{3,2},{4,5},{5,4},{6,7},{7,6},{8,9},{9,8},{10,11... | collective-permute-start | bytes 835592 | tf_op jit(solution)/shard_map/ppermute | solution.py:418
  31.4 8.2 %collective-permute-start.11 = (bf16[272,128]{1,0:T(8,128)(2,1)S(1)}, bf16[272,128]{1,0:T(8,128)(2,1)S(1)}, u32[]{:S(2)}, u32[]{:S(2)}) collective-permute-start(bf16[272,128]{1,0:T(8,128)(2,1)S(1)} %get-tuple-element.54), channel_id=1, source_target_pairs={{0,6},{1,7},{2,4},{3,5},{4,2},{5,3},{6,0},{7,1},{8,14},{9,15},{10,... | collective-permute-start | bytes 208904 | tf_op jit(solution)/shard_map/ppermute | solution.py:418
  35.9 7.0 %collective-permute-start.12 = (bf16[272,128]{1,0:T(8,128)(2,1)S(1)}, bf16[272,128]{1,0:T(8,128)(2,1)S(1)}, u32[]{:S(2)}, u32[]{:S(2)}) collective-permute-start(bf16[272,128]{1,0:T(8,128)(2,1)S(1)} %get-tuple-element.55), channel_id=1, source_target_pairs={{0,4},{1,5},{2,6},{3,7},{4,0},{5,1},{6,2},{7,3},{8,12},{9,13},{10,... | collective-permute-start | bytes 208904 | tf_op jit(solution)/shard_map/ppermute | solution.py:418
  37.1 5.8 %collective-permute-start.13 = (bf16[272,128]{1,0:T(8,128)(2,1)S(1)}, bf16[272,128]{1,0:T(8,128)(2,1)S(1)}, u32[]{:S(2)}, u32[]{:S(2)}) collective-permute-start(bf16[272,128]{1,0:T(8,128)(2,1)S(1)} %get-tuple-element.56), channel_id=1, source_target_pairs={{0,2},{1,3},{2,0},{3,1},{4,6},{5,7},{6,4},{7,5},{8,10},{9,11},{10,... | collective-permute-start | bytes 208904 | tf_op jit(solution)/shard_map/ppermute | solution.py:418

commit v6 on v5

--- a/solution.py
+++ b/solution.py
@@ -324,8 +324,15 @@
     return full, rest, per, 9 * full + (-(-9 // per) if rest else 0)
 
 
-def lines_of(slots, rows):
-    return -(-slots * rows // 16) * 16
+def folds(width, rows):
+    _, rest, per, _ = packing(width)
+    return bool(rest) and 9 % per == 1 and rows % 8 == 0 and rows // 8 * rest <= 128
+
+
+def lines_of(width, rows):
+    slots = packing(width)[3]
+    used = (slots - 1) * rows + 8 if folds(width, rows) else slots * rows
+    return -(-used // 16) * 16
 
 
 def kernel_grad_body(last, chips, *refs):
@@ -376,14 +383,23 @@
         return
     send_ref, keep_ref, _ = outs
     rows = channels // (2 * chips)
-    count = lines_of(slots, rows)
+    count = lines_of(width, rows)
+    fold = folds(width, rows)
     core = lax.axis_index("gy") & 1
-    pad = [jnp.zeros((count - slots * rows, 128), F32)] if count > slots * rows else []
     for chip in range(chips):
         for whose, out in ((1 - core, send_ref), (core, keep_ref)):
             start = pl.multiple_of(rows * (2 * chip + whose), 8)
-            piece = store[:, pl.ds(start, rows), :].reshape(slots * rows, 128)
-            out[chip] = jnp.concatenate([piece] + pad, axis=0).astype(out.dtype)
+            piece = store[:, pl.ds(start, rows), :]
+            if fold:
+                tail = [piece[slots - 1, n : n + 8, :rest] for n in range(0, rows, 8)]
+                tail.append(jnp.zeros((8, 128 - rest * len(tail)), F32))
+                pieces = [piece[: slots - 1].reshape((slots - 1) * rows, 128), jnp.concatenate(tail, axis=1)]
+            else:
+                pieces = [piece.reshape(slots * rows, 128)]
+            used = sum(part.shape[0] for part in pieces)
+            if count > used:
+                pieces.append(jnp.zeros((count - used, 128), F32))
+            out[chip] = jnp.concatenate(pieces, axis=0).astype(out.dtype)
 
 
 def pair_body(chips, keep_ref, recv_ref, own_ref, *send_refs):
@@ -407,7 +423,11 @@
         if rest:
             at = rows * (9 * full + ab // per)
             lane = rest * (ab % per)
-            parts.append(total[at : at + rows, lane : lane + rest])
+            if ab == 8 and folds(width, rows):
+                tail = [total[at : at + 8, rest * n : rest * (n + 1)] for n in range(rows // 8)]
+                parts.append(jnp.concatenate(tail, axis=0))
+            else:
+                parts.append(total[at : at + rows, lane : lane + rest])
         line = parts[0] if len(parts) == 1 else jnp.concatenate(parts, axis=1)
         for c in range(3):
             out_ref[3 * ab + c] = line[:, block * c : block * (c + 1)]
@@ -488,7 +508,7 @@
 
     width = 3 * block
     slots = packing(width)[3]
-    count = lines_of(slots, rows)
+    count = lines_of(width, rows)
     table = (slots, channels, 128)
     lines = [lines[0]] + others
     so_far = []

time: 44.1 us -> 43.8 us (level)
  no operation moved by 1% of the time
where the time goes in v6:
time: 43.8 us; the launch traced here: 43.6 us
  starting transfers between devices  22.6 us (52%)
  Pallas kernels  13.5 us (31%)
  waiting for transfers between devices  6.06 us (14%)
  between operations  1.41 us (3%)
    ppermute x12, starting transfers between devices, xor_step(): return lax.ppermute(value, axis, [(i, i ^ step) for i in range(count)])  21.3 us
    pallas_call x11, Pallas kernels, call(): pl.pallas_call(body, out_shape=tuple(outs), in_specs=specs, out_specs=tup...  13.5 us
    ppermute x12, waiting for transfers between devices, xor_step(): return lax.ppermute(value, axis, [(i, i ^ step) for i in range(count)])  6.05 us
    ppermute x2, starting transfers between devices, swap_pairs(): odd = lax.ppermute(odd, axis, later + [(j, i) for i, j in later])  1.32 us
  transfers between devices with their start and end apart: 14, of which 5 were waited for; matrix products, arithmetic and copies ran while one was open for 0% of the time, Pallas kernels for 23%

profile of v6, /device:TPU:0, one launch (start us, length us, event | category | flops | bytes accessed | tf_op | source)
XLA Modules:
  0.0 43.6 jit_solution(7612963507273317982)
XLA Ops:
  1.3 1.3 %shard_map.76 = (bf16[512,192]{1,0:T(8,128)(2,1)S(1)}, bf16[512,192]{1,0:T(8,128)(2,1)S(1)}, bf16[192,512]{1,0:T(8,128)(2,1)S(1)}, bf16[304,128]{1,0:T(8,128)(2,...) custom-call(s32[1,1,1]{2,1,0:T(1,128)S(6)} %copy.8.pos_hbm, bf16[192,512]{1,0:T(8,128)(2,1)} %bitcast.10, ...), custom_call_target="tpu_custom_call" | custom-call | tf_op jit(solution)/shard_map/pallas_call | solution.py:26
  2.6 3.0 %collective-permute-start = (bf16[304,128]{1,0:T(8,128)(2,1)S(1)}, bf16[304,128]{1,0:T(8,128)(2,1)S(1)}, u32[]{:S(2)}, u32[]{:S(2)}) collective-permute-start(bf16[304,128]{1,0:T(8,128)(2,1)S(1)} %get-tuple-element.33), channel_id=1, source_target_pairs={{0,8},{8,0},{16,24},{24,16},{1,9},{9,1},{17,25},{25,17},{2,10},{10... | collective-permute-start | bytes 233480 | tf_op jit(solution)/shard_map/ppermute | solution.py:438
  5.6 0.7 %collective-permute-start.1 = (bf16[304,128]{1,0:T(8,128)(2,1)S(1)}, bf16[304,128]{1,0:T(8,128)(2,1)S(1)}, u32[]{:S(2)}, u32[]{:S(2)}) collective-permute-start(bf16[304,128]{1,0:T(8,128)(2,1)S(1)} %get-tuple-element.34), channel_id=1, source_target_pairs={{8,16},{16,8},{9,17},{17,9},{10,18},{18,10},{11,19},{19,11},{12,20... | collective-permute-start | bytes 233480 | tf_op jit(solution)/shard_map/ppermute | solution.py:444
  6.3 1.6 %collective-permute-start.4 = (bf16[192,512]{1,0:T(8,128)(2,1)S(1)}, bf16[192,512]{1,0:T(8,128)(2,1)S(1)}, u32[]{:S(2)}, u32[]{:S(2)}) collective-permute-start(bf16[192,512]{1,0:T(8,128)(2,1)S(1)} %get-tuple-element.46.refs_0_), channel_id=1, source_target_pairs={{0,24},{8,16},{16,8},{24,0},{1,25},{9,17},{17,9},{25,1},{2,26},{10... | collective-permute-start | bytes 589832 | tf_op jit(solution)/shard_map/ppermute | solution.py:438
  7.8 1.7 %shard_map.77 = (bf16[27,192,192]{2,1,0:T(8,128)(2,1)S(1)}, bf16[16,128]{1,0:T(8,128)(2,1)S(1)}) custom-call(bf16[27,192,192]{2,1,0:T(8,128)(2,1)} %bitcast.12), custom_call_target="tpu_custom_call" | custom-call | flops 1000000000 | bytes 3985408 | tf_op jit(solution)/shard_map/pallas_call | solution.py:26
  9.6 0.0 collective-permute-done.xeven_ref.refs_3_
  9.6 0.0 collective-permute-done.1.xodd_ref.refs_4_
  9.6 0.2 shard_map.78
  9.8 0.0 collective-permute-start.2
  9.8 0.7 %collective-permute-start.3 = (bf16[432,128]{1,0:T(8,128)(2,1)S(1)}, bf16[432,128]{1,0:T(8,128)(2,1)S(1)}, u32[]{:S(2)}, u32[]{:S(2)}) collective-permute-start(bf16[432,128]{1,0:T(8,128)(2,1)S(1)} %get-tuple-element.40), channel_id=1, source_target_pairs={{1,2},{3,4},{5,6},{2,1},{4,3},{6,5},{9,10},{11,12},{13,14},{10,9},... | collective-permute-start | bytes 331784 | tf_op jit(solution)/shard_map/ppermute | solution.py:444
  10.5 5.7 %collective-permute-start.7 = (bf16[192,512]{1,0:T(8,128)(2,1)S(1)}, bf16[192,512]{1,0:T(8,128)(2,1)S(1)}, u32[]{:S(2)}, u32[]{:S(2)}) collective-permute-start(bf16[192,512]{1,0:T(8,128)(2,1)S(1)} %get-tuple-element.46.refs_0_), channel_id=1, source_target_pairs={{0,16},{8,24},{16,0},{24,8},{1,17},{9,25},{17,1},{25,9},{2,18},{10... | collective-permute-start | bytes 589832 | tf_op jit(solution)/shard_map/ppermute | solution.py:438
  16.1 0.0 collective-permute-start.5
  16.1 0.0 collective-permute-done.2.refs_5_
  16.1 0.0 collective-permute-done.3.refs_6_
  16.2 0.0 collective-permute-done.4.refs_8_.refs_0_
  16.2 3.2 %shard_map.79 = (bf16[512,192]{1,0:T(8,128)(2,1)S(1)}, bf16[10,80,192]{2,1,0:T(8,128)(2,1)S(1)}, bf16[48,896]{1,0:T(8,128)(2,1)S(1)}, bf16[48,896]{1,0:T(8,128)(...) custom-call(bf16[32,192]{1,0:T(8,128)(2,1)S(1)} %get-tuple-element.30.spot_ref.refs_0_, ...), custom_call_target="tpu_custom_call" | custom-call | tf_op jit(solution)/shard_map/pallas_call | solution.py:26
  19.4 1.6 %collective-permute-start.9 = (bf16[48,896]{1,0:T(8,128)(2,1)S(1)}, bf16[48,896]{1,0:T(8,128)(2,1)S(1)}, u32[]{:S(2)}, u32[]{:S(2)}) collective-permute-start(bf16[48,896]{1,0:T(8,128)(2,1)S(1)} %get-tuple-element.49), channel_id=1, source_target_pairs={{0,24},{8,16},{16,8},{24,0},{1,25},{9,17},{17,9},{25,1},{2,26},{10... | collective-permute-start | bytes 258056 | tf_op jit(solution)/shard_map/ppermute | solution.py:438
  21.0 1.9 %collective-permute-start.8 = (bf16[48,896]{1,0:T(8,128)(2,1)S(1)}, bf16[48,896]{1,0:T(8,128)(2,1)S(1)}, u32[]{:S(2)}, u32[]{:S(2)}) collective-permute-start(bf16[48,896]{1,0:T(8,128)(2,1)S(1)} %get-tuple-element.48), channel_id=1, source_target_pairs={{0,16},{8,24},{16,0},{24,8},{1,17},{9,25},{17,1},{25,9},{2,18},{10... | collective-permute-start | bytes 258056 | tf_op jit(solution)/shard_map/ppermute | solution.py:438
  22.9 0.0 collective-permute-start.6
  22.9 0.8 %shard_map.81.refs_2_ = f32[9,192,144]{2,1,0:T(8,128)S(1)} custom-call(bf16[192,512]{1,0:T(8,128)(2,1)S(1)} %get-tuple-element.46.refs_0_, bf16[48,896]{1,0:T(8,128)(2,1)S(1)} %get-tuple-element.50.refs_1_), custom_call_target="tpu_custom_call" | custom-call | flops 254803968 | bytes 1277952 | tf_op jit(solution)/shard_map/pallas_call | solution.py:26
  23.8 1.1 %collective-permute-done.9.refs_1_ = bf16[48,896]{1,0:T(8,128)(2,1)S(1)} collective-permute-done((bf16[48,896]{1,0:T(8,128)(2,1)S(1)}, bf16[48,896]{1,0:T(8,128)(2,1)S(1)}, u32[]{:S(2)}, u32[]{:S(2)}) %collective-permute-start.9) | collective-permute-done | bytes 86048 | tf_op jit(solution)/shard_map/ppermute | solution.py:438
  24.8 0.8 %shard_map.82.refs_2_ = f32[9,192,144]{2,1,0:T(8,128)S(1)} custom-call(bf16[192,512]{1,0:T(8,128)(2,1)S(1)} %collective-permute-done.4.refs_8_.refs_0_, bf16[48,896]{1,0:T(8,128)(2,1)S(1)} %collective-permute-done.9.refs_1_, f32[9,192,144]{2,1,0:T(8,128)S(1)} %shard_map.81.refs_2_), custom_call_target="tpu_custom_call" | custom-call | flops 254803968 | bytes 2273280 | tf_op jit(solution)/shard_map/pallas_call | solution.py:26
  25.7 0.0 collective-permute-done.7.refs_0_
  25.7 0.5 %collective-permute-done.8.refs_1_ = bf16[48,896]{1,0:T(8,128)(2,1)S(1)} collective-permute-done((bf16[48,896]{1,0:T(8,128)(2,1)S(1)}, bf16[48,896]{1,0:T(8,128)(2,1)S(1)}, u32[]{:S(2)}, u32[]{:S(2)}) %collective-permute-start.8) | collective-permute-done | bytes 86048 | tf_op jit(solution)/shard_map/ppermute | solution.py:438
  26.2 0.8 %shard_map.83.refs_2_ = f32[9,192,144]{2,1,0:T(8,128)S(1)} custom-call(bf16[192,512]{1,0:T(8,128)(2,1)S(1)} %collective-permute-done.7.refs_0_, bf16[48,896]{1,0:T(8,128)(2,1)S(1)} %collective-permute-done.8.refs_1_, f32[9,192,144]{2,1,0:T(8,128)S(1)} %shard_map.82.refs_2_), custom_call_target="tpu_custom_call" | custom-call | flops 254803968 | bytes 2273280 | tf_op jit(solution)/shard_map/pallas_call | solution.py:26
  27.1 0.0 copy-start
  27.1 0.0 collective-permute-done.5.refs_0_
  27.1 0.3 collective-permute-done.6.refs_1_
  27.4 1.1 %shard_map.84 = (bf16[4,256,128]{2,1,0:T(8,128)(2,1)S(1)}, f32[4,256,128]{2,1,0:T(8,128)S(1)}) custom-call(bf16[192,512]{1,0:T(8,128)(2,1)S(1)} %collective-permute-done.5.refs_0_, bf16[48,896]{1,0:T(8,128)(2,1)S(1)} %collective-permute-done.6.refs_1_, f32[9,192,144]{2,1,0:T(8,128)S(1)} %shard_map.83.refs_2_), custom_call_target="tpu_custom_call" | custom-call | flops 254803968 | bytes 2064384 | tf_op jit(solution)/shard_map/pallas_call | solution.py:26
  28.6 1.7 %collective-permute-start.10 = (bf16[4,256,128]{2,1,0:T(8,128)(2,1)S(1)}, bf16[4,256,128]{2,1,0:T(8,128)(2,1)S(1)}, u32[]{:S(2)}, u32[]{:S(2)}) collective-permute-start(bf16[4,256,128]{2,1,0:T(8,128)(2,1)S(1)} %get-tuple-element.52), channel_id=1, source_target_pairs={{0,1},{1,0},{2,3},{3,2},{4,5},{5,4},{6,7},{7,6},{8,9},{9,8},{10,11... | collective-permute-start | bytes 786440 | tf_op jit(solution)/shard_map/ppermute | solution.py:438
  30.3 1.2 %collective-permute-done.10.recv_ref = bf16[4,256,128]{2,1,0:T(8,128)(2,1)S(1)} collective-permute-done((bf16[4,256,128]{2,1,0:T(8,128)(2,1)S(1)}, bf16[4,256,128]{2,1,0:T(8,128)(2,1)S(1)}, u32[]{:S(2)}, u32[]{:S(2)}) %collective-permute-start.10) | collective-permute-done | bytes 262176 | tf_op jit(solution)/shard_map/ppermute | solution.py:438
  31.4 0.1 shard_map.85
  31.5 4.5 %collective-permute-start.11 = (bf16[256,128]{1,0:T(8,128)(2,1)S(1)}, bf16[256,128]{1,0:T(8,128)(2,1)S(1)}, u32[]{:S(2)}, u32[]{:S(2)}) collective-permute-start(bf16[256,128]{1,0:T(8,128)(2,1)S(1)} %get-tuple-element.54), channel_id=1, source_target_pairs={{0,6},{1,7},{2,4},{3,5},{4,2},{5,3},{6,0},{7,1},{8,14},{9,15},{10,... | collective-permute-start | bytes 196616 | tf_op jit(solution)/shard_map/ppermute | solution.py:438
  36.0 1.1 %collective-permute-start.12 = (bf16[256,128]{1,0:T(8,128)(2,1)S(1)}, bf16[256,128]{1,0:T(8,128)(2,1)S(1)}, u32[]{:S(2)}, u32[]{:S(2)}) collective-permute-start(bf16[256,128]{1,0:T(8,128)(2,1)S(1)} %get-tuple-element.55), channel_id=1, source_target_pairs={{0,4},{1,5},{2,6},{3,7},{4,0},{5,1},{6,2},{7,3},{8,12},{9,13},{10,... | collective-permute-start | bytes 196616 | tf_op jit(solution)/shard_map/ppermute | solution.py:438
  37.2 0.1 collective-permute-start.13
  37.3 0.0 copy-done
  37.3 2.4 %shard_map.80 = (bf16[192,512]{1,0:T(8,128)(2,1)}, bf16[192,512]{1,0:T(8,128)(2,1)}) custom-call(bf16[10,80,192]{2,1,0:T(8,128)(2,1)S(1)} %get-tuple-element.42.slope_ref, bf16[512,192]{1,0:T(8,128)(2,1)S(1)} %get-tuple-element.43.act_ref, s32[1,512]{1,0:T(1,128)S(1)} %bitcast.8, bf16[27,192,192]{2,1,0:T(8,128)(2,1)S(1)} %get-tuple-element.41.refs_7_.w_ref), custom_call_target="tpu_custom_call" | custom-call | flops 1019215872 | bytes 2889728 | tf_op jit(solution)/shard_map/pallas_call | solution.py:26
  39.7 0.0 collective-permute-done.11.refs_1_
  39.7 2.9 %collective-permute-done.12.refs_2_ = bf16[256,128]{1,0:T(8,128)(2,1)S(1)} collective-permute-done((bf16[256,128]{1,0:T(8,128)(2,1)S(1)}, bf16[256,128]{1,0:T(8,128)(2,1)S(1)}, u32[]{:S(2)}, u32[]{:S(2)}) %collective-permute-start.12) | collective-permute-done | bytes 65568 | tf_op jit(solution)/shard_map/ppermute | solution.py:438
  42.7 0.0 collective-permute-done.13.refs_3_
  42.7 0.9 %shard_map.86 = f32[27,24,48]{2,1,0:T(8,128)} custom-call(f32[256,128]{1,0:T(8,128)S(1)} %get-tuple-element.53.refs_0_, bf16[256,128]{1,0:T(8,128)(2,1)S(1)} %collective-permute-done.11.refs_1_, bf16[256,128]{1,0:T(8,128)(2,1)S(1)} %collective-permute-done.12.refs_2_, bf16[256,128]{1,0:T(8,128)(2,1)S(1)} %collective-permute-done.13.refs_3_), custom_call_target="tpu_custom_call" | custom-call | bytes 452096 | tf_op jit(solution)/shard_map/pallas_call | solution.py:26
Async XLA Ops:
  2.6 7.0 %collective-permute-start = (bf16[304,128]{1,0:T(8,128)(2,1)S(1)}, bf16[304,128]{1,0:T(8,128)(2,1)S(1)}, u32[]{:S(2)}, u32[]{:S(2)}) collective-permute-start(bf16[304,128]{1,0:T(8,128)(2,1)S(1)} %get-tuple-element.33), channel_id=1, source_target_pairs={{0,8},{8,0},{16,24},{24,16},{1,9},{9,1},{17,25},{25,17},{2,10},{10... | collective-permute-start | bytes 233480 | tf_op jit(solution)/shard_map/ppermute | solution.py:438
  5.6 4.0 %collective-permute-start.1 = (bf16[304,128]{1,0:T(8,128)(2,1)S(1)}, bf16[304,128]{1,0:T(8,128)(2,1)S(1)}, u32[]{:S(2)}, u32[]{:S(2)}) collective-permute-start(bf16[304,128]{1,0:T(8,128)(2,1)S(1)} %get-tuple-element.34), channel_id=1, source_target_pairs={{8,16},{16,8},{9,17},{17,9},{10,18},{18,10},{11,19},{19,11},{12,20... | collective-permute-start | bytes 233480 | tf_op jit(solution)/shard_map/ppermute | solution.py:444
  6.3 9.9 %collective-permute-start.4 = (bf16[192,512]{1,0:T(8,128)(2,1)S(1)}, bf16[192,512]{1,0:T(8,128)(2,1)S(1)}, u32[]{:S(2)}, u32[]{:S(2)}) collective-permute-start(bf16[192,512]{1,0:T(8,128)(2,1)S(1)} %get-tuple-element.46.refs_0_), channel_id=1, source_target_pairs={{0,24},{8,16},{16,8},{24,0},{1,25},{9,17},{17,9},{25,1},{2,26},{10... | collective-permute-start | bytes 589832 | tf_op jit(solution)/shard_map/ppermute | solution.py:438
  9.8 6.4 %collective-permute-start.2 = (bf16[432,128]{1,0:T(8,128)(2,1)S(1)}, bf16[432,128]{1,0:T(8,128)(2,1)S(1)}, u32[]{:S(2)}, u32[]{:S(2)}) collective-permute-start(bf16[432,128]{1,0:T(8,128)(2,1)S(1)} %get-tuple-element.39), channel_id=1, source_target_pairs={{0,1},{1,0},{2,3},{3,2},{4,5},{5,4},{6,7},{7,6},{8,9},{9,8},{10,11... | collective-permute-start | bytes 331784 | tf_op jit(solution)/shard_map/ppermute | solution.py:438
  9.8 6.4 %collective-permute-start.3 = (bf16[432,128]{1,0:T(8,128)(2,1)S(1)}, bf16[432,128]{1,0:T(8,128)(2,1)S(1)}, u32[]{:S(2)}, u32[]{:S(2)}) collective-permute-start(bf16[432,128]{1,0:T(8,128)(2,1)S(1)} %get-tuple-element.40), channel_id=1, source_target_pairs={{1,2},{3,4},{5,6},{2,1},{4,3},{6,5},{9,10},{11,12},{13,14},{10,9},... | collective-permute-start | bytes 331784 | tf_op jit(solution)/shard_map/ppermute | solution.py:444
  10.5 15.2 %collective-permute-start.7 = (bf16[192,512]{1,0:T(8,128)(2,1)S(1)}, bf16[192,512]{1,0:T(8,128)(2,1)S(1)}, u32[]{:S(2)}, u32[]{:S(2)}) collective-permute-start(bf16[192,512]{1,0:T(8,128)(2,1)S(1)} %get-tuple-element.46.refs_0_), channel_id=1, source_target_pairs={{0,16},{8,24},{16,0},{24,8},{1,17},{9,25},{17,1},{25,9},{2,18},{10... | collective-permute-start | bytes 589832 | tf_op jit(solution)/shard_map/ppermute | solution.py:438
  16.1 11.0 %collective-permute-start.5 = (bf16[192,512]{1,0:T(8,128)(2,1)S(1)}, bf16[192,512]{1,0:T(8,128)(2,1)S(1)}, u32[]{:S(2)}, u32[]{:S(2)}) collective-permute-start(bf16[192,512]{1,0:T(8,128)(2,1)S(1)} %get-tuple-element.46.refs_0_), channel_id=1, source_target_pairs={{0,8},{8,0},{16,24},{24,16},{1,9},{9,1},{17,25},{25,17},{2,10},{10... | collective-permute-start | bytes 589832 | tf_op jit(solution)/shard_map/ppermute | solution.py:438
  19.4 5.5 %collective-permute-start.9 = (bf16[48,896]{1,0:T(8,128)(2,1)S(1)}, bf16[48,896]{1,0:T(8,128)(2,1)S(1)}, u32[]{:S(2)}, u32[]{:S(2)}) collective-permute-start(bf16[48,896]{1,0:T(8,128)(2,1)S(1)} %get-tuple-element.49), channel_id=1, source_target_pairs={{0,24},{8,16},{16,8},{24,0},{1,25},{9,17},{17,9},{25,1},{2,26},{10... | collective-permute-start | bytes 258056 | tf_op jit(solution)/shard_map/ppermute | solution.py:438
  21.0 5.3 %collective-permute-start.8 = (bf16[48,896]{1,0:T(8,128)(2,1)S(1)}, bf16[48,896]{1,0:T(8,128)(2,1)S(1)}, u32[]{:S(2)}, u32[]{:S(2)}) collective-permute-start(bf16[48,896]{1,0:T(8,128)(2,1)S(1)} %get-tuple-element.48), channel_id=1, source_target_pairs={{0,16},{8,24},{16,0},{24,8},{1,17},{9,25},{17,1},{25,9},{2,18},{10... | collective-permute-start | bytes 258056 | tf_op jit(solution)/shard_map/ppermute | solution.py:438
  22.9 4.5 %collective-permute-start.6 = (bf16[48,896]{1,0:T(8,128)(2,1)S(1)}, bf16[48,896]{1,0:T(8,128)(2,1)S(1)}, u32[]{:S(2)}, u32[]{:S(2)}) collective-permute-start(bf16[48,896]{1,0:T(8,128)(2,1)S(1)} %get-tuple-element.47), channel_id=1, source_target_pairs={{0,8},{8,0},{16,24},{24,16},{1,9},{9,1},{17,25},{25,17},{2,10},{10... | collective-permute-start | bytes 258056 | tf_op jit(solution)/shard_map/ppermute | solution.py:438
  27.1 10.2 %copy-start = (s32[1,1,1,512]{3,2,1,0:T(1,128)S(1)}, s32[1,1,1,512]{3,2,1,0:T(1,128)}, u32[]{:S(2)}) copy-start(s32[1,1,1,512]{3,2,1,0:T(1,128)} %param.6) | copy-start | bytes 6148
  28.6 2.9 %collective-permute-start.10 = (bf16[4,256,128]{2,1,0:T(8,128)(2,1)S(1)}, bf16[4,256,128]{2,1,0:T(8,128)(2,1)S(1)}, u32[]{:S(2)}, u32[]{:S(2)}) collective-permute-start(bf16[4,256,128]{2,1,0:T(8,128)(2,1)S(1)} %get-tuple-element.52), channel_id=1, source_target_pairs={{0,1},{1,0},{2,3},{3,2},{4,5},{5,4},{6,7},{7,6},{8,9},{9,8},{10,11... | collective-permute-start | bytes 786440 | tf_op jit(solution)/shard_map/ppermute | solution.py:438
  31.5 8.2 %collective-permute-start.11 = (bf16[256,128]{1,0:T(8,128)(2,1)S(1)}, bf16[256,128]{1,0:T(8,128)(2,1)S(1)}, u32[]{:S(2)}, u32[]{:S(2)}) collective-permute-start(bf16[256,128]{1,0:T(8,128)(2,1)S(1)} %get-tuple-element.54), channel_id=1, source_target_pairs={{0,6},{1,7},{2,4},{3,5},{4,2},{5,3},{6,0},{7,1},{8,14},{9,15},{10,... | collective-permute-start | bytes 196616 | tf_op jit(solution)/shard_map/ppermute | solution.py:438
  36.0 6.6 %collective-permute-start.12 = (bf16[256,128]{1,0:T(8,128)(2,1)S(1)}, bf16[256,128]{1,0:T(8,128)(2,1)S(1)}, u32[]{:S(2)}, u32[]{:S(2)}) collective-permute-start(bf16[256,128]{1,0:T(8,128)(2,1)S(1)} %get-tuple-element.55), channel_id=1, source_target_pairs={{0,4},{1,5},{2,6},{3,7},{4,0},{5,1},{6,2},{7,3},{8,12},{9,13},{10,... | collective-permute-start | bytes 196616 | tf_op jit(solution)/shard_map/ppermute | solution.py:438
  37.2 5.5 %collective-permute-start.13 = (bf16[256,128]{1,0:T(8,128)(2,1)S(1)}, bf16[256,128]{1,0:T(8,128)(2,1)S(1)}, u32[]{:S(2)}, u32[]{:S(2)}) collective-permute-start(bf16[256,128]{1,0:T(8,128)(2,1)S(1)} %get-tuple-element.56), channel_id=1, source_target_pairs={{0,2},{1,3},{2,0},{3,1},{4,6},{5,7},{6,4},{7,5},{8,10},{9,11},{10,... | collective-permute-start | bytes 196616 | tf_op jit(solution)/shard_map/ppermute | solution.py:438

commit v7 on v6

--- a/solution.py
+++ b/solution.py
@@ -15,7 +15,7 @@
 NT = (((1,), (1,)), ((), ()))
 
 
-def call(body, outs, ins, scratch=(), flops=0, far=(), anywhere=(), short=False):
+def call(body, outs, ins, scratch=(), flops=0, far=(), anywhere=(), out_space=pltpu.VMEM, short=False):
     space = {k: pl.ANY for k in anywhere} | {k: pltpu.HBM for k in far}
     specs = [pl.BlockSpec(memory_space=space.get(k, pltpu.VMEM)) for k in range(len(ins))]
     ins = [
@@ -27,7 +27,7 @@
         body,
         out_shape=tuple(outs),
         in_specs=specs,
-        out_specs=tuple(pl.BlockSpec(memory_space=pltpu.VMEM) for _ in outs),
+        out_specs=tuple(pl.BlockSpec(memory_space=out_space) for _ in outs),
         scratch_shapes=list(scratch),
         compiler_params=pltpu.CompilerParams(vmem_limit_bytes=48 * 1024 * 1024),
         cost_estimate=pl.CostEstimate(flops=flops, bytes_accessed=moved, transcendentals=0),
@@ -411,9 +411,10 @@
 
 
 def last_body(slots, width, scale, *refs):
-    out_ref = refs[-1]
+    out_hbm, out_ref, sems = refs[-3:]
+    copies = []
     total = refs[0][...]
-    for other in refs[1:-1]:
+    for other in refs[1:-3]:
         total = total + other[...].astype(F32)
     total = total * scale
     rows, block = out_ref.shape[1], width // 3
@@ -431,6 +432,12 @@
         line = parts[0] if len(parts) == 1 else jnp.concatenate(parts, axis=1)
         for c in range(3):
             out_ref[3 * ab + c] = line[:, block * c : block * (c + 1)]
+        if ab % 3 == 2:
+            some = pl.ds(3 * ab - 6, 9)
+            copies.append(pltpu.make_async_copy(out_ref.at[some], out_hbm.at[some], sems.at[ab // 3]))
+            copies[-1].start()
+    for copy in copies:
+        copy.wait()
 
 
 def xor_step(value, axis, step):
@@ -546,6 +553,8 @@
         functools.partial(last_body, slots, width, 1.0 / (parts * line)),
         [shape((27, rows, block), F32)],
         [own] + came,
+        scratch=[pltpu.VMEM((27, rows, block), F32), pltpu.SemaphoreType.DMA((3,))],
+        out_space=pltpu.HBM,
     )
     return (
         output.reshape(features.shape),

time: 43.8 us -> 43.8 us (level)
  no operation moved by 1% of the time
where the time goes in v7:
time: 43.8 us; the launch traced here: 43.6 us
  starting transfers between devices  22.6 us (52%)
  Pallas kernels  13.5 us (31%)
  waiting for transfers between devices  6.06 us (14%)
  between operations  1.41 us (3%)
    ppermute x12, starting transfers between devices, xor_step(): return lax.ppermute(value, axis, [(i, i ^ step) for i in range(count)])  21.3 us
    pallas_call x11, Pallas kernels, call(): pl.pallas_call(body, out_shape=tuple(outs), in_specs=specs, out_specs=tup...  13.5 us
    ppermute x12, waiting for transfers between devices, xor_step(): return lax.ppermute(value, axis, [(i, i ^ step) for i in range(count)])  6.05 us
    ppermute x2, starting transfers between devices, swap_pairs(): odd = lax.ppermute(odd, axis, later + [(j, i) for i, j in later])  1.32 us
  transfers between devices with their start and end apart: 14, of which 5 were waited for; matrix products, arithmetic and copies ran while one was open for 0% of the time, Pallas kernels for 23%

profile of v7, /device:TPU:0, one launch (start us, length us, event | category | flops | bytes accessed | tf_op | source)
XLA Modules:
  0.0 43.6 jit_solution(15406394258280257633)
XLA Ops:
  1.3 1.3 %shard_map.76 = (bf16[512,192]{1,0:T(8,128)(2,1)S(1)}, bf16[512,192]{1,0:T(8,128)(2,1)S(1)}, bf16[192,512]{1,0:T(8,128)(2,1)S(1)}, bf16[304,128]{1,0:T(8,128)(2,...) custom-call(s32[1,1,1]{2,1,0:T(1,128)S(6)} %copy.8.pos_hbm, bf16[192,512]{1,0:T(8,128)(2,1)} %bitcast.10, ...), custom_call_target="tpu_custom_call" | custom-call | tf_op jit(solution)/shard_map/pallas_call | solution.py:26
  2.6 3.0 %collective-permute-start = (bf16[304,128]{1,0:T(8,128)(2,1)S(1)}, bf16[304,128]{1,0:T(8,128)(2,1)S(1)}, u32[]{:S(2)}, u32[]{:S(2)}) collective-permute-start(bf16[304,128]{1,0:T(8,128)(2,1)S(1)} %get-tuple-element.33), channel_id=1, source_target_pairs={{0,8},{8,0},{16,24},{24,16},{1,9},{9,1},{17,25},{25,17},{2,10},{10... | collective-permute-start | bytes 233480 | tf_op jit(solution)/shard_map/ppermute | solution.py:445
  5.6 0.7 %collective-permute-start.1 = (bf16[304,128]{1,0:T(8,128)(2,1)S(1)}, bf16[304,128]{1,0:T(8,128)(2,1)S(1)}, u32[]{:S(2)}, u32[]{:S(2)}) collective-permute-start(bf16[304,128]{1,0:T(8,128)(2,1)S(1)} %get-tuple-element.34), channel_id=1, source_target_pairs={{8,16},{16,8},{9,17},{17,9},{10,18},{18,10},{11,19},{19,11},{12,20... | collective-permute-start | bytes 233480 | tf_op jit(solution)/shard_map/ppermute | solution.py:451
  6.3 1.6 %collective-permute-start.4 = (bf16[192,512]{1,0:T(8,128)(2,1)S(1)}, bf16[192,512]{1,0:T(8,128)(2,1)S(1)}, u32[]{:S(2)}, u32[]{:S(2)}) collective-permute-start(bf16[192,512]{1,0:T(8,128)(2,1)S(1)} %get-tuple-element.46.refs_0_), channel_id=1, source_target_pairs={{0,24},{8,16},{16,8},{24,0},{1,25},{9,17},{17,9},{25,1},{2,26},{10... | collective-permute-start | bytes 589832 | tf_op jit(solution)/shard_map/ppermute | solution.py:445
  7.8 1.7 %shard_map.77 = (bf16[27,192,192]{2,1,0:T(8,128)(2,1)S(1)}, bf16[16,128]{1,0:T(8,128)(2,1)S(1)}) custom-call(bf16[27,192,192]{2,1,0:T(8,128)(2,1)} %bitcast.12), custom_call_target="tpu_custom_call" | custom-call | flops 1000000000 | bytes 3985408 | tf_op jit(solution)/shard_map/pallas_call | solution.py:26
  9.6 0.0 collective-permute-done.xeven_ref.refs_3_
  9.6 0.0 collective-permute-done.1.xodd_ref.refs_4_
  9.6 0.2 shard_map.78
  9.8 0.0 collective-permute-start.2
  9.8 0.7 %collective-permute-start.3 = (bf16[432,128]{1,0:T(8,128)(2,1)S(1)}, bf16[432,128]{1,0:T(8,128)(2,1)S(1)}, u32[]{:S(2)}, u32[]{:S(2)}) collective-permute-start(bf16[432,128]{1,0:T(8,128)(2,1)S(1)} %get-tuple-element.40), channel_id=1, source_target_pairs={{1,2},{3,4},{5,6},{2,1},{4,3},{6,5},{9,10},{11,12},{13,14},{10,9},... | collective-permute-start | bytes 331784 | tf_op jit(solution)/shard_map/ppermute | solution.py:451
  10.5 5.7 %collective-permute-start.7 = (bf16[192,512]{1,0:T(8,128)(2,1)S(1)}, bf16[192,512]{1,0:T(8,128)(2,1)S(1)}, u32[]{:S(2)}, u32[]{:S(2)}) collective-permute-start(bf16[192,512]{1,0:T(8,128)(2,1)S(1)} %get-tuple-element.46.refs_0_), channel_id=1, source_target_pairs={{0,16},{8,24},{16,0},{24,8},{1,17},{9,25},{17,1},{25,9},{2,18},{10... | collective-permute-start | bytes 589832 | tf_op jit(solution)/shard_map/ppermute | solution.py:445
  16.1 0.0 collective-permute-start.5
  16.1 0.0 collective-permute-done.2.refs_5_
  16.1 0.0 collective-permute-done.3.refs_6_
  16.2 0.0 collective-permute-done.4.refs_8_.refs_0_
  16.2 3.2 %shard_map.79 = (bf16[512,192]{1,0:T(8,128)(2,1)S(1)}, bf16[10,80,192]{2,1,0:T(8,128)(2,1)S(1)}, bf16[48,896]{1,0:T(8,128)(2,1)S(1)}, bf16[48,896]{1,0:T(8,128)(...) custom-call(bf16[32,192]{1,0:T(8,128)(2,1)S(1)} %get-tuple-element.30.spot_ref.refs_0_, ...), custom_call_target="tpu_custom_call" | custom-call | tf_op jit(solution)/shard_map/pallas_call | solution.py:26
  19.4 1.6 %collective-permute-start.9 = (bf16[48,896]{1,0:T(8,128)(2,1)S(1)}, bf16[48,896]{1,0:T(8,128)(2,1)S(1)}, u32[]{:S(2)}, u32[]{:S(2)}) collective-permute-start(bf16[48,896]{1,0:T(8,128)(2,1)S(1)} %get-tuple-element.49), channel_id=1, source_target_pairs={{0,24},{8,16},{16,8},{24,0},{1,25},{9,17},{17,9},{25,1},{2,26},{10... | collective-permute-start | bytes 258056 | tf_op jit(solution)/shard_map/ppermute | solution.py:445
  21.0 1.9 %collective-permute-start.8 = (bf16[48,896]{1,0:T(8,128)(2,1)S(1)}, bf16[48,896]{1,0:T(8,128)(2,1)S(1)}, u32[]{:S(2)}, u32[]{:S(2)}) collective-permute-start(bf16[48,896]{1,0:T(8,128)(2,1)S(1)} %get-tuple-element.48), channel_id=1, source_target_pairs={{0,16},{8,24},{16,0},{24,8},{1,17},{9,25},{17,1},{25,9},{2,18},{10... | collective-permute-start | bytes 258056 | tf_op jit(solution)/shard_map/ppermute | solution.py:445
  22.9 0.0 collective-permute-start.6
  22.9 0.8 %shard_map.81.refs_2_ = f32[9,192,144]{2,1,0:T(8,128)S(1)} custom-call(bf16[192,512]{1,0:T(8,128)(2,1)S(1)} %get-tuple-element.46.refs_0_, bf16[48,896]{1,0:T(8,128)(2,1)S(1)} %get-tuple-element.50.refs_1_), custom_call_target="tpu_custom_call" | custom-call | flops 254803968 | bytes 1277952 | tf_op jit(solution)/shard_map/pallas_call | solution.py:26
  23.8 1.1 %collective-permute-done.9.refs_1_ = bf16[48,896]{1,0:T(8,128)(2,1)S(1)} collective-permute-done((bf16[48,896]{1,0:T(8,128)(2,1)S(1)}, bf16[48,896]{1,0:T(8,128)(2,1)S(1)}, u32[]{:S(2)}, u32[]{:S(2)}) %collective-permute-start.9) | collective-permute-done | bytes 86048 | tf_op jit(solution)/shard_map/ppermute | solution.py:445
  24.8 0.8 %shard_map.82.refs_2_ = f32[9,192,144]{2,1,0:T(8,128)S(1)} custom-call(bf16[192,512]{1,0:T(8,128)(2,1)S(1)} %collective-permute-done.4.refs_8_.refs_0_, bf16[48,896]{1,0:T(8,128)(2,1)S(1)} %collective-permute-done.9.refs_1_, f32[9,192,144]{2,1,0:T(8,128)S(1)} %shard_map.81.refs_2_), custom_call_target="tpu_custom_call" | custom-call | flops 254803968 | bytes 2273280 | tf_op jit(solution)/shard_map/pallas_call | solution.py:26
  25.7 0.0 collective-permute-done.7.refs_0_
  25.7 0.5 %collective-permute-done.8.refs_1_ = bf16[48,896]{1,0:T(8,128)(2,1)S(1)} collective-permute-done((bf16[48,896]{1,0:T(8,128)(2,1)S(1)}, bf16[48,896]{1,0:T(8,128)(2,1)S(1)}, u32[]{:S(2)}, u32[]{:S(2)}) %collective-permute-start.8) | collective-permute-done | bytes 86048 | tf_op jit(solution)/shard_map/ppermute | solution.py:445
  26.2 0.8 %shard_map.83.refs_2_ = f32[9,192,144]{2,1,0:T(8,128)S(1)} custom-call(bf16[192,512]{1,0:T(8,128)(2,1)S(1)} %collective-permute-done.7.refs_0_, bf16[48,896]{1,0:T(8,128)(2,1)S(1)} %collective-permute-done.8.refs_1_, f32[9,192,144]{2,1,0:T(8,128)S(1)} %shard_map.82.refs_2_), custom_call_target="tpu_custom_call" | custom-call | flops 254803968 | bytes 2273280 | tf_op jit(solution)/shard_map/pallas_call | solution.py:26
  27.1 0.0 copy-start
  27.1 0.0 collective-permute-done.5.refs_0_
  27.1 0.3 collective-permute-done.6.refs_1_
  27.4 1.1 %shard_map.84 = (bf16[4,256,128]{2,1,0:T(8,128)(2,1)S(1)}, f32[4,256,128]{2,1,0:T(8,128)S(1)}) custom-call(bf16[192,512]{1,0:T(8,128)(2,1)S(1)} %collective-permute-done.5.refs_0_, bf16[48,896]{1,0:T(8,128)(2,1)S(1)} %collective-permute-done.6.refs_1_, f32[9,192,144]{2,1,0:T(8,128)S(1)} %shard_map.83.refs_2_), custom_call_target="tpu_custom_call" | custom-call | flops 254803968 | bytes 2064384 | tf_op jit(solution)/shard_map/pallas_call | solution.py:26
  28.6 1.7 %collective-permute-start.10 = (bf16[4,256,128]{2,1,0:T(8,128)(2,1)S(1)}, bf16[4,256,128]{2,1,0:T(8,128)(2,1)S(1)}, u32[]{:S(2)}, u32[]{:S(2)}) collective-permute-start(bf16[4,256,128]{2,1,0:T(8,128)(2,1)S(1)} %get-tuple-element.52), channel_id=1, source_target_pairs={{0,1},{1,0},{2,3},{3,2},{4,5},{5,4},{6,7},{7,6},{8,9},{9,8},{10,11... | collective-permute-start | bytes 786440 | tf_op jit(solution)/shard_map/ppermute | solution.py:445
  30.3 1.2 %collective-permute-done.10.recv_ref = bf16[4,256,128]{2,1,0:T(8,128)(2,1)S(1)} collective-permute-done((bf16[4,256,128]{2,1,0:T(8,128)(2,1)S(1)}, bf16[4,256,128]{2,1,0:T(8,128)(2,1)S(1)}, u32[]{:S(2)}, u32[]{:S(2)}) %collective-permute-start.10) | collective-permute-done | bytes 262176 | tf_op jit(solution)/shard_map/ppermute | solution.py:445
  31.4 0.1 shard_map.85
  31.5 4.5 %collective-permute-start.11 = (bf16[256,128]{1,0:T(8,128)(2,1)S(1)}, bf16[256,128]{1,0:T(8,128)(2,1)S(1)}, u32[]{:S(2)}, u32[]{:S(2)}) collective-permute-start(bf16[256,128]{1,0:T(8,128)(2,1)S(1)} %get-tuple-element.54), channel_id=1, source_target_pairs={{0,6},{1,7},{2,4},{3,5},{4,2},{5,3},{6,0},{7,1},{8,14},{9,15},{10,... | collective-permute-start | bytes 196616 | tf_op jit(solution)/shard_map/ppermute | solution.py:445
  36.0 1.1 %collective-permute-start.12 = (bf16[256,128]{1,0:T(8,128)(2,1)S(1)}, bf16[256,128]{1,0:T(8,128)(2,1)S(1)}, u32[]{:S(2)}, u32[]{:S(2)}) collective-permute-start(bf16[256,128]{1,0:T(8,128)(2,1)S(1)} %get-tuple-element.55), channel_id=1, source_target_pairs={{0,4},{1,5},{2,6},{3,7},{4,0},{5,1},{6,2},{7,3},{8,12},{9,13},{10,... | collective-permute-start | bytes 196616 | tf_op jit(solution)/shard_map/ppermute | solution.py:445
  37.2 0.1 collective-permute-start.13
  37.3 0.0 copy-done
  37.3 2.4 %shard_map.80 = (bf16[192,512]{1,0:T(8,128)(2,1)}, bf16[192,512]{1,0:T(8,128)(2,1)}) custom-call(bf16[10,80,192]{2,1,0:T(8,128)(2,1)S(1)} %get-tuple-element.42.slope_ref, bf16[512,192]{1,0:T(8,128)(2,1)S(1)} %get-tuple-element.43.act_ref, s32[1,512]{1,0:T(1,128)S(1)} %bitcast.8, bf16[27,192,192]{2,1,0:T(8,128)(2,1)S(1)} %get-tuple-element.41.refs_7_.w_ref), custom_call_target="tpu_custom_call" | custom-call | flops 1019215872 | bytes 2889728 | tf_op jit(solution)/shard_map/pallas_call | solution.py:26
  39.7 0.0 collective-permute-done.11.refs_1_
  39.7 2.9 %collective-permute-done.12.refs_2_ = bf16[256,128]{1,0:T(8,128)(2,1)S(1)} collective-permute-done((bf16[256,128]{1,0:T(8,128)(2,1)S(1)}, bf16[256,128]{1,0:T(8,128)(2,1)S(1)}, u32[]{:S(2)}, u32[]{:S(2)}) %collective-permute-start.12) | collective-permute-done | bytes 65568 | tf_op jit(solution)/shard_map/ppermute | solution.py:445
  42.7 0.0 collective-permute-done.13.refs_3_
  42.7 0.9 %shard_map.86 = f32[27,24,48]{2,1,0:T(8,128)} custom-call(f32[256,128]{1,0:T(8,128)S(1)} %get-tuple-element.53.refs_0_, bf16[256,128]{1,0:T(8,128)(2,1)S(1)} %collective-permute-done.11.refs_1_, bf16[256,128]{1,0:T(8,128)(2,1)S(1)} %collective-permute-done.12.refs_2_, bf16[256,128]{1,0:T(8,128)(2,1)S(1)} %collective-permute-done.13.refs_3_), custom_call_target="tpu_custom_call" | custom-call | bytes 452096 | tf_op jit(solution)/shard_map/pallas_call | solution.py:26
Async XLA Ops:
  2.6 7.0 %collective-permute-start = (bf16[304,128]{1,0:T(8,128)(2,1)S(1)}, bf16[304,128]{1,0:T(8,128)(2,1)S(1)}, u32[]{:S(2)}, u32[]{:S(2)}) collective-permute-start(bf16[304,128]{1,0:T(8,128)(2,1)S(1)} %get-tuple-element.33), channel_id=1, source_target_pairs={{0,8},{8,0},{16,24},{24,16},{1,9},{9,1},{17,25},{25,17},{2,10},{10... | collective-permute-start | bytes 233480 | tf_op jit(solution)/shard_map/ppermute | solution.py:445
  5.6 4.0 %collective-permute-start.1 = (bf16[304,128]{1,0:T(8,128)(2,1)S(1)}, bf16[304,128]{1,0:T(8,128)(2,1)S(1)}, u32[]{:S(2)}, u32[]{:S(2)}) collective-permute-start(bf16[304,128]{1,0:T(8,128)(2,1)S(1)} %get-tuple-element.34), channel_id=1, source_target_pairs={{8,16},{16,8},{9,17},{17,9},{10,18},{18,10},{11,19},{19,11},{12,20... | collective-permute-start | bytes 233480 | tf_op jit(solution)/shard_map/ppermute | solution.py:451
  6.3 9.9 %collective-permute-start.4 = (bf16[192,512]{1,0:T(8,128)(2,1)S(1)}, bf16[192,512]{1,0:T(8,128)(2,1)S(1)}, u32[]{:S(2)}, u32[]{:S(2)}) collective-permute-start(bf16[192,512]{1,0:T(8,128)(2,1)S(1)} %get-tuple-element.46.refs_0_), channel_id=1, source_target_pairs={{0,24},{8,16},{16,8},{24,0},{1,25},{9,17},{17,9},{25,1},{2,26},{10... | collective-permute-start | bytes 589832 | tf_op jit(solution)/shard_map/ppermute | solution.py:445
  9.8 6.4 %collective-permute-start.2 = (bf16[432,128]{1,0:T(8,128)(2,1)S(1)}, bf16[432,128]{1,0:T(8,128)(2,1)S(1)}, u32[]{:S(2)}, u32[]{:S(2)}) collective-permute-start(bf16[432,128]{1,0:T(8,128)(2,1)S(1)} %get-tuple-element.39), channel_id=1, source_target_pairs={{0,1},{1,0},{2,3},{3,2},{4,5},{5,4},{6,7},{7,6},{8,9},{9,8},{10,11... | collective-permute-start | bytes 331784 | tf_op jit(solution)/shard_map/ppermute | solution.py:445
  9.8 6.4 %collective-permute-start.3 = (bf16[432,128]{1,0:T(8,128)(2,1)S(1)}, bf16[432,128]{1,0:T(8,128)(2,1)S(1)}, u32[]{:S(2)}, u32[]{:S(2)}) collective-permute-start(bf16[432,128]{1,0:T(8,128)(2,1)S(1)} %get-tuple-element.40), channel_id=1, source_target_pairs={{1,2},{3,4},{5,6},{2,1},{4,3},{6,5},{9,10},{11,12},{13,14},{10,9},... | collective-permute-start | bytes 331784 | tf_op jit(solution)/shard_map/ppermute | solution.py:451
  10.5 15.2 %collective-permute-start.7 = (bf16[192,512]{1,0:T(8,128)(2,1)S(1)}, bf16[192,512]{1,0:T(8,128)(2,1)S(1)}, u32[]{:S(2)}, u32[]{:S(2)}) collective-permute-start(bf16[192,512]{1,0:T(8,128)(2,1)S(1)} %get-tuple-element.46.refs_0_), channel_id=1, source_target_pairs={{0,16},{8,24},{16,0},{24,8},{1,17},{9,25},{17,1},{25,9},{2,18},{10... | collective-permute-start | bytes 589832 | tf_op jit(solution)/shard_map/ppermute | solution.py:445
  16.1 11.0 %collective-permute-start.5 = (bf16[192,512]{1,0:T(8,128)(2,1)S(1)}, bf16[192,512]{1,0:T(8,128)(2,1)S(1)}, u32[]{:S(2)}, u32[]{:S(2)}) collective-permute-start(bf16[192,512]{1,0:T(8,128)(2,1)S(1)} %get-tuple-element.46.refs_0_), channel_id=1, source_target_pairs={{0,8},{8,0},{16,24},{24,16},{1,9},{9,1},{17,25},{25,17},{2,10},{10... | collective-permute-start | bytes 589832 | tf_op jit(solution)/shard_map/ppermute | solution.py:445
  19.4 5.5 %collective-permute-start.9 = (bf16[48,896]{1,0:T(8,128)(2,1)S(1)}, bf16[48,896]{1,0:T(8,128)(2,1)S(1)}, u32[]{:S(2)}, u32[]{:S(2)}) collective-permute-start(bf16[48,896]{1,0:T(8,128)(2,1)S(1)} %get-tuple-element.49), channel_id=1, source_target_pairs={{0,24},{8,16},{16,8},{24,0},{1,25},{9,17},{17,9},{25,1},{2,26},{10... | collective-permute-start | bytes 258056 | tf_op jit(solution)/shard_map/ppermute | solution.py:445
  21.0 5.3 %collective-permute-start.8 = (bf16[48,896]{1,0:T(8,128)(2,1)S(1)}, bf16[48,896]{1,0:T(8,128)(2,1)S(1)}, u32[]{:S(2)}, u32[]{:S(2)}) collective-permute-start(bf16[48,896]{1,0:T(8,128)(2,1)S(1)} %get-tuple-element.48), channel_id=1, source_target_pairs={{0,16},{8,24},{16,0},{24,8},{1,17},{9,25},{17,1},{25,9},{2,18},{10... | collective-permute-start | bytes 258056 | tf_op jit(solution)/shard_map/ppermute | solution.py:445
  22.9 4.5 %collective-permute-start.6 = (bf16[48,896]{1,0:T(8,128)(2,1)S(1)}, bf16[48,896]{1,0:T(8,128)(2,1)S(1)}, u32[]{:S(2)}, u32[]{:S(2)}) collective-permute-start(bf16[48,896]{1,0:T(8,128)(2,1)S(1)} %get-tuple-element.47), channel_id=1, source_target_pairs={{0,8},{8,0},{16,24},{24,16},{1,9},{9,1},{17,25},{25,17},{2,10},{10... | collective-permute-start | bytes 258056 | tf_op jit(solution)/shard_map/ppermute | solution.py:445
  27.1 10.2 %copy-start = (s32[1,1,1,512]{3,2,1,0:T(1,128)S(1)}, s32[1,1,1,512]{3,2,1,0:T(1,128)}, u32[]{:S(2)}) copy-start(s32[1,1,1,512]{3,2,1,0:T(1,128)} %param.6) | copy-start | bytes 6148
  28.6 2.9 %collective-permute-start.10 = (bf16[4,256,128]{2,1,0:T(8,128)(2,1)S(1)}, bf16[4,256,128]{2,1,0:T(8,128)(2,1)S(1)}, u32[]{:S(2)}, u32[]{:S(2)}) collective-permute-start(bf16[4,256,128]{2,1,0:T(8,128)(2,1)S(1)} %get-tuple-element.52), channel_id=1, source_target_pairs={{0,1},{1,0},{2,3},{3,2},{4,5},{5,4},{6,7},{7,6},{8,9},{9,8},{10,11... | collective-permute-start | bytes 786440 | tf_op jit(solution)/shard_map/ppermute | solution.py:445
  31.5 8.2 %collective-permute-start.11 = (bf16[256,128]{1,0:T(8,128)(2,1)S(1)}, bf16[256,128]{1,0:T(8,128)(2,1)S(1)}, u32[]{:S(2)}, u32[]{:S(2)}) collective-permute-start(bf16[256,128]{1,0:T(8,128)(2,1)S(1)} %get-tuple-element.54), channel_id=1, source_target_pairs={{0,6},{1,7},{2,4},{3,5},{4,2},{5,3},{6,0},{7,1},{8,14},{9,15},{10,... | collective-permute-start | bytes 196616 | tf_op jit(solution)/shard_map/ppermute | solution.py:445
  36.0 6.6 %collective-permute-start.12 = (bf16[256,128]{1,0:T(8,128)(2,1)S(1)}, bf16[256,128]{1,0:T(8,128)(2,1)S(1)}, u32[]{:S(2)}, u32[]{:S(2)}) collective-permute-start(bf16[256,128]{1,0:T(8,128)(2,1)S(1)} %get-tuple-element.55), channel_id=1, source_target_pairs={{0,4},{1,5},{2,6},{3,7},{4,0},{5,1},{6,2},{7,3},{8,12},{9,13},{10,... | collective-permute-start | bytes 196616 | tf_op jit(solution)/shard_map/ppermute | solution.py:445
  37.2 5.5 %collective-permute-start.13 = (bf16[256,128]{1,0:T(8,128)(2,1)S(1)}, bf16[256,128]{1,0:T(8,128)(2,1)S(1)}, u32[]{:S(2)}, u32[]{:S(2)}) collective-permute-start(bf16[256,128]{1,0:T(8,128)(2,1)S(1)} %get-tuple-element.56), channel_id=1, source_target_pairs={{0,2},{1,3},{2,0},{3,1},{4,6},{5,7},{6,4},{7,5},{8,10},{9,11},{10,... | collective-permute-start | bytes 196616 | tf_op jit(solution)/shard_map/ppermute | solution.py:445
